TPU v7x, 32 devices: a whole 2x2x4 slice. The times are simulated.
32 devices in a mesh: fsdp: 32 (over z, y, x, core).
Axes of the slice: x: 2, y: 2, z: 4, core: 2. Of those that a mesh axis runs over, the one named last changes fastest.
Arguments:
- tokens: bfloat16 [16384, 1024], P('fsdp'), may hold values from -12 to 12
- cotangent: bfloat16 [16384, 1024], P('fsdp'), may hold values from -6 to 6
- seq_lengths: int32 [64, 4], P('fsdp'), may hold values from 1 to 192, 256 in all within a row
- routes: int32 [16384, 8], P('fsdp'), may hold values from 0 to 15, as said below
- attn_gain: bfloat16 [1024], P('fsdp'), may hold values from 0.099609375 to 1.8984375
- w_query: bfloat16 [1024, 1024], P('fsdp'), may hold values from -0.1875 to 0.1875
- w_keyval: bfloat16 [1024, 1024], P('fsdp'), may hold values from -0.1875 to 0.1875
- w_out: bfloat16 [1024, 1024], P('fsdp'), may hold values from -0.75 to 0.75
- moe_gain: bfloat16 [1024], P('fsdp'), may hold values from 0.099609375 to 1.8984375
- w_router: bfloat16 [1024, 16], P('fsdp'), may hold values from -0.125 to 0.125
- w_gateup: bfloat16 [16, 1024, 1024], P(None, 'fsdp'), may hold values from -0.1875 to 0.1875
- w_down: bfloat16 [16, 512, 1024], P(None, 'fsdp'), may hold values from -0.5 to 0.5
Outputs:
- output: bfloat16 [16384, 1024], P('fsdp')
- grad_tokens: float32 [16384, 1024], P('fsdp')
- grad_attn_gain: float32 [1024], P('fsdp')
- grad_query: float32 [1024, 1024], P('fsdp')
- grad_keyval: float32 [1024, 1024], P('fsdp')
- grad_out: float32 [1024, 1024], P('fsdp')
- grad_moe_gain: float32 [1024], P('fsdp')
- grad_router: float32 [1024, 16], P('fsdp')
- grad_gateup: float32 [16, 1024, 1024], P(None, 'fsdp')
- grad_down: float32 [16, 512, 1024], P(None, 'fsdp')
Inputs may be any that keep to these rules, and one draw needn't show every extreme that they name: `seq_lengths`: row b holds, in order, the lengths of the 4 sequences that fill rows b * 256 to (b + 1) * 256 - 1 of the tokens; they sum to 256. `routes`: the 8 entries of a row differ; within each aligned block of 256 rows (one micro-batch of one device), 8 experts, which ones drawn afresh for each block, are named by exactly 192 rows each, and each of the other experts by exactly 64 rows.
All inputs are finite; a program needn't handle non-finite values.
Results may differ from a plain program's by a relative error of at most 0.014.
Values may be sent and summed in bfloat16 or wider, within the bound.
No kernel may reach another device: no remote copies, remote signals or barrier semaphores. Data moves between devices by JAX's collectives and lax.ppermute only.
A program may use at most 256 MiB of HBM per device.

v0:
```python
import jax
import jax.numpy as jnp
from jax import lax
from jax.sharding import PartitionSpec as P

D = 1024
H = 16
KV = 8
HD = 64
FF = 512
TOPK = 8
E = 16
MICRO = 2
EXP_MOST = 192


EPS = 1e-05


def rotate(values, cosine, sine):
    half = values.shape[-1] // 2
    turned = jnp.concatenate([-values[..., half:], values[..., :half]], axis=-1)
    return values * cosine + turned * sine


def rotate_back(grads, cosine, sine):
    half = grads.shape[-1] // 2
    scaled = grads * sine
    return grads * cosine + jnp.concatenate([scaled[..., half:], -scaled[..., :half]], axis=-1)


def layout(lengths, count):
    ends = jnp.cumsum(lengths)
    index = jnp.arange(count, dtype=jnp.int32)
    segment = jnp.sum((index[:, None] >= ends[None, :]).astype(jnp.int32), axis=1)
    start = jnp.max(jnp.where(ends[None, :] <= index[:, None], ends[None, :], 0), axis=1)
    return (segment, index - start)


def rope_tables(position, width):
    freq = jnp.exp(-(jnp.arange(0, width, 2, dtype=jnp.float32) / width) * jnp.log(10000.0))
    angle = position.astype(jnp.float32)[:, None] * freq[None, :]
    angle = jnp.concatenate([angle, angle], axis=1)
    return (jnp.cos(angle)[:, None, :], jnp.sin(angle)[:, None, :])


def norm_forward(values, gain):
    inverse = lax.rsqrt(jnp.mean(values * values, axis=-1, keepdims=True) + EPS)
    return (values * inverse * gain, inverse)


def norm_backward(values, inverse, gain, grads):
    scaled = grads * gain
    inner = jnp.mean(scaled * values, axis=-1, keepdims=True)
    back = inverse * scaled - values * (inverse * inverse * inverse) * inner
    return (back, jnp.sum(grads * values * inverse, axis=0))


def fetch_attention(gain_in, query_w, keyval_w, out_w, gain_mid, router_w):
    return (
        lax.all_gather(gain_in, "fsdp", axis=0, tiled=True),
        lax.all_gather(query_w, "fsdp", axis=0, tiled=True),
        lax.all_gather(keyval_w, "fsdp", axis=0, tiled=True),
        lax.all_gather(out_w, "fsdp", axis=0, tiled=True),
        lax.all_gather(gain_mid, "fsdp", axis=0, tiled=True),
        lax.all_gather(router_w, "fsdp", axis=0, tiled=True),
    )


def route_slots(route, count):
    hot_int = (route[:, :, None] == jnp.arange(E, dtype=jnp.int32)[None, None, :]).astype(jnp.int32)
    per_row = jnp.sum(hot_int, axis=1)
    rank = jnp.cumsum(per_row, axis=0) - per_row
    place = jnp.sum(hot_int * rank[:, None, :], axis=2)
    slot = route * EXP_MOST + place
    filler = jnp.full((E * EXP_MOST,), count * TOPK, jnp.int32)
    filler = filler.at[slot.reshape(-1)].set(jnp.arange(count * TOPK, dtype=jnp.int32))
    return (hot_int.astype(jnp.float32), slot, filler)


def expert_forward(rows, gateup_w, down_w):
    gateup = jnp.einsum("ecd,edf->ecf", rows, gateup_w, preferred_element_type=jnp.float32)
    act = (jax.nn.silu(gateup[..., :FF]) * gateup[..., FF:]).astype(jnp.bfloat16)
    result = jnp.einsum("ecf,efd->ecd", act, down_w, preferred_element_type=jnp.float32)
    return (gateup, result)


def expert_backward(rows, gateup, d_out, gateup_w, down_w):
    gate_part = gateup[..., :FF]
    up_part = gateup[..., FF:]
    sigmoid = jax.nn.sigmoid(gate_part)
    act = (gate_part * sigmoid * up_part).astype(jnp.bfloat16)
    d_act = jnp.einsum("ecd,efd->ecf", d_out, down_w, preferred_element_type=jnp.float32)
    grad_down = jnp.einsum("ecf,ecd->efd", act, d_out, preferred_element_type=jnp.float32)
    d_gate = d_act * up_part * sigmoid * (1.0 + gate_part * (1.0 - sigmoid))
    d_up = d_act * gate_part * sigmoid
    d_gateup = jnp.concatenate([d_gate, d_up], axis=-1).astype(jnp.bfloat16)
    grad_gateup = jnp.einsum("ecd,ecf->edf", rows, d_gateup, preferred_element_type=jnp.float32)
    d_rows = jnp.einsum("ecf,edf->ecd", d_gateup, gateup_w, preferred_element_type=jnp.float32)
    return (d_rows, grad_gateup, grad_down)


def attention_forward(rows_bf, lengths, attn_set):
    gain_in, query_w, keyval_w, out_w, gain_mid, router_w = attn_set
    count = rows_bf.shape[0]
    rows_in = rows_bf.astype(jnp.float32)
    segment, position = layout(lengths, count)
    index = jnp.arange(count, dtype=jnp.int32)
    allowed = (segment[:, None] == segment[None, :]) & (index[None, :] <= index[:, None])
    cosine, sine = rope_tables(position, HD)
    normed, inverse_in = norm_forward(rows_in, gain_in.astype(jnp.float32))
    normed_in = normed.astype(jnp.bfloat16)
    q_lin = jnp.dot(normed_in, query_w, preferred_element_type=jnp.float32)
    kv_lin = jnp.dot(normed_in, keyval_w, preferred_element_type=jnp.float32)
    query = (
        rotate(q_lin.reshape(count, H, HD), cosine, sine)
        .astype(jnp.bfloat16)
        .reshape(count, KV, H // KV, HD)
    )
    key = rotate(kv_lin[:, : KV * HD].reshape(count, KV, HD), cosine, sine).astype(jnp.bfloat16)
    value = kv_lin[:, KV * HD :].reshape(count, KV, HD).astype(jnp.bfloat16)
    score = jnp.einsum("igjd,ngd->gjin", query, key, preferred_element_type=jnp.float32) * 0.125
    score = jnp.where(allowed, score, -1e30)
    log_total = jax.nn.logsumexp(score, axis=-1, keepdims=True)
    weight = jnp.exp(score - log_total).astype(jnp.bfloat16)
    mixed = jnp.einsum("gjin,ngd->igjd", weight, value, preferred_element_type=jnp.float32)
    mixed = mixed.reshape(count, H * HD).astype(jnp.bfloat16)
    resid = rows_in + jnp.dot(mixed, out_w, preferred_element_type=jnp.float32)
    normed, inverse_mid = norm_forward(resid, gain_mid.astype(jnp.float32))
    normed_mid = normed.astype(jnp.bfloat16)
    kept = (
        rows_in,
        normed_in,
        inverse_in,
        query,
        key,
        value,
        log_total,
        mixed,
        resid,
        inverse_mid,
        allowed,
        cosine,
        sine,
    )
    return (resid, normed_mid, kept)


def attention_backward(d_resid, kept, attn_set):
    gain_in, query_w, keyval_w, out_w, gain_mid, router_w = attn_set
    (
        rows_in,
        normed_in,
        inverse_in,
        query,
        key,
        value,
        log_total,
        mixed,
        resid,
        inverse_mid,
        allowed,
        cosine,
        sine,
    ) = kept
    count = rows_in.shape[0]
    d_branch = d_resid.astype(jnp.bfloat16)
    grad_out = jnp.einsum("rk,rd->kd", mixed, d_branch, preferred_element_type=jnp.float32)
    d_mixed = jnp.einsum("rd,kd->rk", d_branch, out_w, preferred_element_type=jnp.float32)
    d_mixed = d_mixed.astype(jnp.bfloat16).reshape(count, KV, H // KV, HD)
    score = jnp.einsum("igjd,ngd->gjin", query, key, preferred_element_type=jnp.float32) * 0.125
    score = jnp.where(allowed, score, -1e30)
    probs = jnp.exp(score - log_total)
    weight = probs.astype(jnp.bfloat16)
    d_weight = jnp.einsum("igjd,ngd->gjin", d_mixed, value, preferred_element_type=jnp.float32)
    d_score = (probs * (d_weight - jnp.sum(probs * d_weight, axis=-1, keepdims=True))).astype(
        jnp.bfloat16
    )
    d_query = jnp.einsum("gjin,ngd->igjd", d_score, key, preferred_element_type=jnp.float32) * 0.125
    d_key = jnp.einsum("gjin,igjd->ngd", d_score, query, preferred_element_type=jnp.float32) * 0.125
    d_value = jnp.einsum("gjin,igjd->ngd", weight, d_mixed, preferred_element_type=jnp.float32)
    d_qlin = (
        rotate_back(d_query.reshape(count, H, HD), cosine, sine)
        .reshape(count, H * HD)
        .astype(jnp.bfloat16)
    )
    d_klin = rotate_back(d_key, cosine, sine).reshape(count, KV * HD)
    d_kvlin = jnp.concatenate([d_klin, d_value.reshape(count, KV * HD)], axis=1).astype(
        jnp.bfloat16
    )
    grad_query = jnp.einsum("rd,rk->dk", normed_in, d_qlin, preferred_element_type=jnp.float32)
    grad_keyval = jnp.einsum("rd,rk->dk", normed_in, d_kvlin, preferred_element_type=jnp.float32)
    d_normed = jnp.einsum("rk,dk->rd", d_qlin, query_w, preferred_element_type=jnp.float32)
    d_normed = d_normed + jnp.einsum(
        "rk,dk->rd", d_kvlin, keyval_w, preferred_element_type=jnp.float32
    )
    d_rows, grad_gain_in = norm_backward(rows_in, inverse_in, gain_in.astype(jnp.float32), d_normed)
    return (d_rows + d_resid, (grad_gain_in, grad_query, grad_keyval, grad_out))


def shards(
    tokens,
    cotangent,
    seq_lengths,
    routes,
    attn_gain,
    w_query,
    w_keyval,
    w_out,
    moe_gain,
    w_router,
    w_gateup,
    w_down,
):
    rows_micro = tokens.shape[0] // MICRO
    devices_all = lax.axis_size("fsdp")
    groups = devices_all // E
    share = EXP_MOST // groups
    home = (
        lax.all_to_all(
            jnp.repeat(w_gateup, groups, axis=0), "fsdp", split_axis=0, concat_axis=1, tiled=True
        ),
        lax.all_to_all(
            jnp.repeat(w_down, groups, axis=0), "fsdp", split_axis=0, concat_axis=1, tiled=True
        ),
    )
    home_gateup, home_down = home
    expert_acc = (
        jnp.zeros(home_gateup.shape, jnp.float32),
        jnp.zeros(home_down.shape, jnp.float32),
    )
    results = []
    grad_rows = []
    attn_acc = None
    for micro_index in range(MICRO):
        first_row = micro_index * rows_micro
        rows_bf = tokens[first_row : first_row + rows_micro]
        grad_bf = cotangent[first_row : first_row + rows_micro]
        route = routes[first_row : first_row + rows_micro]
        lengths = seq_lengths[micro_index]
        attn_set = fetch_attention(attn_gain, w_query, w_keyval, w_out, moe_gain, w_router)
        resid, normed_mid, kept = attention_forward(rows_bf, lengths, attn_set)
        router_w = attn_set[5]
        logits = jnp.dot(normed_mid, router_w, preferred_element_type=jnp.float32)
        route_hot, slot, filler = route_slots(route, rows_micro)
        chosen = jnp.sum(route_hot * logits[:, None, :], axis=2)
        gates = jax.nn.softmax(chosen, axis=-1)
        padded_rows = jnp.concatenate([normed_mid, jnp.zeros((1, D), jnp.bfloat16)], axis=0)
        buffer = padded_rows[filler // TOPK]
        piece = lax.all_to_all(
            buffer.reshape(devices_all, share, D), "fsdp", split_axis=0, concat_axis=0, tiled=True
        )
        items = piece.shape[1]
        gateup, served = expert_forward(piece.reshape(1, -1, D), home_gateup, home_down)
        recv_gateup = gateup.reshape(devices_all, items, 2 * FF)
        recv_out = served.reshape(devices_all, items, D)
        returned = lax.all_to_all(
            recv_out.astype(jnp.bfloat16), "fsdp", split_axis=0, concat_axis=0, tiled=True
        ).astype(recv_out.dtype)
        out_flat = returned.reshape(E * EXP_MOST, D)
        out_routes = out_flat[slot]
        result = resid + jnp.sum(gates[:, :, None] * out_routes, axis=1)
        result = result.astype(jnp.bfloat16)
        fenced = lax.optimization_barrier(
            ((attn_gain, w_query, w_keyval, w_out, moe_gain, w_router), (w_gateup, w_down), result)
        )
        own_attn, own_expert, result = fenced
        attn_set = fetch_attention(
            own_attn[0], own_attn[1], own_attn[2], own_attn[3], own_attn[4], own_attn[5]
        )
        upstream = grad_bf.astype(jnp.float32)
        d_gates = jnp.sum(out_routes * upstream[:, None, :], axis=2)
        d_route = (
            (gates[:, :, None] * upstream[:, None, :])
            .astype(jnp.bfloat16)
            .reshape(rows_micro * TOPK, D)
        )
        padded_grads = jnp.concatenate([d_route, jnp.zeros((1, D), jnp.bfloat16)], axis=0)
        d_buffer = padded_grads[filler]
        recv_grad = lax.all_to_all(
            d_buffer.reshape(devices_all, share, D), "fsdp", split_axis=0, concat_axis=0, tiled=True
        )
        d_served, grad_gu, grad_dn = expert_backward(
            piece.reshape(1, -1, D),
            recv_gateup.reshape(1, -1, 2 * FF),
            recv_grad.reshape(1, -1, D),
            home_gateup,
            home_down,
        )
        expert_acc = (expert_acc[0] + grad_gu, expert_acc[1] + grad_dn)
        d_back = lax.all_to_all(
            d_served.reshape(devices_all, share, D).astype(jnp.bfloat16),
            "fsdp",
            split_axis=0,
            concat_axis=0,
            tiled=True,
        ).astype(jnp.float32)
        d_flat = d_back.reshape(E * EXP_MOST, D)
        d_mid = jnp.sum(d_flat[slot], axis=1)
        d_chosen = gates * (d_gates - jnp.sum(gates * d_gates, axis=1, keepdims=True))
        d_logits = jnp.sum(d_chosen[:, :, None] * route_hot, axis=1).astype(jnp.bfloat16)
        grad_router = jnp.einsum(
            "rd,re->de", normed_mid, d_logits, preferred_element_type=jnp.float32
        )
        d_mid = d_mid + jnp.einsum(
            "re,de->rd", d_logits, attn_set[5], preferred_element_type=jnp.float32
        )
        resid_kept = kept[8]
        inverse_mid = kept[9]
        d_resid, grad_gain_mid = norm_backward(
            resid_kept, inverse_mid, attn_set[4].astype(jnp.float32), d_mid
        )
        d_resid = d_resid + upstream
        d_rows, attn_grads = attention_backward(d_resid, kept, attn_set)
        grads = (
            attn_grads[0],
            attn_grads[1],
            attn_grads[2],
            attn_grads[3],
            grad_gain_mid,
            grad_router,
        )
        attn_acc = (
            grads
            if attn_acc is None
            else tuple((left + right for left, right in zip(attn_acc, grads)))
        )
        results.append(result)
        grad_rows.append(d_rows)
    totals = (
        lax.psum_scatter(attn_acc[0], "fsdp", scatter_dimension=0, tiled=True),
        lax.psum_scatter(attn_acc[1], "fsdp", scatter_dimension=0, tiled=True),
        lax.psum_scatter(attn_acc[2], "fsdp", scatter_dimension=0, tiled=True),
        lax.psum_scatter(attn_acc[3], "fsdp", scatter_dimension=0, tiled=True),
        lax.psum_scatter(attn_acc[4], "fsdp", scatter_dimension=0, tiled=True),
        lax.psum_scatter(attn_acc[5], "fsdp", scatter_dimension=0, tiled=True),
    )
    homed = (
        lax.all_to_all(
            expert_acc[0].astype(jnp.bfloat16), "fsdp", split_axis=1, concat_axis=0, tiled=True
        ).astype(jnp.float32),
        lax.all_to_all(
            expert_acc[1].astype(jnp.bfloat16), "fsdp", split_axis=1, concat_axis=0, tiled=True
        ).astype(jnp.float32),
    )
    grad_gateup = jnp.sum(homed[0].reshape(E, groups, homed[0].shape[1], homed[0].shape[2]), axis=1)
    grad_down = jnp.sum(homed[1].reshape(E, groups, homed[1].shape[1], homed[1].shape[2]), axis=1)
    output = jnp.concatenate(results, axis=0)
    grad_tokens = jnp.concatenate(grad_rows, axis=0)
    return (
        output,
        grad_tokens,
        totals[0],
        totals[1],
        totals[2],
        totals[3],
        totals[4],
        totals[5],
        grad_gateup,
        grad_down,
    )


def solution(mesh):
    placed = (
        P("fsdp", None),
        P("fsdp", None),
        P("fsdp", None),
        P("fsdp", None),
        P("fsdp"),
        P("fsdp", None),
        P("fsdp", None),
        P("fsdp", None),
        P("fsdp"),
        P("fsdp", None),
        P(None, "fsdp", None),
        P(None, "fsdp", None),
    )
    return jax.shard_map(
        shards,
        mesh=mesh,
        in_specs=placed,
        out_specs=(
            P("fsdp", None),
            P("fsdp", None),
            P("fsdp"),
            P("fsdp", None),
            P("fsdp", None),
            P("fsdp", None),
            P("fsdp"),
            P("fsdp", None),
            P(None, "fsdp", None),
            P(None, "fsdp", None),
        ),
        check_vma=False,
    )
```

profile of v0, /device:TPU:0, one launch (start us, length us, event | category | flops | bytes accessed | tf_op | source)
XLA Modules:
  0.0 2147.7 jit_solution(15842812593548227809)
XLA Ops:
  22.1 44.9 %all-reduce.14 = (bf16[1024]{0:T(1024)(128)(2,1)S(1)}, bf16[1024]{0:T(1024)(128)(2,1)S(1)}) all-reduce(bf16[1024]{0:T(1024)(128)(2,1)S(1)} %dynamic-update-slice, bf16[1024]{0:T(1024)(128)(2,1)S(1)} %dynamic-update-slice.1), channel_id=1, replica_groups=mesh['fsdp'=32] {'fsdp'}, use_global_device_ids=true, to_apply=%add.4 | all-reduce | flops 2048 | bytes 8192
  79.6 41.3 %all-gather = bf16[32,32,16]{1,2,0:T(8,128)(2,1)S(1)} all-gather(bf16[1,32,16]{1,2,0:T(8,128)(2,1)S(1)} %bitcast.425), channel_id=1, replica_groups=mesh['fsdp'=32] {'fsdp'}, dimensions={0}, use_global_device_ids=true | all-gather | bytes 33792 | tf_op jit(solution)/shard_map/all_gather | solution.py:66
  150.2 40.3 %all-gather.17.cloned.1.call-done = bf16[1024,1024]{1,0:T(8,128)(2,1)} async-done(((bf16[32,1024]{1,0:T(8,128)(2,1)}), bf16[1024,1024]{1,0:T(8,128)(2,1)}) %all-gather.17.cloned.1.call-update) | async-done | bytes 2097168 | tf_op jit(solution)/shard_map/all_gather | solution.py:64
  213.9 18.7 gather_fusion.4
  232.6 16.4 all-to-all-done.1
  265.8 18.7 gather_fusion.6
  284.5 108.8 %all-to-all-done.6 = bf16[32,96,1024]{2,1,0:T(8,128)(2,1)} async-done(((bf16[32,96,1024]{2,1,0:T(8,128)(2,1)}), bf16[32,96,1024]{2,1,0:T(8,128)(2,1)}, u32[]{:S(2)}, u32[]{:S(2)}) %all-to-all-start.6) | async-done | bytes 6291488 | tf_op jit(solution)/shard_map/all_to_all | solution.py:280
  411.1 125.9 %all-to-all-done.8 = bf16[32,96,1024]{2,1,0:T(8,128)(2,1)} async-done(((bf16[32,96,1024]{2,1,0:T(8,128)(2,1)}), bf16[32,96,1024]{2,1,0:T(8,128)(2,1)}, u32[]{:S(2)}, u32[]{:S(2)}) %all-to-all-start.8) | async-done | bytes 6291488 | tf_op jit(solution)/shard_map/all_to_all | solution.py:280
  554.7 126.0 %all-to-all-done = bf16[32,96,1024]{2,1,0:T(8,128)(2,1)} async-done(((bf16[32,96,1024]{2,1,0:T(8,128)(2,1)}), bf16[32,96,1024]{2,1,0:T(8,128)(2,1)}, u32[]{:S(2)}, u32[]{:S(2)}) %all-to-all-start) | async-done | bytes 6291488 | tf_op jit(solution)/shard_map/all_to_all | solution.py:250
  713.1 111.5 %all-to-all-done.4 = bf16[32,96,1024]{2,1,0:T(8,128)(2,1)} async-done(((bf16[32,96,1024]{2,1,0:T(8,128)(2,1)}), bf16[32,96,1024]{2,1,0:T(8,128)(2,1)}, u32[]{:S(2)}, u32[]{:S(2)}) %all-to-all-start.4) | async-done | bytes 6291488 | tf_op jit(solution)/shard_map/all_to_all | solution.py:250
  856.9 111.4 %all-to-all-done.3 = bf16[32,96,1024]{2,1,0:T(8,128)(2,1)} async-done(((bf16[32,96,1024]{2,1,0:T(8,128)(2,1)}), bf16[32,96,1024]{2,1,0:T(8,128)(2,1)}, u32[]{:S(2)}, u32[]{:S(2)}) %all-to-all-start.3) | async-done | bytes 6291488 | tf_op jit(solution)/shard_map/all_to_all | solution.py:257
  982.9 129.0 %all-to-all-done.5 = bf16[32,96,1024]{2,1,0:T(8,128)(2,1)} async-done(((bf16[32,96,1024]{2,1,0:T(8,128)(2,1)}), bf16[32,96,1024]{2,1,0:T(8,128)(2,1)}, u32[]{:S(2)}, u32[]{:S(2)}) %all-to-all-start.5) | async-done | bytes 6291488 | tf_op jit(solution)/shard_map/all_to_all | solution.py:257
  1125.1 16.4 gather_fusion.1
  1157.2 16.4 gather_fusion.3
  1200.3 66.3 %all-to-all-done.7 = bf16[32,96,1024]{2,1,0:T(8,128)(2,1)} async-done(((bf16[32,96,1024]{2,1,0:T(8,128)(2,1)}), bf16[32,96,1024]{2,1,0:T(8,128)(2,1)}, u32[]{:S(2)}, u32[]{:S(2)}) %all-to-all-start.7) | async-done | bytes 6291488 | tf_op jit(solution)/shard_map/all_to_all | solution.py:291
  1280.9 16.4 gather_fusion.5
  1297.3 118.5 %all-gather.1 = bf16[32,32,16]{1,2,0:T(8,128)(2,1)S(1)} all-gather(bf16[1,32,16]{1,2,0:T(8,128)(2,1)S(1)} %bitcast.426), channel_id=1, replica_groups=mesh['fsdp'=32] {'fsdp'}, dimensions={0}, use_global_device_ids=true | all-gather | bytes 33792 | tf_op jit(solution)/shard_map/all_gather | solution.py:66
  1416.9 65.6 %all-reduce.13 = (bf16[1024]{0:T(1024)(128)(2,1)S(1)}, bf16[1024]{0:T(1024)(128)(2,1)}, bf16[1024]{0:T(1024)(128)(2,1)S(1)}, bf16[1024]{0:T(1024)(128)(2,1)}) all-reduce(bf16[1024]{0:T(1024)(128)(2,1)S(1)} %dynamic-update-slice.4, bf16[1024]{0:T(1024)(128)(2,1)S(1)} %dynamic-update-slice.5, ...), channel_id=1, replica_groups=mesh['fsdp'=32] {'fsdp'}, use_global_device_ids=true, to_apply=%add.8 | all-reduce | flops 4096 | bytes 16384
  1482.5 41.3 %all-gather.2 = bf16[32,32,16]{1,2,0:T(8,128)(2,1)S(1)} all-gather(bf16[1,32,16]{1,2,0:T(8,128)(2,1)S(1)} %bitcast.427), channel_id=1, replica_groups=mesh['fsdp'=32] {'fsdp'}, dimensions={0}, use_global_device_ids=true | all-gather | bytes 33792 | tf_op jit(solution)/shard_map/all_gather | solution.py:66
  1687.7 45.6 %all-to-all-done.10 = bf16[32,2,16384]{2,1,0:T(2,128)(2,1)S(1)} async-done(((bf16[32,2,16384]{2,1,0:T(2,128)(2,1)}), bf16[32,2,16384]{2,1,0:T(2,128)(2,1)S(1)}, u32[]{:S(2)}, u32[]{:S(2)}) %all-to-all-start.10) | async-done | bytes 2097184 | tf_op jit(solution)/shard_map/all_to_all | solution.py:339
  1765.8 38.8 %all-reduce.12 = (f32[1024]{0:T(1024)S(1)}, f32[1024]{0:T(1024)S(1)}) all-reduce(f32[1024]{0:T(1024)S(1)} %add.273, f32[1024]{0:T(1024)S(1)} %add.277), channel_id=2, replica_groups=mesh['fsdp'=32] {'fsdp'}, use_global_device_ids=true, to_apply=%region_48.49.clone | all-reduce | flops 2048 | bytes 16384
  1809.5 51.5 %reduce-scatter.11.cloned.1.call-done = f32[32,1024]{1,0:T(8,128)} async-done(((f32[1024,1024]{1,0:T(8,128)}), f32[32,1024]{1,0:T(8,128)}) %reduce-scatter.11.cloned.1.call-update) | async-done | bytes 131088 | tf_op jit(solution)/shard_map/reduce_scatter | solution.py:334
  1861.0 139.9 %reduce-scatter.9.cloned.1.call-done = f32[32,1024]{1,0:T(8,128)} async-done(((f32[1024,1024]{1,0:T(8,128)}), f32[32,1024]{1,0:T(8,128)}) %reduce-scatter.9.cloned.1.call-update) | async-done | bytes 131088 | tf_op jit(solution)/shard_map/reduce_scatter | solution.py:333
  2001.0 139.7 %reduce-scatter.7.cloned.1.call-done = f32[32,1024]{1,0:T(8,128)} async-done(((f32[1024,1024]{1,0:T(8,128)}), f32[32,1024]{1,0:T(8,128)}) %reduce-scatter.7.cloned.1.call-update) | async-done | bytes 131088 | tf_op jit(solution)/shard_map/reduce_scatter | solution.py:332
  (537 shorter events, 482.0 us)
Async XLA Ops:
  7.2 117.3 %all-gather.13.cloned.1.call-start = ((), (), s32[]{:S(2)}) async-start(), calls=%async_computation.16 | async-start | bytes 2162688 | tf_op jit(solution)/shard_map/all_gather | solution.py:63
  8.0 124.4 %all-gather.15.cloned.1.call-start = ((), (), s32[]{:S(2)}) async-start(), calls=%async_computation.17 | async-start | bytes 2162688 | tf_op jit(solution)/shard_map/all_gather | solution.py:62
  10.9 182.3 %all-to-all-start.2 = ((bf16[32,16,1024]{2,1,0:T(8,128)(2,1)}), bf16[32,16,1024]{2,1,0:T(8,128)(2,1)}, u32[]{:S(2)}, u32[]{:S(2)}) async-start(bf16[32,16,1024]{2,1,0:T(8,128)(2,1)} %bitcast.25), calls=%async_computation.2 | async-start | bytes 2097152 | tf_op jit(solution)/shard_map/all_to_all | solution.py:223
  18.3 172.2 %all-gather.17.cloned.1.call-start = ((), (), s32[]{:S(2)}) async-start(), calls=%async_computation.18 | async-start | bytes 2162688 | tf_op jit(solution)/shard_map/all_gather | solution.py:64
  196.3 52.7 %all-to-all-start.1 = ((bf16[32,32,1024]{2,1,0:T(8,128)(2,1)}), bf16[32,32,1024]{2,1,0:T(8,128)(2,1)}, u32[]{:S(2)}, u32[]{:S(2)}) async-start(bf16[32,32,1024]{2,1,0:T(8,128)(2,1)} %bitcast.389), calls=%async_computation.1 | async-start | bytes 4194304 | tf_op jit(solution)/shard_map/all_to_all | solution.py:220
  249.1 144.2 %all-to-all-start.6 = ((bf16[32,96,1024]{2,1,0:T(8,128)(2,1)}), bf16[32,96,1024]{2,1,0:T(8,128)(2,1)}, u32[]{:S(2)}, u32[]{:S(2)}) async-start(bf16[32,96,1024]{2,1,0:T(8,128)(2,1)} %bitcast.382), calls=%async_computation.6 | async-start | bytes 12582912 | tf_op jit(solution)/shard_map/all_to_all | solution.py:280
  393.2 143.7 %all-to-all-start.8 = ((bf16[32,96,1024]{2,1,0:T(8,128)(2,1)}), bf16[32,96,1024]{2,1,0:T(8,128)(2,1)}, u32[]{:S(2)}, u32[]{:S(2)}) async-start(bf16[32,96,1024]{2,1,0:T(8,128)(2,1)} %bitcast.384), calls=%async_computation.8 | async-start | bytes 12582912 | tf_op jit(solution)/shard_map/all_to_all | solution.py:280
  536.9 143.7 %all-to-all-start = ((bf16[32,96,1024]{2,1,0:T(8,128)(2,1)}), bf16[32,96,1024]{2,1,0:T(8,128)(2,1)}, u32[]{:S(2)}, u32[]{:S(2)}) async-start(bf16[32,96,1024]{2,1,0:T(8,128)(2,1)} %bitcast.385), calls=%async_computation | async-start | bytes 12582912 | tf_op jit(solution)/shard_map/all_to_all | solution.py:250
  680.6 144.0 %all-to-all-start.4 = ((bf16[32,96,1024]{2,1,0:T(8,128)(2,1)}), bf16[32,96,1024]{2,1,0:T(8,128)(2,1)}, u32[]{:S(2)}, u32[]{:S(2)}) async-start(bf16[32,96,1024]{2,1,0:T(8,128)(2,1)} %bitcast.383), calls=%async_computation.4 | async-start | bytes 12582912 | tf_op jit(solution)/shard_map/all_to_all | solution.py:250
  824.6 143.7 %all-to-all-start.3 = ((bf16[32,96,1024]{2,1,0:T(8,128)(2,1)}), bf16[32,96,1024]{2,1,0:T(8,128)(2,1)}, u32[]{:S(2)}, u32[]{:S(2)}) async-start(bf16[32,96,1024]{2,1,0:T(8,128)(2,1)} %convolution_convert_fusion.1), calls=%async_computation.3 | async-start | bytes 12582912 | tf_op jit(solution)/shard_map/all_to_all | solution.py:257
  968.3 143.6 %all-to-all-start.5 = ((bf16[32,96,1024]{2,1,0:T(8,128)(2,1)}), bf16[32,96,1024]{2,1,0:T(8,128)(2,1)}, u32[]{:S(2)}, u32[]{:S(2)}) async-start(bf16[32,96,1024]{2,1,0:T(8,128)(2,1)} %convolution_convert_fusion), calls=%async_computation.5 | async-start | bytes 12582912 | tf_op jit(solution)/shard_map/all_to_all | solution.py:257
  1111.9 154.7 %all-to-all-start.7 = ((bf16[32,96,1024]{2,1,0:T(8,128)(2,1)}), bf16[32,96,1024]{2,1,0:T(8,128)(2,1)}, u32[]{:S(2)}, u32[]{:S(2)}) async-start(bf16[32,96,1024]{2,1,0:T(8,128)(2,1)} %fusion.41), calls=%async_computation.7 | async-start | bytes 12582912 | tf_op jit(solution)/shard_map/all_to_all | solution.py:291
  1115.5 449.2 %all-gather.19.cloned.1.call-start = ((), (), s32[]{:S(2)}) async-start(), calls=%async_computation.19 | async-start | bytes 2162688 | tf_op jit(solution)/shard_map/all_gather | solution.py:64
  1148.0 419.9 %all-gather.25.cloned.1.call-start = ((), (), s32[]{:S(2)}) async-start(), calls=%async_computation.22 | async-start | bytes 2162688 | tf_op jit(solution)/shard_map/all_gather | solution.py:64
  1180.3 570.3 %reduce-scatter.13.cloned.1.call-start = ((), (), s32[]{:S(2)}) async-start(), calls=%async_computation.28 | async-start | bytes 540672
  1188.3 563.7 %all-gather.21.cloned.1.call-start = ((), (), s32[]{:S(2)}) async-start(), calls=%async_computation.20 | async-start | bytes 2162688 | tf_op jit(solution)/shard_map/all_gather | solution.py:62
  1266.6 257.5 %all-to-all-start.9 = ((bf16[32,96,1024]{2,1,0:T(8,128)(2,1)}), bf16[32,96,1024]{2,1,0:T(8,128)(2,1)}, u32[]{:S(2)}, u32[]{:S(2)}) async-start(bf16[32,96,1024]{2,1,0:T(8,128)(2,1)} %fusion.38), calls=%async_computation.9 | async-start | bytes 12582912 | tf_op jit(solution)/shard_map/all_to_all | solution.py:291
  1270.4 483.9 %all-gather.27.cloned.1.call-start = ((), (), s32[]{:S(2)}) async-start(), calls=%async_computation.23 | async-start | bytes 2162688 | tf_op jit(solution)/shard_map/all_gather | solution.py:62
  1271.2 486.5 %all-gather.23.cloned.1.call-start = ((), (), s32[]{:S(2)}) async-start(), calls=%async_computation.21 | async-start | bytes 2162688 | tf_op jit(solution)/shard_map/all_gather | solution.py:63
  1271.9 489.3 %all-gather.29.cloned.1.call-start = ((), (), s32[]{:S(2)}) async-start(), calls=%async_computation.24 | async-start | bytes 2162688 | tf_op jit(solution)/shard_map/all_gather | solution.py:63
  1524.0 337.0 %reduce-scatter.11.cloned.1.call-start = ((), (), s32[]{:S(2)}) async-start(), calls=%async_computation.27 | async-start | bytes 4325376 | tf_op jit(solution)/shard_map/reduce_scatter | solution.py:334
  1564.2 436.8 %reduce-scatter.9.cloned.1.call-start = ((), (), s32[]{:S(2)}) async-start(), calls=%async_computation.26 | async-start | bytes 4325376 | tf_op jit(solution)/shard_map/reduce_scatter | solution.py:333
  1620.9 519.8 %reduce-scatter.7.cloned.1.call-start = ((), (), s32[]{:S(2)}) async-start(), calls=%async_computation.25 | async-start | bytes 4325376 | tf_op jit(solution)/shard_map/reduce_scatter | solution.py:332
  1669.6 63.7 %all-to-all-start.10 = ((bf16[32,2,16384]{2,1,0:T(2,128)(2,1)}), bf16[32,2,16384]{2,1,0:T(2,128)(2,1)S(1)}, u32[]{:S(2)}, u32[]{:S(2)}) async-start(bf16[32,2,16384]{2,1,0:T(2,128)(2,1)} %reshape.1033), calls=%async_computation.13 | async-start | bytes 4194304 | tf_op jit(solution)/shard_map/all_to_all | solution.py:339
  (129 other events, 2471.6 us)
Sparse Core Ops, SparseCore 0:
  10.9 63.0 all-gather.12
  76.8 55.5 all-gather.14
  135.2 55.2 all-gather.16
  1148.1 90.6 all-gather.18
  1241.5 80.7 all-gather.24
  1324.4 142.3 reduce-scatter.12
  1470.0 57.3 all-gather.20
  1530.7 55.1 all-gather.26
  1589.2 60.8 all-gather.22
  1653.2 65.2 all-gather.28
  1721.4 139.6 reduce-scatter.10
  1863.8 137.0 reduce-scatter.8
  2003.9 136.7 reduce-scatter.6
where the time goes:
time: 2150 us
  waiting for transfers between devices  1220 us (57%)
  blocking collectives  350 us (16%)
  local copies, waits for them, and re-layouts  219 us (10%)
  matrix products  171 us (8%)
  other arithmetic  118 us (5%)
  starting transfers between devices  52.7 us (2%)
    all_to_all x2, waiting for transfers between devices, shards(): lax.all_to_all(recv_out.astype(jnp.bfloat16), 'fsdp', split_axis=0, conca...  240 us
    all_to_all x2, waiting for transfers between devices, shards(): lax.all_to_all(buffer.reshape(devices_all, share, D), 'fsdp', split_axis=...  237 us
    all_to_all x2, waiting for transfers between devices, shards(): lax.all_to_all(d_buffer.reshape(devices_all, share, D), 'fsdp', split_axi...  235 us
    all_gather x3, blocking collectives, fetch_attention(): lax.all_gather(router_w, 'fsdp', axis=0, tiled=True)  201 us
    unnamed x3, blocking collectives  149 us
    reduce_scatter x1, waiting for transfers between devices, shards(): lax.psum_scatter(attn_acc[2], 'fsdp', scatter_dimension=0, tiled=True)  140 us
    reduce_scatter x1, waiting for transfers between devices, shards(): lax.psum_scatter(attn_acc[1], 'fsdp', scatter_dimension=0, tiled=True)  140 us
    all_to_all x2, waiting for transfers between devices, shards(): lax.all_to_all(d_served.reshape(devices_all, share, D).astype(jnp.bfloat1...  66.3 us
  transfers between devices with their start and end apart: 25, of which 14 were waited for; matrix products, arithmetic and copies ran while one was open for 23% of the time, Pallas kernels for 0%

commit v1 on v0

v1 whole, which is shorter than its diff:
```python
import functools

import jax
import jax.numpy as jnp
from jax import lax
from jax.experimental import pallas as pl
from jax.experimental.pallas import tpu as pltpu
from jax.sharding import Mesh, PartitionSpec as P

D = 1024
HD = 64
FF = 512
E = 16
MB = 256
GROUPS = 8
PLANE = 8
OWN = E // PLANE
LANES = 128
WIDE = 3 * D + LANES
EPS = 1e-05
NEG = -1e30

BF = jnp.bfloat16
F32 = jnp.float32
PLANE_AXES = ("y", "x", "c")
ALL = ("z", "y", "x", "c")


def dot(a, b, ca=1, cb=0):
    return lax.dot_general(a, b, (((ca,), (cb,)), ((), ())), preferred_element_type=F32)


def mean_rows(v):
    return jnp.sum(v, axis=-1, keepdims=True) * (1.0 / v.shape[-1])


def lane_of(rows):
    return lax.broadcasted_iota(jnp.int32, (rows, LANES), 1)


def turned(t, low):
    return jnp.where(low, pltpu.roll(t, LANES - HD // 2, 1), pltpu.roll(t, HD // 2, 1))


def swap(t):
    return pltpu.roll(t, HD, 1)


def gain_rows(w_ref):
    cols = w_ref[:, 3 * D :].astype(F32).T
    return cols[E : E + 1, :], cols[E + 1 : E + 2, :]


def bias_of(lens_ref, micro):
    row = lax.broadcasted_iota(jnp.int32, (MB, MB), 0)
    col = lax.broadcasted_iota(jnp.int32, (MB, MB), 1)
    start = jnp.zeros((MB, MB), jnp.int32)
    end = jnp.int32(0)
    for s in range(3):
        end = end + lens_ref[micro, s]
        start = jnp.where(row >= end, end, start)
    return jnp.where((col >= start) & (col <= row), 0.0, NEG)


def split_pair(block, half):
    low = lane_of(block.shape[0]) < HD
    other = swap(block)
    here, there = (block, other) if half == 0 else (other, block)
    return jnp.concatenate(
        [jnp.where(low, here, 0.0), jnp.where(low, 0.0, there)], axis=0
    ).astype(BF)


def softmax_pair(score, bias):
    halves = []
    for h in range(2):
        s = score[:, h * MB : (h + 1) * MB] * 0.125 + bias
        e = jnp.exp(s - jnp.max(s, axis=1, keepdims=True))
        halves.append(e * (1.0 / jnp.sum(e, axis=1, keepdims=True)))
    return jnp.concatenate(halves, axis=1)


def attention_forward_kernel(lens_ref, tok_ref, w_ref, cos_ref, sin_ref, nm_ref, q_ref, kv_ref, mixed_ref, resid_ref):
    micro = pl.program_id(0)
    gain_in, gain_mid = gain_rows(w_ref)
    x = tok_ref[...].astype(F32)
    normed = (x * lax.rsqrt(mean_rows(x * x) + EPS) * gain_in).astype(BF)
    q_lin = dot(normed, w_ref[:, :D])
    kv_lin = dot(normed, w_ref[:, D : 2 * D])
    cosine, sine = cos_ref[...], sin_ref[...]
    low = (lane_of(MB) % HD) < HD // 2
    bias = bias_of(lens_ref, micro)
    mixed = []
    for pair in range(GROUPS // 2):
        lanes = slice(pair * LANES, (pair + 1) * LANES)
        k_pair = kv_lin[:, lanes]
        k_pair = k_pair * cosine + turned(k_pair, low) * sine
        v_pair = kv_lin[:, D // 2 + pair * LANES : D // 2 + (pair + 1) * LANES]
        kv_ref[:, lanes] = k_pair.astype(BF)
        kv_ref[:, D // 2 + pair * LANES : D // 2 + (pair + 1) * LANES] = v_pair.astype(BF)
        for half in range(2):
            group = 2 * pair + half
            q = q_lin[:, group * LANES : (group + 1) * LANES]
            q = (q * cosine + turned(q, low) * sine).astype(BF)
            q_ref[:, group * LANES : (group + 1) * LANES] = q
            score = dot(q, split_pair(k_pair, half), 1, 1)
            weight = softmax_pair(score, bias).astype(BF)
            mixed.append(dot(weight, split_pair(v_pair, half)).astype(BF))
    mixed = jnp.concatenate(mixed, axis=1)
    mixed_ref[...] = mixed
    resid = x + dot(mixed, w_ref[:, 2 * D : 3 * D])
    resid_ref[...] = resid
    nm_ref[...] = (resid * lax.rsqrt(mean_rows(resid * resid) + EPS) * gain_mid).astype(BF)


def masked_gates(logits, routed):
    top = jnp.max(jnp.where(routed, logits, NEG), axis=1, keepdims=True)
    e = jnp.where(routed, jnp.exp(jnp.minimum(logits - top, 0.0)), 0.0)
    return e * (1.0 / jnp.sum(e, axis=1, keepdims=True))


def expert_kernel(me_ref, nm_ref, cot_ref, wr_ref, *refs):
    weights = [(refs[2 * e], refs[2 * e + 1]) for e in range(OWN)]
    out_ref, dmid_ref, grad_ref, acc_gu, acc_dn = refs[2 * OWN :]
    step = pl.program_id(0)

    @pl.when(step == 0)
    def _():
        acc_gu[...] = jnp.zeros_like(acc_gu)
        acc_dn[...] = jnp.zeros_like(acc_dn)

    rows = nm_ref.shape[0]
    nm = nm_ref[...]
    cot = cot_ref[:, :D]
    lane = lane_of(rows)
    gates = masked_gates(dot(nm, wr_ref[...]), cot_ref[:, D:].astype(F32) > 0.5)
    out = jnp.zeros((rows, D), F32)
    d_mid = jnp.zeros((rows, D), F32)
    extra = jnp.zeros((rows, LANES), F32)
    for e in range(OWN):
        expert = me_ref[0] * OWN + e
        w_gu = weights[e][0][...].reshape(D, 2 * FF)
        w_dn = weights[e][1][...].reshape(FF, D)
        combine = jnp.sum(jnp.where(lane == expert, gates, 0.0), axis=1, keepdims=True)
        gateup = dot(nm, w_gu)
        gate, up = gateup[:, :FF], gateup[:, FF:]
        s = 1.0 / (1.0 + jnp.exp(-gate))
        silu = gate * s
        act = silu * up
        d_plain = dot(cot, w_dn, 1, 1)
        d_combine = jnp.sum(act * d_plain, axis=1, keepdims=True)
        act = (act * combine).astype(BF)
        out = out + dot(act, w_dn)
        d_act = d_plain * combine
        d_gateup = jnp.concatenate(
            [(d_act * up * (s * (1.0 + gate * (1.0 - s)))).astype(BF), (d_act * silu).astype(BF)], axis=1
        )
        d_mid = d_mid + dot(d_gateup, w_gu, 1, 1)
        acc_gu[e] += dot(nm, d_gateup, 0, 0)
        acc_dn[e] += dot(act, cot, 0, 0)
        high = d_combine.astype(BF).astype(F32)
        extra = extra + jnp.where(lane == expert, high, 0.0) + jnp.where(lane == expert + E, d_combine - high, 0.0)
    out_ref[...] = out.astype(BF)
    dmid_ref[:, :D] = d_mid.astype(BF)
    dmid_ref[:, D:] = extra.astype(BF)

    @pl.when(step == pl.num_programs(0) - 1)
    def _():
        outer = grad_ref.shape[1]
        up_rows, down_rows = D // outer, FF // outer
        for e in range(OWN):
            for z in range(outer):
                grad_ref[e, z, :up_rows] = acc_gu[e, z * up_rows : (z + 1) * up_rows].astype(BF)
                grad_ref[e, z, up_rows:] = acc_dn[e, z * down_rows : (z + 1) * down_rows].astype(BF)


def join_pair(a0, b0, a1, b1, low):
    return jnp.where(low, a0, b1) + swap(jnp.where(low, a1, b0))


def attention_backward_kernel(
    lens_ref, tok_ref, cot_ref, resid_ref, q_ref, kv_ref, mixed_ref, nm_ref, dmid_ref, w_ref, cos_ref, sin_ref,
    rows_ref, grad_ref, acc_ref, gain_ref,
):
    micro = pl.program_id(0)

    @pl.when(micro == 0)
    def _():
        acc_ref[...] = jnp.zeros_like(acc_ref)
        gain_ref[...] = jnp.zeros_like(gain_ref)

    gain_in, gain_mid = gain_rows(w_ref)
    lane = lane_of(MB)
    cot = cot_ref[:, :D].astype(F32)
    resid = resid_ref[...]
    nm = nm_ref[...]
    w_small = w_ref[:, 3 * D :]
    gates = masked_gates(dot(nm, w_small), cot_ref[:, D:].astype(F32) > 0.5)
    pieces = dmid_ref[:, D:].astype(F32)
    d_gates = pieces + pltpu.roll(pieces, LANES - E, 1)
    d_logits = gates * (d_gates - jnp.sum(gates * d_gates, axis=1, keepdims=True))
    d_logits = jnp.where(lane < E, d_logits, 0.0).astype(BF)
    acc_ref[:, 3 * D :] += dot(nm, d_logits, 0, 0)
    d_mid = dmid_ref[:, :D].astype(F32) + dot(d_logits, w_small, 1, 1)
    inverse = lax.rsqrt(mean_rows(resid * resid) + EPS)
    u = d_mid * gain_mid
    d_resid = cot + inverse * u - resid * (inverse * inverse * inverse) * mean_rows(u * resid)
    gain_ref[1:2, :] += jnp.sum(d_mid * resid * inverse, axis=0, keepdims=True)
    d_branch = d_resid.astype(BF)
    acc_ref[:, 2 * D : 3 * D] += dot(mixed_ref[...], d_branch, 0, 0)
    d_mixed = dot(d_branch, w_ref[:, 2 * D : 3 * D], 1, 1).astype(BF)

    cosine, sine = cos_ref[...], sin_ref[...]
    low = (lane % HD) < HD // 2
    head_low = lane < HD
    bias = bias_of(lens_ref, micro)
    d_q, d_k, d_v = [], [], []
    for pair in range(GROUPS // 2):
        k_pair = kv_ref[:, pair * LANES : (pair + 1) * LANES].astype(F32)
        v_pair = kv_ref[:, D // 2 + pair * LANES : D // 2 + (pair + 1) * LANES].astype(F32)
        keys, values = [], []
        for half in range(2):
            group = 2 * pair + half
            q = q_ref[:, group * LANES : (group + 1) * LANES]
            dm = d_mixed[:, group * LANES : (group + 1) * LANES]
            k_two = split_pair(k_pair, half)
            p = softmax_pair(dot(q, k_two, 1, 1), bias)
            d_weight = dot(dm, split_pair(v_pair, half), 1, 1)
            scored = p * d_weight
            d_score = []
            for h in range(2):
                part = slice(h * MB, (h + 1) * MB)
                total = jnp.sum(scored[:, part], axis=1, keepdims=True)
                d_score.append((p[:, part] * (d_weight[:, part] - total)).astype(BF))
            d_score = jnp.concatenate(d_score, axis=1)
            d_query = dot(d_score, k_two) * 0.125
            d_q.append((d_query * cosine - turned(d_query, low) * sine).astype(BF))
            d_key = dot(d_score, q, 0, 0) * 0.125
            d_value = dot(p.astype(BF), dm, 0, 0)
            keys += [d_key[:MB], d_key[MB:]]
            values += [d_value[:MB], d_value[MB:]]
        d_key = join_pair(*keys, head_low)
        d_k.append((d_key * cosine - turned(d_key, low) * sine).astype(BF))
        d_v.append(join_pair(*values, head_low).astype(BF))
    d_q = jnp.concatenate(d_q, axis=1)
    d_kv = jnp.concatenate(d_k + d_v, axis=1)

    x = tok_ref[...].astype(F32)
    inverse = lax.rsqrt(mean_rows(x * x) + EPS)
    normed = (x * inverse * gain_in).astype(BF)
    acc_ref[:, :D] += dot(normed, d_q, 0, 0)
    acc_ref[:, D : 2 * D] += dot(normed, d_kv, 0, 0)
    d_in = dot(d_q, w_ref[:, :D], 1, 1) + dot(d_kv, w_ref[:, D : 2 * D], 1, 1)
    v = d_in * gain_in
    rows_ref[...] = d_resid + inverse * v - x * (inverse * inverse * inverse) * mean_rows(v * x)
    gain_ref[0:1, :] += jnp.sum(d_in * x * inverse, axis=0, keepdims=True)

    @pl.when(micro == pl.num_programs(0) - 1)
    def _():
        grad_ref[:, : 3 * D] = acc_ref[:, : 3 * D].astype(BF)
        gains = jnp.concatenate(
            [jnp.zeros((E, D), F32), gain_ref[...], jnp.zeros((LANES - E - gain_ref.shape[0], D), F32)], axis=0
        )
        grad_ref[:, 3 * D :] = (acc_ref[:, 3 * D :] + gains.T).astype(BF)


def blk(shape, index, buffers=None):
    if buffers is None:
        return pl.BlockSpec(shape, index)
    return pl.BlockSpec(shape, index, pipeline_mode=pl.Buffered(buffers))


def kernel_params(mib=58):
    return pltpu.CompilerParams(dimension_semantics=("arbitrary",), vmem_limit_bytes=mib << 20)


def rows_spec(width):
    return blk((MB, width), lambda i, *_: (i, 0))


def attention_forward(tokens, lengths, packed, cosine, sine):
    rows = tokens.shape[0]
    shape = jax.ShapeDtypeStruct
    return pl.pallas_call(
        attention_forward_kernel,
        grid_spec=pltpu.PrefetchScalarGridSpec(
            num_scalar_prefetch=1,
            grid=(rows // MB,),
            in_specs=[
                rows_spec(D),
                blk((D, WIDE), lambda i, *_: (0, 0), 1),
                rows_spec(LANES),
                rows_spec(LANES),
            ],
            out_specs=[rows_spec(D)] * 5,
        ),
        out_shape=[shape((rows, D), BF)] * 4 + [shape((rows, D), F32)],
        compiler_params=kernel_params(),
        name="attention_forward",
    )(lengths, tokens, packed, cosine, sine)


def experts(me, nm, cot, packed, homes, step_rows=512):
    rows = nm.shape[0]
    outer = homes[0].shape[0]
    up_rows, down_rows = D // outer, FF // outer
    shape = jax.ShapeDtypeStruct
    spec = lambda width: blk((step_rows, width), lambda i, *_: (i, 0))
    home_specs, home_args = [], []
    for home in homes:
        home_specs += [
            blk((outer, up_rows, D), lambda i, *_: (0, 0, 0), 1),
            blk((outer, down_rows, D), lambda i, *_: (0, 2, 0), 1),
        ]
        home_args += [home, home]
    return pl.pallas_call(
        expert_kernel,
        grid_spec=pltpu.PrefetchScalarGridSpec(
            num_scalar_prefetch=1,
            grid=(rows // step_rows,),
            in_specs=[spec(D), spec(D + LANES), blk((D, LANES), lambda i, *_: (0, 3 * D // LANES), 1)] + home_specs,
            out_specs=[
                spec(D),
                spec(D + LANES),
                blk((OWN, outer, up_rows + down_rows, D), lambda i, *_: (0, 0, 0, 0), 1),
            ],
            scratch_shapes=[pltpu.VMEM((OWN, D, 2 * FF), F32), pltpu.VMEM((OWN, FF, D), F32)],
        ),
        out_shape=[
            shape((rows, D), BF),
            shape((rows, D + LANES), BF),
            shape((OWN, outer, up_rows + down_rows, D), BF),
        ],
        compiler_params=kernel_params(),
        name="experts",
    )(me, nm, cot, packed, *home_args)


def attention_backward(tokens, lengths, cot, resid, q, kv, mixed, nm, d_mid, packed, cosine, sine):
    rows = tokens.shape[0]
    shape = jax.ShapeDtypeStruct
    return pl.pallas_call(
        attention_backward_kernel,
        grid_spec=pltpu.PrefetchScalarGridSpec(
            num_scalar_prefetch=1,
            grid=(rows // MB,),
            in_specs=[
                rows_spec(D),
                rows_spec(D + LANES),
                rows_spec(D),
                rows_spec(D),
                rows_spec(D),
                rows_spec(D),
                rows_spec(D),
                rows_spec(D + LANES),
                blk((D, WIDE), lambda i, *_: (0, 0), 1),
                rows_spec(LANES),
                rows_spec(LANES),
            ],
            out_specs=[rows_spec(D), blk((D, WIDE), lambda i, *_: (0, 0), 1)],
            scratch_shapes=[pltpu.VMEM((D, WIDE), F32), pltpu.VMEM((8, D), F32)],
        ),
        out_shape=[shape((rows, D), F32), shape((D, WIDE), BF)],
        compiler_params=kernel_params(),
        name="attention_backward",
    )(lengths, tokens, cot, resid, q, kv, mixed, nm, d_mid, packed, cosine, sine)


def rope_tables(lengths):
    ends = jnp.stack([jnp.sum(lengths[:, : s + 1], axis=1) for s in range(lengths.shape[1] - 1)], axis=1)
    index = jnp.arange(MB, dtype=jnp.int32)
    start = jnp.max(jnp.where(ends[:, None, :] <= index[None, :, None], ends[:, None, :], 0), axis=2)
    position = (index[None, :] - start).astype(F32).reshape(-1)
    lane = jnp.arange(LANES, dtype=jnp.int32)
    freq = jnp.exp(-((2 * (lane % (HD // 2))).astype(F32) / HD) * jnp.log(10000.0))
    angle = position[:, None] * freq[None, :]
    sign = jnp.where(lane % HD < HD // 2, -1.0, 1.0)
    return jnp.cos(angle), jnp.sin(angle) * sign[None, :]


def gather(v, axes):
    return lax.all_gather(v, axes, axis=0, tiled=True)


def scatter_sum(v, axes, dim=0):
    return lax.psum_scatter(v, axes, scatter_dimension=dim, tiled=True)


def shards(tokens, cotangent, lengths, routes, attn_gain, w_query, w_keyval, w_out, moe_gain, w_router, w_gateup, w_down):
    rows, share = tokens.shape[0], w_query.shape[0]
    outer = lax.axis_size("z")
    me = lax.axis_index(PLANE_AXES).astype(jnp.int32).reshape(1)

    small = jnp.concatenate(
        [w_router, attn_gain[:, None], moe_gain[:, None], jnp.zeros((share, LANES - E - 2), BF)], axis=1
    )
    packed = gather(jnp.concatenate([w_query, w_keyval, w_out, small], axis=1), ALL)

    sent = jnp.concatenate([w_gateup, w_down], axis=1)
    own = lax.all_to_all(sent.reshape(PLANE, OWN, *sent.shape[1:]), PLANE_AXES, split_axis=0, concat_axis=0, tiled=True)
    homes = []
    for e in range(OWN):
        home = jnp.concatenate(
            [own[:, e, :share].reshape(PLANE * share, D), own[:, e, share:].reshape(PLANE * share // 2, D)], axis=0
        )
        homes.append(gather(home, "z").reshape(outer, -1, D))

    hot = jnp.sum((routes[:, :, None] == jnp.arange(LANES, dtype=jnp.int32)[None, None, :]).astype(F32), axis=1)
    cot = jnp.concatenate([cotangent, hot.astype(BF)], axis=1)
    cot_all = gather(cot, PLANE_AXES)

    cosine, sine = rope_tables(lengths)
    nm, q, kv, mixed, resid = attention_forward(tokens, lengths, packed, cosine, sine)
    nm_all = gather(nm, PLANE_AXES)
    out_part, d_mid_part, expert_grads = experts(me, nm_all, cot_all, packed, homes)
    d_mid = scatter_sum(d_mid_part, PLANE_AXES)
    out_sum = scatter_sum(out_part, PLANE_AXES)
    output = (resid + out_sum.astype(F32)).astype(BF)
    grad_tokens, grads = attention_backward(tokens, lengths, cot, resid, q, kv, mixed, nm, d_mid, packed, cosine, sine)
    grads = scatter_sum(grads.reshape(outer, PLANE * share, WIDE), PLANE_AXES, 1)
    grads = scatter_sum(grads.reshape(outer * share, WIDE), "z").astype(F32)

    back = []
    for e in range(OWN):
        summed = scatter_sum(expert_grads[e].reshape(-1, D), "z")
        back.append(
            jnp.concatenate(
                [
                    summed[: PLANE * share].reshape(PLANE, share, D),
                    summed[PLANE * share :].reshape(PLANE, share // 2, D),
                ],
                axis=1,
            )
        )
    back = lax.all_to_all(jnp.stack(back, axis=1), PLANE_AXES, split_axis=0, concat_axis=0, tiled=True)
    back = back.reshape(E, -1, D).astype(F32)
    return (
        output,
        grad_tokens,
        grads[:, 3 * D + E],
        grads[:, :D],
        grads[:, D : 2 * D],
        grads[:, 2 * D : 3 * D],
        grads[:, 3 * D + E + 1],
        grads[:, 3 * D : 3 * D + E],
        back[:, :share],
        back[:, share:],
    )


def solution(mesh):
    count = mesh.shape["fsdp"]
    inner = Mesh(mesh.devices.reshape(count // PLANE, 2, 2, 2), ALL)
    row, vec, mid = P(ALL, None), P(ALL), P(None, ALL, None)
    return jax.shard_map(
        shards,
        mesh=inner,
        in_specs=(row, row, row, row, vec, row, row, row, vec, row, mid, mid),
        out_specs=(row, row, vec, row, row, row, vec, row, mid, mid),
        check_vma=False,
    )
```

time: 2150 us -> 809 us (0.38)
  waiting for transfers between devices: 1220 us -> 582 us
  blocking collectives: 350 us -> 27.4 us
  local copies, waits for them, and re-layouts: 219 us -> 18 us
  matrix products: 171 us -> 0 us
  Pallas kernels: 0 us -> 148 us
  other arithmetic: 118 us -> 15 us
  starting transfers between devices: 52.7 us -> 4.28 us
    all_to_all x12 -> x1, waiting for transfers between devices: 841 us -> 0.01 us  [shards(): lax.all_to_all(jnp.stack(back, axis=1), PLANE_AXES, split_axis=0, concat_...]
    all_gather x9 -> x5, waiting for transfers between devices: 44.5 us -> 265 us  [gather(): return lax.all_gather(v, axes, axis=0, tiled=True)]
    all_gather x3 -> x0, blocking collectives: 201 us -> none  [fetch_attention(): lax.all_gather(router_w, 'fsdp', axis=0, tiled=True)]
    dot_general x48 -> x0, matrix products: 171 us -> none  [the longest x2 22.9 us: expert_backward(): jnp.einsum('ecf,edf->ecd', d_gateup, gateup_w, preferred_element_type=jnp...]
    unnamed x3 -> x0, blocking collectives: 149 us -> none
    pallas_call x0 -> x3, Pallas kernels: none -> 148 us  [the longest x1 95.7 us: experts(): pl.pallas_call(expert_kernel, grid_spec=pltpu.PrefetchScalarGridSpec(num_...]
    gather x8 -> x0, local copies, waits for them, and re-layouts: 131 us -> none  [the longest x2 37.4 us: shards(): d_buffer = padded_grads[filler]]
    all_to_all x12 -> x1, starting transfers between devices: 51.2 us -> 3.66 us  [shards(): lax.all_to_all(jnp.stack(back, axis=1), PLANE_AXES, split_axis=0, concat_...]
  transfers between devices with their start and end apart: 25 -> 12, of which waited for: 14 -> 11; matrix products, arithmetic and copies ran while one was open for 23% -> 3% of each run, Pallas kernels for 0% -> 6%
where the time goes in v1:
time: 809 us
  waiting for transfers between devices  582 us (72%)
  Pallas kernels  148 us (18%)
  blocking collectives  27.4 us (3%)
  local copies, waits for them, and re-layouts  18 us (2%)
  other arithmetic  15 us (2%)
  between operations  14 us (2%)
    reduce_scatter x6, waiting for transfers between devices, scatter_sum(): return lax.psum_scatter(v, axes, scatter_dimension=dim, tiled=True)  315 us
    all_gather x5, waiting for transfers between devices, gather(): return lax.all_gather(v, axes, axis=0, tiled=True)  265 us
    pallas_call x1, Pallas kernels, experts(): pl.pallas_call(expert_kernel, grid_spec=pltpu.PrefetchScalarGridSpec(num_...  95.7 us
    pallas_call x1, Pallas kernels, attention_backward(): pl.pallas_call(attention_backward_kernel, grid_spec=pltpu.PrefetchScalarG...  34.3 us
    all_to_all x1, blocking collectives, shards(): lax.all_to_all(sent.reshape(PLANE, OWN, *sent.shape[1:]), PLANE_AXES, spl...  27.4 us
    pallas_call x1, Pallas kernels, attention_forward(): pl.pallas_call(attention_forward_kernel, grid_spec=pltpu.PrefetchScalarGr...  18.2 us
  transfers between devices with their start and end apart: 12, of which 11 were waited for; matrix products, arithmetic and copies ran while one was open for 3% of the time, Pallas kernels for 6%

profile of v1, /device:TPU:0, one launch (start us, length us, event | category | flops | bytes accessed | tf_op | source)
XLA Modules:
  0.0 808.7 jit_solution(4130223370904736643)
XLA Ops:
  9.5 1.7 concatenate.21
  11.2 1.5 pad_maximum_fusion
  12.8 27.4 %all_to_all.10 = bf16[8,2,48,1024]{3,2,1,0:T(8,128)(2,1)S(1)} all-to-all(bf16[8,2,48,1024]{3,2,1,0:T(8,128)(2,1)S(1)} %bitcast.38), channel_id=1, replica_groups=mesh['z'=4,'y'=2,'x'=2,'c'=2] {'y','x','c'}, dimensions={0} | all-to-all | bytes 3145728 | tf_op jit(solution)/shard_map/all_to_all | solution.py:400
  42.5 2.9 convert_reduce_fusion
  47.1 1.8 fusion
  48.9 39.0 %all-gather.6.cloned.1.call-done.w_ref.wr_ref = bf16[1024,3200]{1,0:T(8,128)(2,1)} async-done(((bf16[32,3200]{1,0:T(8,128)(2,1)}), bf16[1024,3200]{1,0:T(8,128)(2,1)}) %all-gather.6.cloned.1.call-update) | async-done | bytes 6553616 | tf_op jit(solution)/shard_map/all_gather | solution.py:382
  87.9 18.2 %attention_forward.1 = (bf16[512,1024]{1,0:T(8,128)(2,1)}, bf16[512,1024]{1,0:T(8,128)(2,1)}, bf16[512,1024]{1,0:T(8,128)(2,1)}, bf16[512,1024]{1,0:T(8,128)(2,1)}, f32[512,1024]{1,0:T(8,128)}) custom-call(s32[2,4]{1,0:T(2,128)} %lens_ref.3, bf16[512,1024]{1,0:T(8,128)(2,1)} %tok_ref.3, bf16[1024,3200]{1,0:T(8,128)(2,1)} %all-gather.6.cloned.1.call-done.w_ref.wr_ref, ...), custom_call_target="tpu_custom_call" | custom-call | tf_op jit(solution)/shard_map/attention_forward/pallas_call | solution.py:284
  106.4 45.7 %all-gather.12.cloned.1.call-done = bf16[1536,1024]{1,0:T(8,128)(2,1)} async-done(((bf16[384,1024]{1,0:T(8,128)(2,1)}), bf16[1536,1024]{1,0:T(8,128)(2,1)}) %all-gather.12.cloned.1.call-update) | async-done | bytes 3145744 | tf_op jit(solution)/shard_map/all_gather | solution.py:382
  152.1 63.8 %all-gather.14.cloned.1.call-done = bf16[1536,1024]{1,0:T(8,128)(2,1)} async-done(((bf16[384,1024]{1,0:T(8,128)(2,1)}), bf16[1536,1024]{1,0:T(8,128)(2,1)}) %all-gather.14.cloned.1.call-update) | async-done | bytes 3145744 | tf_op jit(solution)/shard_map/all_gather | solution.py:382
  215.9 59.8 %all-gather.10.cloned.1.call-done.cot_ref = bf16[4096,1152]{1,0:T(8,128)(2,1)} async-done(((bf16[512,1152]{1,0:T(8,128)(2,1)}), bf16[4096,1152]{1,0:T(8,128)(2,1)}) %all-gather.10.cloned.1.call-update) | async-done | bytes 9437200 | tf_op jit(solution)/shard_map/all_gather | solution.py:382
  275.7 56.7 %all-gather.8.cloned.1.call-done.nm_ref = bf16[4096,1024]{1,0:T(8,128)(2,1)} async-done(((bf16[512,1024]{1,0:T(8,128)(2,1)}), bf16[4096,1024]{1,0:T(8,128)(2,1)}) %all-gather.8.cloned.1.call-update) | async-done | bytes 8388624 | tf_op jit(solution)/shard_map/all_gather | solution.py:382
  332.4 95.7 %experts.1 = (bf16[4096,1024]{1,0:T(8,128)(2,1)}, bf16[4096,1152]{1,0:T(8,128)(2,1)}, bf16[2,4,384,1024]{3,2,1,0:T(8,128)(2,1)}) custom-call(s32[1]{0:T(128)} %bitcast.4.me_ref, bf16[4096,1024]{1,0:T(8,128)(2,1)} %all-gather.8.cloned.1.call-done.nm_ref, bf16[4096,1152]{1,0:T(8,128)(2,1)} %all-gather.10.cloned.1.call-done.cot_ref, ...), custom_call_target="tpu_custom_call" | custom-call | tf_op jit(solution)/shard_map/experts/pallas_call | solution.py:316
  428.2 6.4 fusion.8
  435.4 69.4 %reduce-scatter.9.cloned.1.call-done.dmid_ref = bf16[512,1152]{1,0:T(8,128)(2,1)} async-done(((bf16[4096,1152]{1,0:T(8,128)(2,1)}), bf16[512,1152]{1,0:T(8,128)(2,1)}) %reduce-scatter.9.cloned.1.call-update) | async-done | bytes 1179664 | tf_op jit(solution)/shard_map/reduce_scatter | solution.py:386
  504.8 34.3 %attention_backward.1 = (f32[512,1024]{1,0:T(8,128)}, bf16[1024,3200]{1,0:T(8,128)(2,1)}) custom-call(s32[2,4]{1,0:T(2,128)} %lens_ref.3, bf16[512,1024]{1,0:T(8,128)(2,1)} %tok_ref.3, bf16[512,1152]{1,0:T(8,128)(2,1)} %pad_maximum_fusion.2.cot_ref, f32[512,1024]{1,0:T(8,128)} %get-tuple-element.20.resid_ref, bf16[512,1024]{1,0:T(8,128)(2,1)} %get-tuple-element.23.q_ref, ...), custom_call_target="tpu_custom_call" | custom-call | tf_op jit(solution)/shard_map/attention_backward/pallas_call | solution.py:342
  539.7 27.7 %reduce-scatter.15.cloned.1.call-done = bf16[384,1024]{1,0:T(8,128)(2,1)} async-done(((bf16[1536,1024]{1,0:T(8,128)(2,1)}), bf16[384,1024]{1,0:T(8,128)(2,1)}) %reduce-scatter.15.cloned.1.call-update) | async-done | bytes 786448 | tf_op jit(solution)/shard_map/reduce_scatter | solution.py:386
  567.4 62.6 %reduce-scatter.17.cloned.1.call-done = bf16[384,1024]{1,0:T(8,128)(2,1)} async-done(((bf16[1536,1024]{1,0:T(8,128)(2,1)}), bf16[384,1024]{1,0:T(8,128)(2,1)}) %reduce-scatter.17.cloned.1.call-update) | async-done | bytes 786448 | tf_op jit(solution)/shard_map/reduce_scatter | solution.py:386
  632.5 3.7 all-to-all-start.1
  636.2 60.3 %reduce-scatter.11.cloned.1.call-done = bf16[4,32,3200]{2,1,0:T(8,128)(2,1)} async-done(((bf16[4,256,3200]{2,1,0:T(8,128)(2,1)}), bf16[4,32,3200]{2,1,0:T(8,128)(2,1)}) %reduce-scatter.11.cloned.1.call-update) | async-done | bytes 819216 | tf_op jit(solution)/shard_map/reduce_scatter | solution.py:386
  698.1 1.5 slice.98
  699.6 71.9 %reduce-scatter.7.cloned.1.call-done = bf16[512,1024]{1,0:T(8,128)(2,1)} async-done(((bf16[4096,1024]{1,0:T(8,128)(2,1)}), bf16[512,1024]{1,0:T(8,128)(2,1)}) %reduce-scatter.7.cloned.1.call-update) | async-done | bytes 1048592 | tf_op jit(solution)/shard_map/reduce_scatter | solution.py:386
  771.5 2.5 add_convert_fusion
  774.0 23.4 %reduce-scatter.13.cloned.1.call-done = bf16[32,3200]{1,0:T(8,128)(2,1)} async-done(((bf16[128,3200]{1,0:T(8,128)(2,1)}), bf16[32,3200]{1,0:T(8,128)(2,1)}) %reduce-scatter.13.cloned.1.call-update) | async-done | bytes 204816 | tf_op jit(solution)/shard_map/reduce_scatter | solution.py:386
  800.5 1.7 fusion.11
  (66 shorter events, 15.0 us)
Async XLA Ops:
  7.2 80.8 %all-gather.6.cloned.1.call-start = ((), (), s32[]{:S(2)}) async-start(), calls=%async_computation.8 | async-start | bytes 6758400 | tf_op jit(solution)/shard_map/all_gather | solution.py:382
  11.2 140.9 %all-gather.12.cloned.1.call-start = ((), (), s32[]{:S(2)}) async-start(), calls=%async_computation.11 | async-start | bytes 3932160 | tf_op jit(solution)/shard_map/all_gather | solution.py:382
  40.3 2.1 copy-start.2
  41.3 4.2 copy-start.1
  41.3 174.6 %all-gather.14.cloned.1.call-start = ((), (), s32[]{:S(2)}) async-start(), calls=%async_computation.12 | async-start | bytes 3932160 | tf_op jit(solution)/shard_map/all_gather | solution.py:382
  42.3 4.3 copy-start.3
  42.3 233.4 %all-gather.10.cloned.1.call-start = ((), (), s32[]{:S(2)}) async-start(), calls=%async_computation.10 | async-start | bytes 10616832 | tf_op jit(solution)/shard_map/all_gather | solution.py:382
  46.6 285.8 %all-gather.8.cloned.1.call-start = ((), (), s32[]{:S(2)}) async-start(), calls=%async_computation.9 | async-start | bytes 9437184 | tf_op jit(solution)/shard_map/all_gather | solution.py:382
  106.2 398.6 %reduce-scatter.9.cloned.1.call-start = ((), (), s32[]{:S(2)}) async-start(), calls=%async_computation.14 | async-start | bytes 10616832 | tf_op jit(solution)/shard_map/reduce_scatter | solution.py:386
  428.1 139.2 %reduce-scatter.15.cloned.1.call-start = ((), (), s32[]{:S(2)}) async-start(), calls=%async_computation.17 | async-start | bytes 3932160 | tf_op jit(solution)/shard_map/reduce_scatter | solution.py:386
  434.6 195.4 %reduce-scatter.17.cloned.1.call-start = ((), (), s32[]{:S(2)}) async-start(), calls=%async_computation.18 | async-start | bytes 3932160 | tf_op jit(solution)/shard_map/reduce_scatter | solution.py:386
  435.4 261.1 %reduce-scatter.11.cloned.1.call-start = ((), (), s32[]{:S(2)}) async-start(), calls=%async_computation.15 | async-start | bytes 7372800 | tf_op jit(solution)/shard_map/reduce_scatter | solution.py:386
  539.1 232.4 %reduce-scatter.7.cloned.1.call-start = ((), (), s32[]{:S(2)}) async-start(), calls=%async_computation.13 | async-start | bytes 9437184 | tf_op jit(solution)/shard_map/reduce_scatter | solution.py:386
  567.4 62.6 %slice-start = ((bf16[384,1024]{1,0:T(8,128)(2,1)}), bf16[128,1024]{1,0:T(8,128)(2,1)S(1)}, s32[]{:S(2)}) async-start(bf16[384,1024]{1,0:T(8,128)(2,1)} %reduce-scatter.15.cloned.1.call-done), calls=%async_computation.19 | async-start | bytes 524288 | tf_op jit(solution)/shard_map/slice | solution.py:430
  567.4 62.6 %slice-start.1 = ((bf16[384,1024]{1,0:T(8,128)(2,1)}), bf16[256,1024]{1,0:T(8,128)(2,1)S(1)}, s32[]{:S(2)}) async-start(bf16[384,1024]{1,0:T(8,128)(2,1)} %reduce-scatter.15.cloned.1.call-done), calls=%async_computation.20 | async-start | bytes 1048576 | tf_op jit(solution)/shard_map/slice | solution.py:429
  630.0 0.9 slice-start.2
  630.0 1.1 slice-start.3
  632.5 64.1 %all-to-all-start.1 = ((bf16[8,2,48,1024]{3,2,1,0:T(8,128)(2,1)}), bf16[8,2,48,1024]{3,2,1,0:T(8,128)(2,1)S(1)}, u32[]{:S(2)}, u32[]{:S(2)}) async-start(bf16[8,2,48,1024]{3,2,1,0:T(8,128)(2,1)} %pad_maximum_fusion.1), calls=%async_computation.7 | async-start | bytes 3145728 | tf_op jit(solution)/shard_map/all_to_all | solution.py:435
  636.1 161.3 %reduce-scatter.13.cloned.1.call-start = ((), (), s32[]{:S(2)}) async-start(), calls=%async_computation.16 | async-start | bytes 1024000 | tf_op jit(solution)/shard_map/reduce_scatter | solution.py:386
  698.1 73.4 %copy-start = (f32[512,1024]{1,0:T(8,128)S(1)}, f32[512,1024]{1,0:T(8,128)}, u32[]{:S(2)}) copy-start(f32[512,1024]{1,0:T(8,128)} %get-tuple-element.20.resid_ref) | copy-start | bytes 6291460
Sparse Core Ops, SparseCore 0:
  11.4 76.4 all-gather.5
  90.1 62.0 all-gather.11
  153.7 62.1 all-gather.13
  218.2 57.4 all-gather.9
  278.0 54.3 all-gather.7
  428.3 76.4 reduce-scatter.8
  507.1 60.2 reduce-scatter.14
  569.7 60.2 reduce-scatter.16
  633.5 63.0 reduce-scatter.10
  700.2 71.2 reduce-scatter.6
  773.8 23.6 reduce-scatter.12

commit v2 on v1

v2 whole, which is shorter than its diff:
```python
import functools

import jax
import jax.numpy as jnp
from jax import lax
from jax.experimental import pallas as pl
from jax.experimental.pallas import tpu as pltpu
from jax.sharding import Mesh, PartitionSpec as P

D = 1024
HD = 64
FF = 512
E = 16
MB = 256
GROUPS = 8
PLANE = 8
OWN = E // PLANE
LANES = 128
WIDE = 3 * D + LANES
DMID = D + LANES
EPS = 1e-05
NEG = -1e30

BF = jnp.bfloat16
F32 = jnp.float32
PLANE_AXES = ("y", "x", "c")
ALL = ("z", "y", "x", "c")


def dot(a, b, ca=1, cb=0):
    return lax.dot_general(a, b, (((ca,), (cb,)), ((), ())), preferred_element_type=F32)


def mean_rows(v):
    return jnp.sum(v, axis=-1, keepdims=True) * (1.0 / v.shape[-1])


def lane_of(rows):
    return lax.broadcasted_iota(jnp.int32, (rows, LANES), 1)


def turned(t, low):
    return jnp.where(low, pltpu.roll(t, LANES - HD // 2, 1), pltpu.roll(t, HD // 2, 1))


def swap(t):
    return pltpu.roll(t, HD, 1)


def gain_rows(w_ref):
    cols = w_ref[:, 3 * D :].astype(F32).T
    return cols[E : E + 1, :], cols[E + 1 : E + 2, :]


def bias_of(lens_ref, micro):
    row = lax.broadcasted_iota(jnp.int32, (MB, MB), 0)
    col = lax.broadcasted_iota(jnp.int32, (MB, MB), 1)
    start = jnp.zeros((MB, MB), jnp.int32)
    end = jnp.int32(0)
    for s in range(3):
        end = end + lens_ref[micro, s]
        start = jnp.where(row >= end, end, start)
    return jnp.where((col >= start) & (col <= row), 0.0, NEG)


def split_pair(block, half):
    low = lane_of(block.shape[0]) < HD
    other = swap(block)
    here, there = (block, other) if half == 0 else (other, block)
    return jnp.concatenate(
        [jnp.where(low, here, 0.0), jnp.where(low, 0.0, there)], axis=0
    ).astype(BF)


def softmax_pair(score, bias):
    halves = []
    for h in range(2):
        s = score[:, h * MB : (h + 1) * MB] * 0.125 + bias
        e = jnp.exp(s - jnp.max(s, axis=1, keepdims=True))
        halves.append(e * (1.0 / jnp.sum(e, axis=1, keepdims=True)))
    return jnp.concatenate(halves, axis=1)


def attention_forward_kernel(
    micro, outer, place_ref, lens_ref, tok_ref, cot_ref, w_ref, cos_ref, sin_ref,
    nm_ref, q_ref, kv_ref, mixed_ref, resid_ref, weight_ref, *ordering,
):
    if not micro:
        ordered_ref, w_all, sems, out_sem = ordering
        share = D // outer // PLANE
        copies = []
        for p in range(PLANE):
            for s in range(outer):
                z = lax.rem(place_ref[1] + outer - s, outer)
                at = pl.ds(pl.multiple_of((z * PLANE + p) * share, share), share)
                block = w_ref.at[(p * outer + s) * share : (p * outer + s + 1) * share]
                copies.append(pltpu.make_async_copy(block, w_all.at[at], sems.at[p * outer + s]))
        for copy in copies:
            copy.start()
        for copy in copies:
            copy.wait()
        write = pltpu.make_async_copy(w_all, ordered_ref, out_sem)
        write.start()
        w_ref = w_all
    gain_in, gain_mid = gain_rows(w_ref)
    x = tok_ref[...].astype(F32)
    normed = (x * lax.rsqrt(mean_rows(x * x) + EPS) * gain_in).astype(BF)
    q_lin = dot(normed, w_ref[:, :D])
    kv_lin = dot(normed, w_ref[:, D : 2 * D])
    cosine, sine = cos_ref[...], sin_ref[...]
    low = (lane_of(MB) % HD) < HD // 2
    bias = bias_of(lens_ref, micro)
    mixed = []
    for pair in range(GROUPS // 2):
        lanes = slice(pair * LANES, (pair + 1) * LANES)
        k_pair = kv_lin[:, lanes]
        k_pair = k_pair * cosine + turned(k_pair, low) * sine
        v_pair = kv_lin[:, D // 2 + pair * LANES : D // 2 + (pair + 1) * LANES]
        kv_ref[:, lanes] = k_pair.astype(BF)
        kv_ref[:, D // 2 + pair * LANES : D // 2 + (pair + 1) * LANES] = v_pair.astype(BF)
        for half in range(2):
            group = 2 * pair + half
            q = q_lin[:, group * LANES : (group + 1) * LANES]
            q = (q * cosine + turned(q, low) * sine).astype(BF)
            q_ref[:, group * LANES : (group + 1) * LANES] = q
            score = dot(q, split_pair(k_pair, half), 1, 1)
            weight = softmax_pair(score, bias).astype(BF)
            weight_ref[:, group * 2 * MB : (group + 1) * 2 * MB] = weight
            mixed.append(dot(weight, split_pair(v_pair, half)).astype(BF))
    mixed = jnp.concatenate(mixed, axis=1)
    mixed_ref[...] = mixed
    resid = x + dot(mixed, w_ref[:, 2 * D : 3 * D])
    resid_ref[...] = resid
    nm_ref[:, -D:] = (resid * lax.rsqrt(mean_rows(resid * resid) + EPS) * gain_mid).astype(BF)
    if micro:
        nm_ref[:, :DMID] = cot_ref[...]
    else:
        write.wait()


def masked_gates(logits, routed):
    top = jnp.max(jnp.where(routed, logits, NEG), axis=1, keepdims=True)
    e = jnp.where(routed, jnp.exp(jnp.minimum(logits - top, 0.0)), 0.0)
    return e * (1.0 / jnp.sum(e, axis=1, keepdims=True))


def plane_back(place_ref, s, outer, rows):
    z = lax.rem(place_ref[1] + outer - s, outer)
    return pl.ds(pl.multiple_of(z * rows, rows), rows)


def expert_kernel(outer, micro, e, *refs):
    refs = list(refs)
    take = lambda k: [refs.pop(0) for _ in range(k)]
    place_ref, *peers = take(3 if micro else 5)
    wr_ref = take(1)[0]
    homes = take(outer)
    partial_ref = take(1)[0] if e else None
    carried = take(2) if micro else []
    out_ref = take(1)[0]
    dmid_refs = take(2) if micro and e else []
    grads = take(outer) if micro else []
    acc_gu, acc_dn, w_gu, w_dn, sems = take(5)
    old_gu, old_dn = take(2) if micro else (None, None)
    step = pl.program_id(0)
    up_rows, down_rows = D // outer, FF // outer

    def old_copies():
        return [
            pltpu.make_async_copy(source, target, sems.at[outer, k])
            for k, (source, target) in enumerate(zip(carried, (old_gu, old_dn)))
        ]

    @pl.when(step == 0)
    def _():
        copies = []
        for s in range(outer):
            copies += [
                pltpu.make_async_copy(
                    homes[s].at[:up_rows], w_gu.at[plane_back(place_ref, s, outer, up_rows)], sems.at[s, 0]
                ),
                pltpu.make_async_copy(
                    homes[s].at[up_rows:], w_dn.at[plane_back(place_ref, s, outer, down_rows)], sems.at[s, 1]
                ),
            ]
        for copy in copies + (old_copies() if micro else []):
            copy.start()
        acc_gu[...] = jnp.zeros_like(acc_gu)
        acc_dn[...] = jnp.zeros_like(acc_dn)
        for copy in copies:
            copy.wait()

    cots, nms = (peers, peers) if micro else (peers[:2], peers[2:])
    nm = jnp.concatenate([ref[:, -D:] for ref in nms], axis=0)
    cot = jnp.concatenate([ref[:, :D] for ref in cots], axis=0)
    hot = jnp.concatenate([ref[:, D:DMID] for ref in cots], axis=0).astype(F32)
    lane = lane_of(nm.shape[0])
    gates = masked_gates(dot(nm, wr_ref[...]), hot > 0.5)
    expert = place_ref[0] * OWN + e
    combine = jnp.sum(jnp.where(lane == expert, gates, 0.0), axis=1, keepdims=True)
    gateup = dot(nm, w_gu[...])
    gate, up = gateup[:, :FF], gateup[:, FF:]
    s = 1.0 / (1.0 + jnp.exp(-gate))
    silu = gate * s
    act = silu * up
    d_plain = dot(cot, w_dn[...], 1, 1)
    d_combine = jnp.sum(act * d_plain, axis=1, keepdims=True)
    act = (act * combine).astype(BF)
    out = dot(act, w_dn[...])
    d_act = d_plain * combine
    d_gateup = jnp.concatenate(
        [(d_act * up * (s * (1.0 + gate * (1.0 - s)))).astype(BF), (d_act * silu).astype(BF)], axis=1
    )
    d_mid = dot(d_gateup, w_gu[...], 1, 1)
    acc_gu[...] += dot(nm, d_gateup, 0, 0)
    acc_dn[...] += dot(act, cot, 0, 0)
    high = d_combine.astype(BF).astype(F32)
    extra = jnp.where(lane == expert, high, 0.0) + jnp.where(lane == expert + E, d_combine - high, 0.0)
    if e:
        d_mid = d_mid + partial_ref[:, :D].astype(F32)
        extra = extra + partial_ref[:, D:DMID].astype(F32)
        out = out + partial_ref[:, DMID:].astype(F32)
    d_mid = jnp.concatenate([d_mid.astype(BF), extra.astype(BF)], axis=1)
    out = out.astype(BF)
    if not e:
        out_ref[:, :DMID] = d_mid
        out_ref[:, DMID:] = out
    else:
        core = lax.rem(place_ref[0], 2)
        for half in range(2):
            part = slice(half * MB, (half + 1) * MB)
            at = pl.ds(pl.multiple_of((core if half == 0 else 1 - core) * MB, MB), MB)
            if micro:
                out_ref[at, :] = out[part]
                dmid_refs[half][...] = d_mid[part]
            else:
                out_ref[at, :DMID] = d_mid[part]
                out_ref[at, DMID:] = out[part]

    if micro:

        @pl.when(step == pl.num_programs(0) - 1)
        def _():
            for copy in old_copies():
                copy.wait()
            for s in range(outer):
                at = plane_back(place_ref, s, outer, up_rows)
                grads[s][:up_rows] = (acc_gu[at] + old_gu[at]).astype(BF)
                at = plane_back(place_ref, s, outer, down_rows)
                grads[s][up_rows:] = (acc_dn[at] + old_dn[at]).astype(BF)


def join_pair(a0, b0, a1, b1, low):
    return jnp.where(low, a0, b1) + swap(jnp.where(low, a1, b0))


def attention_backward_kernel(last, *refs):
    refs = list(refs)
    take = lambda k: [refs.pop(0) for _ in range(k)]
    (tok_ref, cot_ref, nm_ref, q_ref, kv_ref, mixed_ref, resid_ref, weight_ref, dmid_ref, w_ref, cos_ref, sin_ref) = take(12)
    old = take(8) if last else []
    rows_ref = take(1)[0]
    kept = refs

    gain_in, gain_mid = gain_rows(w_ref)
    lane = lane_of(MB)
    cot = cot_ref[:, :D].astype(F32)
    resid = resid_ref[...]
    nm = nm_ref[:, -D:]
    w_small = w_ref[:, 3 * D :]
    gates = masked_gates(dot(nm, w_small), cot_ref[:, D:].astype(F32) > 0.5)
    pieces = dmid_ref[:, D:].astype(F32)
    d_gates = pieces + pltpu.roll(pieces, LANES - E, 1)
    d_logits = gates * (d_gates - jnp.sum(gates * d_gates, axis=1, keepdims=True))
    d_logits = jnp.where(lane < E, d_logits, 0.0).astype(BF)
    d_mid = dmid_ref[:, :D].astype(F32) + dot(d_logits, w_small, 1, 1)
    inverse = lax.rsqrt(mean_rows(resid * resid) + EPS)
    u = d_mid * gain_mid
    d_resid = cot + inverse * u - resid * (inverse * inverse * inverse) * mean_rows(u * resid)
    gain_mid_grad = jnp.sum(d_mid * resid * inverse, axis=0, keepdims=True)
    d_branch = d_resid.astype(BF)
    d_mixed = dot(d_branch, w_ref[:, 2 * D : 3 * D], 1, 1).astype(BF)

    cosine, sine = cos_ref[...], sin_ref[...]
    low = (lane % HD) < HD // 2
    head_low = lane < HD
    d_q, d_k, d_v = [], [], []
    for pair in range(GROUPS // 2):
        k_pair = kv_ref[:, pair * LANES : (pair + 1) * LANES].astype(F32)
        v_pair = kv_ref[:, D // 2 + pair * LANES : D // 2 + (pair + 1) * LANES].astype(F32)
        keys, values = [], []
        for half in range(2):
            group = 2 * pair + half
            q = q_ref[:, group * LANES : (group + 1) * LANES]
            dm = d_mixed[:, group * LANES : (group + 1) * LANES]
            k_two = split_pair(k_pair, half)
            weight = weight_ref[:, group * 2 * MB : (group + 1) * 2 * MB]
            p = weight.astype(F32)
            d_weight = dot(dm, split_pair(v_pair, half), 1, 1)
            scored = p * d_weight
            d_score = []
            for h in range(2):
                part = slice(h * MB, (h + 1) * MB)
                total = jnp.sum(scored[:, part], axis=1, keepdims=True)
                d_score.append((p[:, part] * (d_weight[:, part] - total)).astype(BF))
            d_score = jnp.concatenate(d_score, axis=1)
            d_query = dot(d_score, k_two) * 0.125
            d_q.append((d_query * cosine - turned(d_query, low) * sine).astype(BF))
            d_key = dot(d_score, q, 0, 0) * 0.125
            d_value = dot(weight, dm, 0, 0)
            keys += [d_key[:MB], d_key[MB:]]
            values += [d_value[:MB], d_value[MB:]]
        d_key = join_pair(*keys, head_low)
        d_k.append((d_key * cosine - turned(d_key, low) * sine).astype(BF))
        d_v.append(join_pair(*values, head_low).astype(BF))
    d_q = jnp.concatenate(d_q, axis=1)
    d_kv = jnp.concatenate(d_k + d_v, axis=1)

    x = tok_ref[...].astype(F32)
    inverse = lax.rsqrt(mean_rows(x * x) + EPS)
    normed = (x * inverse * gain_in).astype(BF)
    d_in = dot(d_q, w_ref[:, :D], 1, 1) + dot(d_kv, w_ref[:, D : 2 * D], 1, 1)
    v = d_in * gain_in
    rows_ref[...] = d_resid + inverse * v - x * (inverse * inverse * inverse) * mean_rows(v * x)
    gain_in_grad = jnp.sum(d_in * x * inverse, axis=0, keepdims=True)
    gains = jnp.concatenate([gain_in_grad, gain_mid_grad, jnp.zeros((6, D), F32)], axis=0)

    if not last:
        for ref, value in zip(kept, (normed, d_q, d_kv, d_branch, d_logits, gains)):
            ref[...] = value
        return
    grad_ref = kept[0]
    both = lambda k, value: jnp.concatenate([old[k][...], value], axis=0)
    normed_two = both(0, normed)
    grad_ref[:, :D] = dot(normed_two, both(1, d_q), 0, 0).astype(BF)
    grad_ref[:, D : 2 * D] = dot(normed_two, both(2, d_kv), 0, 0).astype(BF)
    grad_ref[:, 2 * D : 3 * D] = dot(both(6, mixed_ref[...]), both(3, d_branch), 0, 0).astype(BF)
    gains = jnp.concatenate([jnp.zeros((E, D), F32), gains + old[5][...], jnp.zeros((LANES - E - 8, D), F32)], axis=0)
    grad_ref[:, 3 * D :] = (dot(both(7, nm), both(4, d_logits), 0, 0) + gains.T).astype(BF)


def blk(shape, index, buffers=None):
    if buffers is None:
        return pl.BlockSpec(shape, index)
    return pl.BlockSpec(shape, index, pipeline_mode=pl.Buffered(buffers))


def kernel_params(mib=58):
    return pltpu.CompilerParams(dimension_semantics=("arbitrary",), vmem_limit_bytes=mib << 20)


def takes(us):
    return pl.CostEstimate(flops=int(us * 1.15e9), bytes_accessed=1 << 20, transcendentals=0)


def shaped(rows, width, kind=BF):
    return jax.ShapeDtypeStruct((rows, width), kind)


def own_rows(width, micro=0):
    return blk((MB, width), lambda i, *_: (micro, 0))


def whole(shape):
    return blk(shape, lambda i, *_: (0,) * len(shape), 1)


def attention_forward(micro, outer, place, lengths, tokens, cot, packed, cosine, sine):
    width = DMID + D if micro else D
    any_ref = pl.BlockSpec(memory_space=pl.ANY)
    return pl.pallas_call(
        functools.partial(attention_forward_kernel, micro, outer),
        grid_spec=pltpu.PrefetchScalarGridSpec(
            num_scalar_prefetch=2,
            grid=(1,),
            in_specs=[own_rows(D, micro), own_rows(DMID, micro), whole((D, WIDE)) if micro else any_ref]
            + [own_rows(LANES, micro)] * 2,
            out_specs=[own_rows(width)] + [own_rows(D)] * 4 + [own_rows(D * 4)] + ([] if micro else [any_ref]),
            scratch_shapes=[]
            if micro
            else [pltpu.VMEM((D, WIDE), BF), pltpu.SemaphoreType.DMA((PLANE * outer,)), pltpu.SemaphoreType.DMA],
        ),
        out_shape=[shaped(MB, width)]
        + [shaped(MB, D)] * 3
        + [shaped(MB, D, F32), shaped(MB, D * 4)]
        + ([] if micro else [shaped(D, WIDE)]),
        compiler_params=kernel_params(),
        cost_estimate=takes(12),
        name=f"attention_forward_{micro}",
    )(place, lengths, tokens, cot, packed, cosine, sine)


def experts(micro, e, place, rows, packed, homes, carried=(), partial=()):
    outer = len(homes)
    wide = DMID + D
    any_ref = pl.BlockSpec(memory_space=pl.ANY)
    shape = jax.ShapeDtypeStruct

    def peer(k, width):
        return blk((MB, width), lambda i, place, *_: (lax.bitwise_xor(place[0], 2 * i + k), 0))

    near = blk((MB, DMID), lambda i, *_: (i, 0))
    pair = blk((2 * MB, wide), lambda i, *_: (i, 0))
    home = shape(homes[0].shape, BF)
    acc = [shape((D, 2 * FF), F32), shape((FF, D), F32)]
    in_specs = [peer(0, wide), peer(1, wide)] if micro else [near, near, peer(0, D), peer(1, D)]
    in_specs += [blk((D, LANES), lambda i, *_: (0, 3 * D // LANES), 1)]
    in_specs += [any_ref] * outer + [pair] * len(partial) + [any_ref] * len(carried)
    scratch = [
        pltpu.VMEM((D, 2 * FF), BF),
        pltpu.VMEM((FF, D), BF),
        pltpu.SemaphoreType.DMA((outer + 1, 2)),
    ]
    if not e:
        out_specs, out_shape = [pair], [shaped(PLANE * MB, wide)]
    else:
        width = D if micro else wide
        out_specs = [blk((2 * MB, width), lambda i, place, *_: (lax.bitwise_xor(place[0] // 2, i), 0))]
        out_shape = [shaped(PLANE * MB, width)]
        if micro:
            out_specs += [near, near]
            out_shape += [shaped(PLANE // 2 * MB, DMID)] * 2
    if micro:
        out_specs += [whole(home.shape)] * outer
        out_shape += [home] * outer
        scratch = [pltpu.VMEM(a.shape, F32) for a in acc] + scratch + [pltpu.VMEM(a.shape, F32) for a in acc]
    else:
        out_specs += [whole(a.shape) for a in acc]
        out_shape += acc
    return pl.pallas_call(
        functools.partial(expert_kernel, outer, micro, e),
        grid_spec=pltpu.PrefetchScalarGridSpec(
            num_scalar_prefetch=1,
            grid=(PLANE // 2,),
            in_specs=in_specs,
            out_specs=out_specs,
            scratch_shapes=scratch,
        ),
        out_shape=out_shape,
        compiler_params=kernel_params(),
        cost_estimate=takes(28),
        name=f"experts_{micro}_{e}",
    )(place, *rows, packed, *homes, *partial, *carried)


def attention_backward(micro, tokens, cot, saved, d_mid, packed, cosine, sine, old):
    last = old is not None
    in_specs = [own_rows(D, micro), own_rows(DMID, micro)] + [own_rows(v.shape[1]) for v in saved]
    in_specs += [own_rows(DMID), whole((D, WIDE)), own_rows(LANES, micro), own_rows(LANES, micro)]
    args = [tokens, cot, *saved, d_mid, packed, cosine, sine]
    kept = [shaped(MB, D)] * 4 + [shaped(MB, LANES), shaped(8, D, F32)]
    if last:
        args += old
        in_specs += [whole(a.shape) for a in old]
        kept = [shaped(D, WIDE)]
    return pl.pallas_call(
        functools.partial(attention_backward_kernel, last),
        grid=(1,),
        in_specs=in_specs,
        out_specs=[own_rows(D)] + [whole(a.shape) for a in kept],
        out_shape=[shaped(MB, D, F32)] + kept,
        compiler_params=kernel_params(),
        cost_estimate=takes(22 if last else 16),
        name=f"attention_backward_{micro}",
    )(*args)


def rope_tables(lengths):
    ends = jnp.stack([jnp.sum(lengths[:, : s + 1], axis=1) for s in range(lengths.shape[1] - 1)], axis=1)
    index = jnp.arange(MB, dtype=jnp.int32)
    start = jnp.max(jnp.where(ends[:, None, :] <= index[None, :, None], ends[:, None, :], 0), axis=2)
    position = (index[None, :] - start).astype(F32).reshape(-1)
    lane = jnp.arange(LANES, dtype=jnp.int32)
    freq = jnp.exp(-((2 * (lane % (HD // 2))).astype(F32) / HD) * jnp.log(10000.0))
    angle = position[:, None] * freq[None, :]
    sign = jnp.where(lane % HD < HD // 2, -1.0, 1.0)
    return jnp.cos(angle), jnp.sin(angle) * sign[None, :]


def gather(v, axes):
    return lax.all_gather(v, axes, axis=0, tiled=True)


def scatter_sum(v, axes, dim=0):
    return lax.psum_scatter(v, axes, scatter_dimension=dim, tiled=True)


def tie(*values):
    return lax.optimization_barrier(values)


def after(v, *others):
    return tie(v, *others)[0]


def across(v, axis):
    return lax.ppermute(v, axis, [(0, 1), (1, 0)])


def onward(v, steps=1):
    count = lax.axis_size("z")
    return lax.ppermute(v, "z", [(i, (i + steps) % count) for i in range(count)])


def plus(a, b):
    return (a.astype(F32) + b.astype(F32)).astype(BF)


def pick(v, index, axis):
    return lax.dynamic_index_in_dim(v, index, axis, keepdims=False)


def sum_weights(g, beside):
    outer = g.shape[0]
    z, y, x, c = (lax.axis_index(axis) for axis in ALL)
    cut = g.shape[-1] // 2 // LANES * LANES
    got, _ = tie(across(pick(g, 1 - c, 3), "c"), beside[0]())
    total = plus(pick(g, c, 3), got)
    first, second = total[..., :cut], total[..., cut:]
    got_x, got_y, _ = tie(across(pick(first, 1 - x, 2), "x"), across(pick(second, 1 - y, 1), "y"), beside[1]())
    first, second = plus(pick(first, x, 2), got_x), plus(pick(second, y, 1), got_y)
    got_y, got_x, _ = tie(across(pick(first, 1 - y, 1), "y"), across(pick(second, 1 - x, 1), "x"), beside[2]())
    total = jnp.concatenate([plus(pick(first, y, 1), got_y), plus(pick(second, x, 1), got_x)], axis=-1)
    terms = [pick(total, z, 0)] + [onward(pick(total, (z + s) % outer, 0), s) for s in range(1, outer)]
    return sum(term.astype(F32) for term in terms)


def sum_to_owners(same, other, hold):
    total = plus(same, across(other, "c"))
    total = total.reshape(4, 2, MB // 2, -1)
    first = [total[i, 0] for i in range(4)]
    second = [total[i, 1] for i in range(4)]
    got_x = across(jnp.stack([first[1], first[3]]), "x")
    got_y = across(jnp.stack([second[2], second[3]]), "y")
    got_x, got_y, hold = tie(got_x, got_y, hold)
    last_x, last_y = across(plus(second[1], got_y[1]), "x"), across(plus(first[2], got_x[1]), "y")
    return jnp.concatenate(
        [
            (first[0].astype(F32) + got_x[0].astype(F32) + last_y.astype(F32)).astype(BF),
            (second[0].astype(F32) + got_y[0].astype(F32) + last_x.astype(F32)).astype(BF),
        ],
        axis=0,
    ), hold


def shards(tokens, cotangent, lengths, routes, attn_gain, w_query, w_keyval, w_out, moe_gain, w_router, w_gateup, w_down):
    share = w_query.shape[0]
    outer = lax.axis_size("z")
    place = jnp.stack([lax.axis_index(PLANE_AXES), lax.axis_index("z")]).astype(jnp.int32)

    small = jnp.concatenate(
        [w_router, attn_gain[:, None], moe_gain[:, None], jnp.zeros((share, LANES - E - 2), BF)], axis=1
    )
    own = jnp.concatenate([w_query, w_keyval, w_out, small], axis=1)
    pieces = [own] + [onward(own, s) for s in range(1, outer)]
    sent = jnp.concatenate([w_gateup, w_down], axis=1)
    sent = sent.reshape(PLANE, OWN, *sent.shape[1:])

    def bring(part):
        got = lax.all_to_all(part, PLANE_AXES, split_axis=0, concat_axis=0, tiled=True)
        return jnp.concatenate(
            [got[:, :share].reshape(PLANE * share, D), got[:, share:].reshape(PLANE * share // 2, D)], axis=0
        )

    def ring(e, count=1):
        for _ in range(count):
            homes[e].append(onward(homes[e][-1]))
        return homes[e][-1]

    homes = [[bring(sent[:, 0])], []]
    *pieces, homes[0][0] = tie(*pieces, homes[0][0])
    packed = gather(jnp.concatenate(pieces, axis=0), PLANE_AXES)
    part, homes[0][-1] = tie(sent[:, 1], ring(0))
    homes[1].append(bring(part))
    hot = jnp.sum((routes[:, :, None] == jnp.arange(LANES, dtype=jnp.int32)[None, None, :]).astype(F32), axis=1)
    cot = jnp.concatenate([cotangent, hot.astype(BF)], axis=1)
    cot_0, homes[1][0] = tie(cot[:MB], homes[1][0])
    cosine, sine = rope_tables(lengths)

    from_x, from_y = across(cot_0, "x"), across(cot_0, "y")
    packed, from_x, from_y, homes[0][-1] = tie(packed, from_x, from_y, ring(0, outer - 2))
    *saved_0, packed = attention_forward(0, outer, place, lengths, tokens, cot, packed, cosine, sine)
    nm_0 = gather(saved_0[0], PLANE_AXES)
    corner_a, corner_b = across(from_x[: MB // 2], "y"), across(from_y[MB // 2 :], "x")
    packed, corner_a, corner_b, homes[1][-1] = tie(packed, corner_a, corner_b, ring(1, max(outer - 3, 0)))
    cot_same = jnp.concatenate([cot_0, from_x, from_y, corner_a, corner_b], axis=0)
    saved_1 = attention_forward(1, outer, place, lengths, tokens, cot, packed, cosine, sine)
    nm_1, homes[1][-1] = tie(saved_1[0], ring(1))
    nm_1 = gather(nm_1, PLANE_AXES)
    cot_other = across(cot_same, "c")
    ring(1, outer - len(homes[1]))

    rows = [cot_same, cot_other, nm_0, nm_0]
    partial, *carried_a = experts(0, 0, place, rows, packed, homes[0])
    both_0, *carried_b = experts(0, 1, place, rows, packed, homes[1], partial=[partial])
    rows = [nm_1, nm_1]
    partial, *turns_a = experts(1, 0, place, rows, packed, homes[0], carried_a)
    out_1, same_1, other_1, *turns_b = experts(1, 1, place, rows, packed, homes[1], carried_b, [partial])

    turns = [turns_a, turns_b]
    moved = [turns_a[1], turns_b[1]]

    def pass_on(e, first, last):
        for s in range(first, last):
            moved[e] = onward(moved[e] if s == 1 else plus(turns[e][s], moved[e]))
        return moved[e]

    other_1, moved[0] = tie(other_1, pass_on(0, 1, 2))
    both_0 = scatter_sum(both_0, PLANE_AXES)
    rows_0, *old = attention_backward(0, tokens, cot, saved_0, both_0, packed, cosine, sine, None)
    old = old + [saved_0[3], saved_0[0]]
    d_mid_1, rows_0 = sum_to_owners(same_1, other_1, rows_0)
    d_mid_1, *moved = tie(d_mid_1, pass_on(0, 2, outer - 1), pass_on(1, 1, outer - 2))
    rows_1, grads = attention_backward(1, tokens, cot, saved_1, d_mid_1, packed, cosine, sine, old)
    out_sums = both_0[:, DMID:], scatter_sum(out_1, PLANE_AXES)
    output = [(saved[4] + part.astype(F32)).astype(BF) for saved, part in zip((saved_0, saved_1), out_sums)]
    grads, moved[0] = tie(grads, pass_on(0, outer - 1, outer))

    def send_home(e):
        m = plus(turns[e][0], moved[e])
        m = jnp.concatenate(
            [m[: PLANE * share].reshape(PLANE, share, D), m[PLANE * share :].reshape(PLANE, share // 2, D)], axis=1
        )
        got = lax.all_to_all(m, PLANE_AXES, split_axis=0, concat_axis=0, tiled=True)
        kept.append(got)
        return got

    kept = []
    beside = (
        lambda: send_home(0),
        lambda: pass_on(1, outer - 2, outer - 1),
        lambda: pass_on(1, outer - 1, outer),
    )
    grads = sum_weights(grads.reshape(outer, 2, 2, 2, share, WIDE), beside)
    send_home(1)
    home = jnp.stack(kept, axis=1).reshape(E, -1, D).astype(F32)
    return (
        jnp.concatenate(output, axis=0),
        jnp.concatenate([rows_0, rows_1], axis=0),
        grads[:, 3 * D + E],
        grads[:, :D],
        grads[:, D : 2 * D],
        grads[:, 2 * D : 3 * D],
        grads[:, 3 * D + E + 1],
        grads[:, 3 * D : 3 * D + E],
        home[:, :share],
        home[:, share:],
    )


def solution(mesh):
    count = mesh.shape["fsdp"]
    inner = Mesh(mesh.devices.reshape(count // PLANE, 2, 2, 2), ALL)
    row, vec, mid = P(ALL, None), P(ALL), P(None, ALL, None)
    return jax.shard_map(
        shards,
        mesh=inner,
        in_specs=(row, row, row, row, vec, row, row, row, vec, row, mid, mid),
        out_specs=(row, row, vec, row, row, row, vec, row, mid, mid),
        check_vma=False,
    )
```

time: 809 us -> 496 us (0.61)
  waiting for transfers between devices: 582 us -> 175 us
  starting transfers between devices: 4.28 us -> 50.2 us
  Pallas kernels: 148 us -> 184 us
  other arithmetic: 15 us -> 44.5 us
  blocking collectives: 27.4 us -> 0 us
    reduce_scatter x6 -> x2, waiting for transfers between devices: 315 us -> 0.02 us  [scatter_sum(): return lax.psum_scatter(v, axes, scatter_dimension=dim, tiled=True)]
    all_gather x5 -> x3, waiting for transfers between devices: 265 us -> 0.03 us  [gather(): return lax.all_gather(v, axes, axis=0, tiled=True)]
    ppermute x0 -> x33, waiting for transfers between devices: none -> 160 us  [the longest x18 109 us: onward(): lax.ppermute(v, 'z', [(i, (i + steps) % count) for i in range(count)])]
    pallas_call x3 -> x8, Pallas kernels: 148 us -> 184 us  [the longest x4 123 us: experts(): pl.pallas_call(functools.partial(expert_kernel, outer, micro, e), grid_sp...]
    ppermute x0 -> x33, starting transfers between devices: none -> 32.8 us  [the longest x18 19.9 us: onward(): lax.ppermute(v, 'z', [(i, (i + steps) % count) for i in range(count)])]
    all_to_all x1 -> x0, blocking collectives: 27.4 us -> none  [shards(): lax.all_to_all(sent.reshape(PLANE, OWN, *sent.shape[1:]), PLANE_AXES, spl...]
    convert_element_type x3 -> x18, other arithmetic: 4.01 us -> 27 us  [the longest x13 18.7 us: plus(): return (a.astype(F32) + b.astype(F32)).astype(BF)]
    all_to_all x1 -> x4, waiting for transfers between devices: 0.01 us -> 15 us  [the longest x2 15 us: bring(): lax.all_to_all(part, PLANE_AXES, split_axis=0, concat_axis=0, tiled=True)]
  transfers between devices with their start and end apart: 12 -> 42, of which waited for: 11 -> 21; matrix products, arithmetic and copies ran while one was open for 3% -> 10% of each run, Pallas kernels for 6% -> 35%
where the time goes in v2:
time: 496 us; the launch traced here: 488 us
  Pallas kernels  184 us (37%)
  waiting for transfers between devices  175 us (35%)
  starting transfers between devices  50.2 us (10%)
  other arithmetic  44.5 us (9%)
  local copies, waits for them, and re-layouts  19.6 us (4%)
  between operations  14.7 us (3%)
    pallas_call x4, Pallas kernels, experts(): pl.pallas_call(functools.partial(expert_kernel, outer, micro, e), grid_sp...  123 us
    ppermute x18, waiting for transfers between devices, onward(): lax.ppermute(v, 'z', [(i, (i + steps) % count) for i in range(count)])  109 us
    ppermute x15, waiting for transfers between devices, across(): return lax.ppermute(v, axis, [(0, 1), (1, 0)])  51.3 us
    pallas_call x2, Pallas kernels, attention_backward(): pl.pallas_call(functools.partial(attention_backward_kernel, last), grid=(...  34.1 us
    pallas_call x2, Pallas kernels, attention_forward(): pl.pallas_call(functools.partial(attention_forward_kernel, micro, outer),...  26.9 us
    ppermute x18, starting transfers between devices, onward(): lax.ppermute(v, 'z', [(i, (i + steps) % count) for i in range(count)])  19.9 us
    convert_element_type x13, other arithmetic, plus(): return (a.astype(F32) + b.astype(F32)).astype(BF)  18.7 us
    all_to_all x2, waiting for transfers between devices, bring(): lax.all_to_all(part, PLANE_AXES, split_axis=0, concat_axis=0, tiled=True)  15 us
  transfers between devices with their start and end apart: 42, of which 21 were waited for; matrix products, arithmetic and copies ran while one was open for 10% of the time, Pallas kernels for 35%

profile of v2, /device:TPU:0, one launch (start us, length us, event | category | flops | bytes accessed | tf_op | source)
XLA Modules:
  0.0 488.3 jit_solution(5921658668645183886)
XLA Ops:
  10.0 5.2 %all-to-all-start = ((bf16[8,48,1024]{2,1,0:T(8,128)(2,1)}), bf16[8,48,1024]{2,1,0:T(8,128)(2,1)S(1)}, u32[]{:S(2)}, u32[]{:S(2)}) async-start(bf16[8,48,1024]{2,1,0:T(8,128)(2,1)} %get-tuple-element.207), calls=%async_computation | async-start | bytes 1572864 | tf_op jit(solution)/shard_map/all_to_all | solution.py:560
  21.2 6.6 %all-to-all-done = bf16[8,48,1024]{2,1,0:T(8,128)(2,1)S(1)} async-done(((bf16[8,48,1024]{2,1,0:T(8,128)(2,1)}), bf16[8,48,1024]{2,1,0:T(8,128)(2,1)S(1)}, u32[]{:S(2)}, u32[]{:S(2)}) %all-to-all-start) | async-done | bytes 786464 | tf_op jit(solution)/shard_map/all_to_all | solution.py:560
  28.0 5.9 %collective-permute-done.1 = bf16[32,3200]{1,0:T(8,128)(2,1)S(1)} collective-permute-done((bf16[32,3200]{1,0:T(8,128)(2,1)S(1)}, bf16[32,3200]{1,0:T(8,128)(2,1)S(1)}, u32[]{:S(2)}, u32[]{:S(2)}) %collective-permute-start.1) | collective-permute-done | bytes 204832 | tf_op jit(solution)/shard_map/ppermute | solution.py:502
  40.3 18.0 %collective-permute-done.3.refs_7_.refs_5_ = bf16[384,1024]{1,0:T(8,128)(2,1)} collective-permute-done((bf16[384,1024]{1,0:T(8,128)(2,1)S(1)}, bf16[384,1024]{1,0:T(8,128)(2,1)}, u32[]{:S(2)}, u32[]{:S(2)}) %collective-permute-start.3) | collective-permute-done | bytes 786464 | tf_op jit(solution)/shard_map/ppermute | solution.py:502
  66.4 12.6 %collective-permute-done.6.refs_8_.refs_6_ = bf16[384,1024]{1,0:T(8,128)(2,1)} collective-permute-done((bf16[384,1024]{1,0:T(8,128)(2,1)}, bf16[384,1024]{1,0:T(8,128)(2,1)}, u32[]{:S(2)}, u32[]{:S(2)}) %collective-permute-start.6) | collective-permute-done | bytes 786464 | tf_op jit(solution)/shard_map/ppermute | solution.py:502
  79.0 8.4 %all-to-all-done.1 = bf16[8,48,1024]{2,1,0:T(8,128)(2,1)S(1)} async-done(((bf16[8,48,1024]{2,1,0:T(8,128)(2,1)}), bf16[8,48,1024]{2,1,0:T(8,128)(2,1)S(1)}, u32[]{:S(2)}, u32[]{:S(2)}) %all-to-all-start.1) | async-done | bytes 786464 | tf_op jit(solution)/shard_map/all_to_all | solution.py:560
  93.1 11.4 %collective-permute-done.4 = bf16[256,1152]{1,0:T(8,128)(2,1)S(1)} collective-permute-done((bf16[256,1152]{1,0:T(8,128)(2,1)S(1)}, bf16[256,1152]{1,0:T(8,128)(2,1)S(1)}, u32[]{:S(2)}, u32[]{:S(2)}) %collective-permute-start.4) | collective-permute-done | bytes 589856 | tf_op jit(solution)/shard_map/ppermute | solution.py:497
  104.6 14.3 %attention_forward_0.1 = (bf16[256,1024]{1,0:T(8,128)(2,1)}, bf16[256,1024]{1,0:T(8,128)(2,1)}, bf16[256,1024]{1,0:T(8,128)(2,1)}, bf16[256,1024]{1,0:T(8,128)(2...) custom-call(s32[2]{0:T(128)} %pad_add_fusion.1.place_ref.refs_0_, ...), custom_call_target="tpu_custom_call" | custom-call | flops 13799999488 | bytes 1048576 | tf_op jit(solution)/shard_map/attention_forward_0/pallas_call | solution.py:371
  122.8 16.6 %collective-permute-done.10.refs_7_.refs_5_ = bf16[384,1024]{1,0:T(8,128)(2,1)S(1)} collective-permute-done((bf16[384,1024]{1,0:T(8,128)(2,1)S(1)}, bf16[384,1024]{1,0:T(8,128)(2,1)S(1)}, u32[]{:S(2)}, u32[]{:S(2)}) %collective-permute-start.10) | collective-permute-done | bytes 786464 | tf_op jit(solution)/shard_map/ppermute | solution.py:502
  139.9 12.5 %attention_forward_1.1 = (bf16[256,2176]{1,0:T(8,128)(2,1)}, bf16[256,1024]{1,0:T(8,128)(2,1)}, bf16[256,1024]{1,0:T(8,128)(2,1)}, bf16[256,1024]{1,0:T(8,128)(2...) custom-call(s32[2]{0:T(128)} %pad_add_fusion.1.place_ref.refs_0_, s32[2,4]{1,0:T(2,128)} %lens_ref.3, ...), custom_call_target="tpu_custom_call" | custom-call | flops 13799999488 | bytes 1048576 | tf_op jit(solution)/shard_map/attention_forward_1/pallas_call | solution.py:371
  152.5 7.0 %collective-permute-done.12.refs_8_.refs_6_ = bf16[384,1024]{1,0:T(8,128)(2,1)} collective-permute-done((bf16[384,1024]{1,0:T(8,128)(2,1)S(1)}, bf16[384,1024]{1,0:T(8,128)(2,1)}, u32[]{:S(2)}, u32[]{:S(2)}) %collective-permute-start.12) | collective-permute-done | bytes 786464 | tf_op jit(solution)/shard_map/ppermute | solution.py:502
  168.1 30.3 %experts_0_0.1 = (bf16[2048,2176]{1,0:T(8,128)(2,1)}, f32[1024,1024]{1,0:T(8,128)}, f32[512,1024]{1,0:T(8,128)}) custom-call(s32[2]{0:T(128)} %pad_add_fusion.1.place_ref.refs_0_, bf16[1024,1152]{1,0:T(8,128)(2,1)} %copy-done.17, bf16[1024,1152]{1,0:T(8,128)(2,1)} %copy-done.25, bf16[2048,1024]{1,0:T(8,128)(2,1)} %all-gather.6.cloned.1.call-done.refs_3_.refs_4_, ...), custom_call_target="tpu_custom_call" | custom-call | flops 32199999488 | bytes 1048576 | tf_op jit(solution)/shard_map/experts_0_0/pallas_call | solution.py:430
  199.3 30.2 %experts_0_1.1 = (bf16[2048,2176]{1,0:T(8,128)(2,1)}, f32[1024,1024]{1,0:T(8,128)}, f32[512,1024]{1,0:T(8,128)}) custom-call(s32[2]{0:T(128)} %pad_add_fusion.1.place_ref.refs_0_, bf16[1024,1152]{1,0:T(8,128)(2,1)} %copy-done.17, bf16[1024,1152]{1,0:T(8,128)(2,1)} %copy-done.25, bf16[2048,1024]{1,0:T(8,128)(2,1)} %all-gather.6.cloned.1.call-done.refs_3_.refs_4_, ...), custom_call_target="tpu_custom_call" | custom-call | flops 32199999488 | bytes 1048576 | tf_op jit(solution)/shard_map/experts_0_1/pallas_call | solution.py:430
  229.7 30.6 %experts_1_0.1 = (bf16[2048,2176]{1,0:T(8,128)(2,1)}, bf16[384,1024]{1,0:T(8,128)(2,1)}, bf16[384,1024]{1,0:T(8,128)(2,1)}, bf16[384,1024]{1,0:T(8,128)(2,1)}, bf16[384,1024]{1,0:T(8,128)(2,1)}) custom-call(s32[2]{0:T(128)} %pad_add_fusion.1.place_ref.refs_0_, bf16[2048,2176]{1,0:T(8,128)(2,1)} %all-gather.8.cloned.1.call-done.refs_1_.refs_2_, ...), custom_call_target="tpu_custom_call" | custom-call | flops 32199999488 | bytes 1048576 | tf_op jit(solution)/shard_map/experts_1_0/pallas_call | solution.py:430
  260.4 32.2 %experts_1_1.1 = (bf16[2048,1024]{1,0:T(8,128)(2,1)}, bf16[1024,1152]{1,0:T(8,128)(2,1)}, bf16[1024,1152]{1,0:T(8,128)(2,1)}, bf16[384,1024]{1,0:T(8,128)(2,1)},...) custom-call(s32[2]{0:T(128)} %pad_add_fusion.1.place_ref.refs_0_, ...), custom_call_target="tpu_custom_call" | custom-call | flops 32199999488 | bytes 1048576 | tf_op jit(solution)/shard_map/experts_1_1/pallas_call | solution.py:430
  304.3 13.9 %attention_backward_0.1 = (f32[256,1024]{1,0:T(8,128)}, bf16[256,1024]{1,0:T(8,128)(2,1)}, bf16[256,1024]{1,0:T(8,128)(2,1)}, bf16[256,1024]{1,0:T(8,128)(2,1)},...) custom-call(bf16[512,1024]{1,0:T(8,128)(2,1)} %refs_0_.3, ...), custom_call_target="tpu_custom_call" | custom-call | flops 18400000000 | bytes 1048576 | tf_op jit(solution)/shard_map/attention_backward_0/pallas_call | solution.py:456
  319.4 7.4 %collective-permute-done.18 = bf16[128,1152]{1,0:T(8,128)(2,1)S(1)} collective-permute-done((bf16[128,1152]{1,0:T(8,128)(2,1)S(1)}, bf16[128,1152]{1,0:T(8,128)(2,1)S(1)}, u32[]{:S(2)}, u32[]{:S(2)}) %collective-permute-start.18) | collective-permute-done | bytes 294944 | tf_op jit(solution)/shard_map/ppermute | solution.py:497
  330.8 5.4 %collective-permute-done.19 = bf16[128,1152]{1,0:T(8,128)(2,1)} collective-permute-done((bf16[128,1152]{1,0:T(8,128)(2,1)}, bf16[128,1152]{1,0:T(8,128)(2,1)}, u32[]{:S(2)}, u32[]{:S(2)}) %collective-permute-start.19) | collective-permute-done | bytes 294944 | tf_op jit(solution)/shard_map/ppermute | solution.py:497
  342.0 14.7 %collective-permute-done.20 = bf16[384,1024]{1,0:T(8,128)(2,1)} collective-permute-done((bf16[384,1024]{1,0:T(8,128)(2,1)}, bf16[384,1024]{1,0:T(8,128)(2,1)}, u32[]{:S(2)}, u32[]{:S(2)}) %collective-permute-start.20) | collective-permute-done | bytes 786464 | tf_op jit(solution)/shard_map/ppermute | solution.py:502
  358.6 20.2 %attention_backward_1.1 = (f32[256,1024]{1,0:T(8,128)}, bf16[1024,3200]{1,0:T(8,128)(2,1)}) custom-call(bf16[512,1024]{1,0:T(8,128)(2,1)} %refs_0_.3, bf16[512,1152]{1,0:T(8,128)(2,1)} %pad_maximum_fusion.2.cot_ref.refs_1_, bf16[256,2176]{1,0:T(8,128)(2,1)} %get-tuple-element.109.refs_2_, bf16[256,1024]{1,0:T(8,128)(2,1)} %get-tuple-element.126.refs_3_, ...), custom_call_target="tpu_custom_call" | custom-call | flops 25300000768 | bytes 1048576 | tf_op jit(solution)/shard_map/attention_backward_1/pallas_call | solution.py:456
  391.9 16.2 %collective-permute-done.26 = bf16[384,1024]{1,0:T(8,128)(2,1)} collective-permute-done((bf16[384,1024]{1,0:T(8,128)(2,1)}, bf16[384,1024]{1,0:T(8,128)(2,1)}, u32[]{:S(2)}, u32[]{:S(2)}) %collective-permute-start.26) | collective-permute-done | bytes 786464 | tf_op jit(solution)/shard_map/ppermute | solution.py:502
  422.3 9.8 %collective-permute-done.29 = bf16[384,1024]{1,0:T(8,128)(2,1)} collective-permute-done((bf16[384,1024]{1,0:T(8,128)(2,1)}, bf16[384,1024]{1,0:T(8,128)(2,1)}, u32[]{:S(2)}, u32[]{:S(2)}) %collective-permute-start.29) | collective-permute-done | bytes 786464 | tf_op jit(solution)/shard_map/ppermute | solution.py:502
  433.6 9.0 %collective-permute-done.24 = bf16[4,2,32,1536]{3,2,1,0:T(8,128)(2,1)} collective-permute-done((bf16[4,2,32,1536]{3,2,1,0:T(8,128)(2,1)}, bf16[4,2,32,1536]{3,2,1,0:T(8,128)(2,1)}, u32[]{:S(2)}, u32[]{:S(2)}) %collective-permute-start.24) | collective-permute-done | bytes 786464 | tf_op jit(solution)/shard_map/ppermute | solution.py:497
  456.0 7.4 %collective-permute-done.27 = bf16[4,32,1536]{2,1,0:T(8,128)(2,1)S(1)} collective-permute-done((bf16[4,32,1536]{2,1,0:T(8,128)(2,1)S(1)}, bf16[4,32,1536]{2,1,0:T(8,128)(2,1)S(1)}, u32[]{:S(2)}, u32[]{:S(2)}) %collective-permute-start.27) | collective-permute-done | bytes 393248 | tf_op jit(solution)/shard_map/ppermute | solution.py:497
  (214 shorter events, 127.6 us)
Async XLA Ops:
  15.2 89.4 %all-gather.4.cloned.1.call-start = ((), (), s32[]{:S(2)}) async-start(), calls=%async_computation.6 | async-start | bytes 7372800 | tf_op jit(solution)/shard_map/all_gather | solution.py:481
  34.9 23.4 %collective-permute-start.3 = (bf16[384,1024]{1,0:T(8,128)(2,1)S(1)}, bf16[384,1024]{1,0:T(8,128)(2,1)}, u32[]{:S(2)}, u32[]{:S(2)}) collective-permute-start(bf16[384,1024]{1,0:T(8,128)(2,1)S(1)} %pad_maximum_fusion.5.refs_6_.refs_4_), channel_id=1, source_target_pairs={{0,8},{8,16},{16,24},{24,0},{1,9},{9,17},{17,25},{25,1},{2,10},{10... | collective-permute-start | bytes 2359304 | tf_op jit(solution)/shard_map/ppermute | solution.py:502
  58.3 20.7 %collective-permute-start.6 = (bf16[384,1024]{1,0:T(8,128)(2,1)}, bf16[384,1024]{1,0:T(8,128)(2,1)}, u32[]{:S(2)}, u32[]{:S(2)}) collective-permute-start(bf16[384,1024]{1,0:T(8,128)(2,1)} %collective-permute-done.3.refs_7_.refs_5_), channel_id=1, source_target_pairs={{0,8},{8,16},{16,24},{24,0},{1,9},{9,17},{17,25},{25,1},{2,10},{10... | collective-permute-start | bytes 2359304 | tf_op jit(solution)/shard_map/ppermute | solution.py:502
  62.3 25.1 %all-to-all-start.1 = ((bf16[8,48,1024]{2,1,0:T(8,128)(2,1)}), bf16[8,48,1024]{2,1,0:T(8,128)(2,1)S(1)}, u32[]{:S(2)}, u32[]{:S(2)}) async-start(bf16[8,48,1024]{2,1,0:T(8,128)(2,1)} %get-tuple-element.89), calls=%async_computation.1 | async-start | bytes 1572864 | tf_op jit(solution)/shard_map/all_to_all | solution.py:560
  66.2 100.5 %all-gather.6.cloned.1.call-start = ((), (), s32[]{:S(2)}) async-start(), calls=%async_computation.7 | async-start | bytes 4718592 | tf_op jit(solution)/shard_map/all_gather | solution.py:481
  79.0 25.6 %collective-permute-start.7 = (bf16[384,1024]{1,0:T(8,128)(2,1)}, bf16[384,1024]{1,0:T(8,128)(2,1)}, u32[]{:S(2)}, u32[]{:S(2)}) collective-permute-start(bf16[384,1024]{1,0:T(8,128)(2,1)} %collective-permute-done.6.refs_8_.refs_6_), channel_id=1, source_target_pairs={{0,8},{8,16},{16,24},{24,0},{1,9},{9,17},{17,25},{25,1},{2,10},{10... | collective-permute-start | bytes 2359304 | tf_op jit(solution)/shard_map/ppermute | solution.py:502
  118.9 110.8 %all-gather.8.cloned.1.call-start = ((), (), s32[]{:S(2)}) async-start(), calls=%async_computation.9 | async-start | bytes 10027008 | tf_op jit(solution)/shard_map/all_gather | solution.py:481
  119.0 20.4 %collective-permute-start.10 = (bf16[384,1024]{1,0:T(8,128)(2,1)S(1)}, bf16[384,1024]{1,0:T(8,128)(2,1)S(1)}, u32[]{:S(2)}, u32[]{:S(2)}) collective-permute-start(bf16[384,1024]{1,0:T(8,128)(2,1)S(1)} %copy-done.8), channel_id=1, source_target_pairs={{0,8},{8,16},{16,24},{24,0},{1,9},{9,17},{17,25},{25,1},{2,10},{10... | collective-permute-start | bytes 2359304 | tf_op jit(solution)/shard_map/ppermute | solution.py:502
  120.6 18.8 %collective-permute-start.8 = (bf16[128,1152]{1,0:T(8,128)(2,1)S(1)}, bf16[128,1152]{1,0:T(8,128)(2,1)S(1)}, u32[]{:S(2)}, u32[]{:S(2)}) collective-permute-start(bf16[128,1152]{1,0:T(8,128)(2,1)S(1)} %slice.127), channel_id=1, source_target_pairs={{0,4},{4,0},{1,5},{5,1},{2,6},{6,2},{3,7},{7,3},{8,12},{12,8},{9,1... | collective-permute-start | bytes 884744 | tf_op jit(solution)/shard_map/ppermute | solution.py:497
  139.4 20.0 %collective-permute-start.12 = (bf16[384,1024]{1,0:T(8,128)(2,1)S(1)}, bf16[384,1024]{1,0:T(8,128)(2,1)}, u32[]{:S(2)}, u32[]{:S(2)}) collective-permute-start(bf16[384,1024]{1,0:T(8,128)(2,1)S(1)} %collective-permute-done.10.refs_7_.refs_5_), channel_id=1, source_target_pairs={{0,8},{8,16},{16,24},{24,0},{1,9},{9,17},{17,25},{25,1},{2,10},{10... | collective-permute-start | bytes 2359304 | tf_op jit(solution)/shard_map/ppermute | solution.py:502
  159.5 144.8 %reduce-scatter.3.cloned.1.call-start = ((), (), s32[]{:S(2)}) async-start(), calls=%async_computation.8 | async-start | bytes 10027008 | tf_op jit(solution)/shard_map/reduce_scatter | solution.py:485
  162.1 36.2 %collective-permute-start.13 = (bf16[384,1024]{1,0:T(8,128)(2,1)}, bf16[384,1024]{1,0:T(8,128)(2,1)S(1)}, u32[]{:S(2)}, u32[]{:S(2)}) collective-permute-start(bf16[384,1024]{1,0:T(8,128)(2,1)} %collective-permute-done.12.refs_8_.refs_6_), channel_id=1, source_target_pairs={{0,8},{8,16},{16,24},{24,0},{1,9},{9,17},{17,25},{25,1},{2,10},{10... | collective-permute-start | bytes 2359304 | tf_op jit(solution)/shard_map/ppermute | solution.py:502
  229.5 225.0 %reduce-scatter.5.cloned.1.call-start = ((), (), s32[]{:S(2)}) async-start(), calls=%async_computation.10 | async-start | bytes 4718592 | tf_op jit(solution)/shard_map/reduce_scatter | solution.py:485
  260.3 32.3 %collective-permute-start.14 = (bf16[384,1024]{1,0:T(8,128)(2,1)}, bf16[384,1024]{1,0:T(8,128)(2,1)S(1)}, u32[]{:S(2)}, u32[]{:S(2)}) collective-permute-start(bf16[384,1024]{1,0:T(8,128)(2,1)} %get-tuple-element.118), channel_id=1, source_target_pairs={{0,8},{8,16},{16,24},{24,0},{1,9},{9,17},{17,25},{25,1},{2,10},{10... | collective-permute-start | bytes 2359304 | tf_op jit(solution)/shard_map/ppermute | solution.py:502
  319.4 22.6 %collective-permute-start.21 = (bf16[384,1024]{1,0:T(8,128)(2,1)}, bf16[384,1024]{1,0:T(8,128)(2,1)}, u32[]{:S(2)}, u32[]{:S(2)}) collective-permute-start(bf16[384,1024]{1,0:T(8,128)(2,1)} %get-tuple-element.134), channel_id=1, source_target_pairs={{0,8},{8,16},{16,24},{24,0},{1,9},{9,17},{17,25},{25,1},{2,10},{10... | collective-permute-start | bytes 2359304 | tf_op jit(solution)/shard_map/ppermute | solution.py:502
  330.8 25.9 %collective-permute-start.20 = (bf16[384,1024]{1,0:T(8,128)(2,1)}, bf16[384,1024]{1,0:T(8,128)(2,1)}, u32[]{:S(2)}, u32[]{:S(2)}) collective-permute-start(bf16[384,1024]{1,0:T(8,128)(2,1)} %add_convert_fusion.6), channel_id=1, source_target_pairs={{0,8},{8,16},{16,24},{24,0},{1,9},{9,17},{17,25},{25,1},{2,10},{10... | collective-permute-start | bytes 2359304 | tf_op jit(solution)/shard_map/ppermute | solution.py:502
  358.1 20.7 %collective-permute-start.22 = (bf16[384,1024]{1,0:T(8,128)(2,1)S(1)}, bf16[384,1024]{1,0:T(8,128)(2,1)S(1)}, u32[]{:S(2)}, u32[]{:S(2)}) collective-permute-start(bf16[384,1024]{1,0:T(8,128)(2,1)S(1)} %add_convert_fusion.5), channel_id=1, source_target_pairs={{0,8},{8,16},{16,24},{24,0},{1,9},{9,17},{17,25},{25,1},{2,10},{10... | collective-permute-start | bytes 2359304 | tf_op jit(solution)/shard_map/ppermute | solution.py:502
  383.1 27.6 %collective-permute-start.23 = (bf16[4,2,2,32,3200]{4,3,2,1,0:T(8,128)(2,1)}, bf16[4,2,2,32,3200]{4,3,2,1,0:T(8,128)(2,1)S(1)}, u32[]{:S(2)}, u32[]{:S(2)}) collective-permute-start(bf16[4,2,2,32,3200]{4,3,2,1,0:T(8,128)(2,1)} %dynamic-slice_bitcast_fusion), channel_id=1, source_target_pairs={{0,1},{1,0},{2,3},{3,2},{4,5},{5,4},{6,7},{7,6},{8,9},{9,8},{10,11... | collective-permute-start | bytes 9830408 | tf_op jit(solution)/shard_map/ppermute | solution.py:497
  385.8 22.3 %collective-permute-start.26 = (bf16[384,1024]{1,0:T(8,128)(2,1)}, bf16[384,1024]{1,0:T(8,128)(2,1)}, u32[]{:S(2)}, u32[]{:S(2)}) collective-permute-start(bf16[384,1024]{1,0:T(8,128)(2,1)} %add_convert_fusion.3), channel_id=1, source_target_pairs={{0,8},{8,16},{16,24},{24,0},{1,9},{9,17},{17,25},{25,1},{2,10},{10... | collective-permute-start | bytes 2359304 | tf_op jit(solution)/shard_map/ppermute | solution.py:502
  387.5 23.2 %all-to-all-start.2 = ((bf16[8,48,1024]{2,1,0:T(8,128)(2,1)}), bf16[8,48,1024]{2,1,0:T(8,128)(2,1)}, u32[]{:S(2)}, u32[]{:S(2)}) async-start(bf16[8,48,1024]{2,1,0:T(8,128)(2,1)} %pad_maximum_fusion.7), calls=%async_computation.4 | async-start | bytes 1572864 | tf_op jit(solution)/shard_map/all_to_all | solution.py:624
  410.7 21.5 %collective-permute-start.29 = (bf16[384,1024]{1,0:T(8,128)(2,1)}, bf16[384,1024]{1,0:T(8,128)(2,1)}, u32[]{:S(2)}, u32[]{:S(2)}) collective-permute-start(bf16[384,1024]{1,0:T(8,128)(2,1)} %add_convert_fusion.2), channel_id=1, source_target_pairs={{0,8},{8,16},{16,24},{24,0},{1,9},{9,17},{17,25},{25,1},{2,10},{10... | collective-permute-start | bytes 2359304 | tf_op jit(solution)/shard_map/ppermute | solution.py:502
  414.7 29.3 %collective-permute-start.25 = (bf16[4,2,32,1664]{3,2,1,0:T(8,128)(2,1)}, bf16[4,2,32,1664]{3,2,1,0:T(8,128)(2,1)}, u32[]{:S(2)}, u32[]{:S(2)}) collective-permute-start(bf16[4,2,32,1664]{3,2,1,0:T(8,128)(2,1)} %dynamic-slice_bitcast_fusion.1), channel_id=1, source_target_pairs={{0,4},{4,0},{1,5},{5,1},{2,6},{6,2},{3,7},{7,3},{8,12},{12,8},{9,1... | collective-permute-start | bytes 2555912 | tf_op jit(solution)/shard_map/ppermute | solution.py:497
  417.2 25.4 %collective-permute-start.24 = (bf16[4,2,32,1536]{3,2,1,0:T(8,128)(2,1)}, bf16[4,2,32,1536]{3,2,1,0:T(8,128)(2,1)}, u32[]{:S(2)}, u32[]{:S(2)}) collective-permute-start(bf16[4,2,32,1536]{3,2,1,0:T(8,128)(2,1)} %dynamic-slice_bitcast_fusion.2), channel_id=1, source_target_pairs={{0,2},{2,0},{1,3},{3,1},{4,6},{6,4},{5,7},{7,5},{8,10},{10,8},{9,1... | collective-permute-start | bytes 2359304 | tf_op jit(solution)/shard_map/ppermute | solution.py:497
  450.8 20.4 %all-to-all-start.3 = ((bf16[8,48,1024]{2,1,0:T(8,128)(2,1)}), bf16[8,48,1024]{2,1,0:T(8,128)(2,1)S(1)}, u32[]{:S(2)}, u32[]{:S(2)}) async-start(bf16[8,48,1024]{2,1,0:T(8,128)(2,1)} %pad_maximum_fusion.8), calls=%async_computation.5 | async-start | bytes 1572864 | tf_op jit(solution)/shard_map/all_to_all | solution.py:624
  (49 other events, 533.3 us)
Sparse Core Ops, SparseCore 0:
  35.0 61.3 all-gather.3
  119.1 36.7 all-gather.5
  159.6 54.7 all-gather.7
  229.6 71.6 reduce-scatter.2
  383.2 60.5 reduce-scatter.4

commit v3 on v2

--- a/solution.py
+++ b/solution.py
@@ -254,14 +254,14 @@
     return jnp.where(low, a0, b1) + swap(jnp.where(low, a1, b0))
 
 
-def attention_backward_kernel(last, *refs):
+def attention_backward_kernel(outer, last, *refs):
     refs = list(refs)
     take = lambda k: [refs.pop(0) for _ in range(k)]
+    place_ref = take(1)[0]
     (tok_ref, cot_ref, nm_ref, q_ref, kv_ref, mixed_ref, resid_ref, weight_ref, dmid_ref, w_ref, cos_ref, sin_ref) = take(12)
     old = take(8) if last else []
     rows_ref = take(1)[0]
-    kept = refs
-
+    kept = take(2 if last else 6)
     gain_in, gain_mid = gain_rows(w_ref)
     lane = lane_of(MB)
     cot = cot_ref[:, :D].astype(F32)
@@ -324,19 +324,32 @@
     rows_ref[...] = d_resid + inverse * v - x * (inverse * inverse * inverse) * mean_rows(v * x)
     gain_in_grad = jnp.sum(d_in * x * inverse, axis=0, keepdims=True)
     gains = jnp.concatenate([gain_in_grad, gain_mid_grad, jnp.zeros((6, D), F32)], axis=0)
-
     if not last:
         for ref, value in zip(kept, (normed, d_q, d_kv, d_branch, d_logits, gains)):
             ref[...] = value
         return
-    grad_ref = kept[0]
     both = lambda k, value: jnp.concatenate([old[k][...], value], axis=0)
+    grad_ref, sems = refs
     normed_two = both(0, normed)
     grad_ref[:, :D] = dot(normed_two, both(1, d_q), 0, 0).astype(BF)
     grad_ref[:, D : 2 * D] = dot(normed_two, both(2, d_kv), 0, 0).astype(BF)
     grad_ref[:, 2 * D : 3 * D] = dot(both(6, mixed_ref[...]), both(3, d_branch), 0, 0).astype(BF)
     gains = jnp.concatenate([jnp.zeros((E, D), F32), gains + old[5][...], jnp.zeros((LANES - E - 8, D), F32)], axis=0)
     grad_ref[:, 3 * D :] = (dot(both(7, nm), both(4, d_logits), 0, 0) + gains.T).astype(BF)
+    share = D // outer // PLANE
+    copies = []
+    for s in range(outer):
+        z = lax.rem(place_ref[1] + s, outer)
+        for q in range(PLANE // 2):
+            for other in range(2):
+                device = lax.bitwise_xor(place_ref[0], 2 * q + other)
+                at = pl.ds(pl.multiple_of((z * PLANE + device) * share, share), share)
+                sem = sems.at[s * PLANE + 2 * q + other]
+                copies.append(pltpu.make_async_copy(grad_ref.at[at], kept[other].at[s, q], sem))
+    for copy in copies:
+        copy.start()
+    for copy in copies:
+        copy.wait()
 
 
 def blk(shape, index, buffers=None):
@@ -443,26 +456,36 @@
     )(place, *rows, packed, *homes, *partial, *carried)
 
 
-def attention_backward(micro, tokens, cot, saved, d_mid, packed, cosine, sine, old):
+def attention_backward(micro, outer, place, tokens, cot, saved, d_mid, packed, cosine, sine, old):
     last = old is not None
+    any_ref = pl.BlockSpec(memory_space=pl.ANY)
     in_specs = [own_rows(D, micro), own_rows(DMID, micro)] + [own_rows(v.shape[1]) for v in saved]
     in_specs += [own_rows(DMID), whole((D, WIDE)), own_rows(LANES, micro), own_rows(LANES, micro)]
     args = [tokens, cot, *saved, d_mid, packed, cosine, sine]
     kept = [shaped(MB, D)] * 4 + [shaped(MB, LANES), shaped(8, D, F32)]
+    kept_specs = [whole(a.shape) for a in kept]
+    scratch = []
     if last:
         args += old
         in_specs += [whole(a.shape) for a in old]
-        kept = [shaped(D, WIDE)]
+        share = D // outer // PLANE
+        kept = [jax.ShapeDtypeStruct((outer, PLANE // 2, share, WIDE), BF)] * 2
+        kept_specs = [any_ref] * 2
+        scratch = [pltpu.VMEM((D, WIDE), BF), pltpu.SemaphoreType.DMA((outer * PLANE,))]
     return pl.pallas_call(
-        functools.partial(attention_backward_kernel, last),
-        grid=(1,),
-        in_specs=in_specs,
-        out_specs=[own_rows(D)] + [whole(a.shape) for a in kept],
+        functools.partial(attention_backward_kernel, outer, last),
+        grid_spec=pltpu.PrefetchScalarGridSpec(
+            num_scalar_prefetch=1,
+            grid=(1,),
+            in_specs=in_specs,
+            out_specs=[own_rows(D)] + kept_specs,
+            scratch_shapes=scratch,
+        ),
         out_shape=[shaped(MB, D, F32)] + kept,
         compiler_params=kernel_params(),
-        cost_estimate=takes(22 if last else 16),
+        cost_estimate=takes(18 if last else 13),
         name=f"attention_backward_{micro}",
-    )(*args)
+    )(place, *args)
 
 
 def rope_tables(lengths):
@@ -506,41 +529,43 @@
     return (a.astype(F32) + b.astype(F32)).astype(BF)
 
 
-def pick(v, index, axis):
-    return lax.dynamic_index_in_dim(v, index, axis, keepdims=False)
-
-
-def sum_weights(g, beside):
-    outer = g.shape[0]
-    z, y, x, c = (lax.axis_index(axis) for axis in ALL)
-    cut = g.shape[-1] // 2 // LANES * LANES
-    got, _ = tie(across(pick(g, 1 - c, 3), "c"), beside[0]())
-    total = plus(pick(g, c, 3), got)
+def sum_weights(same, other, beside):
+    outer = same.shape[0]
+    cut = same.shape[-1] // 2 // LANES * LANES
+
+    def both(stage, *values):
+        start, took = beside[stage]
+        *values, extra = tie(*values, start())
+        took(extra)
+        return values
+
+    total = plus(same, across(other, "c"))
     first, second = total[..., :cut], total[..., cut:]
-    got_x, got_y, _ = tie(across(pick(first, 1 - x, 2), "x"), across(pick(second, 1 - y, 1), "y"), beside[1]())
-    first, second = plus(pick(first, x, 2), got_x), plus(pick(second, y, 1), got_y)
-    got_y, got_x, _ = tie(across(pick(first, 1 - y, 1), "y"), across(pick(second, 1 - x, 1), "x"), beside[2]())
-    total = jnp.concatenate([plus(pick(first, y, 1), got_y), plus(pick(second, x, 1), got_x)], axis=-1)
-    terms = [pick(total, z, 0)] + [onward(pick(total, (z + s) % outer, 0), s) for s in range(1, outer)]
+    got_x, got_y = both(0, across(first[:, 1::2], "x"), across(second[:, 2:], "y"))
+    first, second = plus(first[:, ::2], got_x), plus(second[:, :2], got_y)
+    got_y, got_x = both(1, across(first[:, 1], "y"), across(second[:, 1], "x"))
+    total = jnp.concatenate([plus(first[:, 0], got_y), plus(second[:, 0], got_x)], axis=-1)
+    terms = [total[0]] + [onward(total[s], s) for s in range(1, outer)]
     return sum(term.astype(F32) for term in terms)
 
 
-def sum_to_owners(same, other, hold):
+def sum_to_owners(same, other, early, late):
     total = plus(same, across(other, "c"))
     total = total.reshape(4, 2, MB // 2, -1)
     first = [total[i, 0] for i in range(4)]
     second = [total[i, 1] for i in range(4)]
     got_x = across(jnp.stack([first[1], first[3]]), "x")
     got_y = across(jnp.stack([second[2], second[3]]), "y")
-    got_x, got_y, hold = tie(got_x, got_y, hold)
+    got_x, got_y, early = tie(got_x, got_y, early)
     last_x, last_y = across(plus(second[1], got_y[1]), "x"), across(plus(first[2], got_x[1]), "y")
+    last_x, last_y, late = tie(last_x, last_y, late)
     return jnp.concatenate(
         [
             (first[0].astype(F32) + got_x[0].astype(F32) + last_y.astype(F32)).astype(BF),
             (second[0].astype(F32) + got_y[0].astype(F32) + last_x.astype(F32)).astype(BF),
         ],
         axis=0,
-    ), hold
+    ), early, late
 
 
 def shards(tokens, cotangent, lengths, routes, attn_gain, w_query, w_keyval, w_out, moe_gain, w_router, w_gateup, w_down):
@@ -554,38 +579,36 @@
     own = jnp.concatenate([w_query, w_keyval, w_out, small], axis=1)
     pieces = [own] + [onward(own, s) for s in range(1, outer)]
     sent = jnp.concatenate([w_gateup, w_down], axis=1)
-    sent = sent.reshape(PLANE, OWN, *sent.shape[1:])
-
-    def bring(part):
-        got = lax.all_to_all(part, PLANE_AXES, split_axis=0, concat_axis=0, tiled=True)
-        return jnp.concatenate(
-            [got[:, :share].reshape(PLANE * share, D), got[:, share:].reshape(PLANE * share // 2, D)], axis=0
-        )
+    got = lax.all_to_all(
+        sent.reshape(PLANE, OWN, *sent.shape[1:]), PLANE_AXES, split_axis=0, concat_axis=0, tiled=True
+    )
+    homes = [
+        [jnp.concatenate([got[:, e, :share].reshape(-1, D), got[:, e, share:].reshape(-1, D)], axis=0)]
+        for e in range(OWN)
+    ]
+    *pieces, homes[0][0], homes[1][0] = tie(*pieces, homes[0][0], homes[1][0])
+    packed = gather(jnp.concatenate(pieces, axis=0), PLANE_AXES)
 
     def ring(e, count=1):
         for _ in range(count):
             homes[e].append(onward(homes[e][-1]))
         return homes[e][-1]
 
-    homes = [[bring(sent[:, 0])], []]
-    *pieces, homes[0][0] = tie(*pieces, homes[0][0])
-    packed = gather(jnp.concatenate(pieces, axis=0), PLANE_AXES)
-    part, homes[0][-1] = tie(sent[:, 1], ring(0))
-    homes[1].append(bring(part))
     hot = jnp.sum((routes[:, :, None] == jnp.arange(LANES, dtype=jnp.int32)[None, None, :]).astype(F32), axis=1)
     cot = jnp.concatenate([cotangent, hot.astype(BF)], axis=1)
-    cot_0, homes[1][0] = tie(cot[:MB], homes[1][0])
     cosine, sine = rope_tables(lengths)
 
+    packed, homes[0][-1] = tie(packed, ring(0, outer - 2))
+    cot_0 = after(cot[:MB], homes[0][-1])
     from_x, from_y = across(cot_0, "x"), across(cot_0, "y")
-    packed, from_x, from_y, homes[0][-1] = tie(packed, from_x, from_y, ring(0, outer - 2))
     *saved_0, packed = attention_forward(0, outer, place, lengths, tokens, cot, packed, cosine, sine)
-    nm_0 = gather(saved_0[0], PLANE_AXES)
+    nm_0, from_x, from_y, homes[0][-1] = tie(saved_0[0], from_x, from_y, ring(0))
+    nm_0 = gather(nm_0, PLANE_AXES)
+    packed, homes[1][-1] = tie(packed, ring(1, max(outer - 3, 0)))
     corner_a, corner_b = across(from_x[: MB // 2], "y"), across(from_y[MB // 2 :], "x")
-    packed, corner_a, corner_b, homes[1][-1] = tie(packed, corner_a, corner_b, ring(1, max(outer - 3, 0)))
+    saved_1 = attention_forward(1, outer, place, lengths, tokens, cot, packed, cosine, sine)
+    nm_1, corner_a, corner_b, homes[1][-1] = tie(saved_1[0], corner_a, corner_b, ring(1))
     cot_same = jnp.concatenate([cot_0, from_x, from_y, corner_a, corner_b], axis=0)
-    saved_1 = attention_forward(1, outer, place, lengths, tokens, cot, packed, cosine, sine)
-    nm_1, homes[1][-1] = tie(saved_1[0], ring(1))
     nm_1 = gather(nm_1, PLANE_AXES)
     cot_other = across(cot_same, "c")
     ring(1, outer - len(homes[1]))
@@ -607,33 +630,28 @@
 
     other_1, moved[0] = tie(other_1, pass_on(0, 1, 2))
     both_0 = scatter_sum(both_0, PLANE_AXES)
-    rows_0, *old = attention_backward(0, tokens, cot, saved_0, both_0, packed, cosine, sine, None)
+    rows_0, *old = attention_backward(0, outer, place, tokens, cot, saved_0, both_0, packed, cosine, sine, None)
     old = old + [saved_0[3], saved_0[0]]
-    d_mid_1, rows_0 = sum_to_owners(same_1, other_1, rows_0)
-    d_mid_1, *moved = tie(d_mid_1, pass_on(0, 2, outer - 1), pass_on(1, 1, outer - 2))
-    rows_1, grads = attention_backward(1, tokens, cot, saved_1, d_mid_1, packed, cosine, sine, old)
+    early = rows_0, pass_on(0, 2, outer - 1)
+    moved[1] = after(moved[1], rows_0)
+    d_mid_1, (rows_0, moved[0]), moved[1] = sum_to_owners(same_1, other_1, early, pass_on(1, 1, outer - 2))
+    rows_1, grads, grads_other = attention_backward(1, outer, place, tokens, cot, saved_1, d_mid_1, packed, cosine, sine, old)
     out_sums = both_0[:, DMID:], scatter_sum(out_1, PLANE_AXES)
     output = [(saved[4] + part.astype(F32)).astype(BF) for saved, part in zip((saved_0, saved_1), out_sums)]
-    grads, moved[0] = tie(grads, pass_on(0, outer - 1, outer))
-
-    def send_home(e):
-        m = plus(turns[e][0], moved[e])
-        m = jnp.concatenate(
-            [m[: PLANE * share].reshape(PLANE, share, D), m[PLANE * share :].reshape(PLANE, share // 2, D)], axis=1
-        )
-        got = lax.all_to_all(m, PLANE_AXES, split_axis=0, concat_axis=0, tiled=True)
-        kept.append(got)
-        return got
-
-    kept = []
+    grads, grads_other, moved[0], output[1] = tie(grads, grads_other, pass_on(0, outer - 1, outer), output[1])
+
     beside = (
-        lambda: send_home(0),
-        lambda: pass_on(1, outer - 2, outer - 1),
-        lambda: pass_on(1, outer - 1, outer),
+        (lambda: pass_on(1, outer - 2, outer - 1), lambda v: moved.__setitem__(1, v)),
+        (lambda: pass_on(1, outer - 1, outer), lambda v: moved.__setitem__(1, v)),
     )
-    grads = sum_weights(grads.reshape(outer, 2, 2, 2, share, WIDE), beside)
-    send_home(1)
-    home = jnp.stack(kept, axis=1).reshape(E, -1, D).astype(F32)
+    grads = sum_weights(grads, grads_other, beside)
+    home = jnp.stack([plus(turns[e][0], moved[e]) for e in range(OWN)])
+    up, down = home[:, : PLANE * share], home[:, PLANE * share :]
+    home = jnp.concatenate(
+        [up.reshape(OWN, PLANE, share, D), down.reshape(OWN, PLANE, share // 2, D)], axis=2
+    ).transpose(1, 0, 2, 3)
+    home = lax.all_to_all(home, PLANE_AXES, split_axis=0, concat_axis=0, tiled=True)
+    home = home.reshape(E, -1, D).astype(F32)
     return (
         jnp.concatenate(output, axis=0),
         jnp.concatenate([rows_0, rows_1], axis=0),

time: 496 us -> 457 us (0.921)
  waiting for transfers between devices: 175 us -> 155 us
  starting transfers between devices: 50.2 us -> 41.4 us
  other arithmetic: 44.5 us -> 37.3 us
  local copies, waits for them, and re-layouts: 19.6 us -> 13.3 us
    ppermute x15, waiting for transfers between devices: 51.3 us -> 27.8 us  [across(): return lax.ppermute(v, axis, [(0, 1), (1, 0)])]
    ppermute x18, waiting for transfers between devices: 109 us -> 95.3 us  [onward(): lax.ppermute(v, 'z', [(i, (i + steps) % count) for i in range(count)])]
    all_to_all x4 -> x2, waiting for transfers between devices: 15 us -> 24.9 us  [the longest x1 15 us: shards(): lax.all_to_all(sent.reshape(PLANE, OWN, *sent.shape[1:]), PLANE_AXES, spl...]
    squeeze x6 -> x2, local copies, waits for them, and re-layouts: 8.34 us -> 0.06 us  [sum_weights(): got_y, got_x = both(1, across(first[:, 1], 'y'), across(second[:, 1], 'x'))]
    convert_element_type x13 -> x11, other arithmetic: 18.7 us -> 10.5 us  [plus(): return (a.astype(F32) + b.astype(F32)).astype(BF)]
    all_to_all x4 -> x2, starting transfers between devices: 17.1 us -> 9.03 us  [the longest x1 5.31 us: shards(): lax.all_to_all(sent.reshape(PLANE, OWN, *sent.shape[1:]), PLANE_AXES, spl...]
    all_gather x3, waiting for transfers between devices: 0.03 us -> 6.84 us  [gather(): return lax.all_gather(v, axes, axis=0, tiled=True)]
  transfers between devices with their start and end apart: 42 -> 40, of which waited for: 21 -> 21; matrix products, arithmetic and copies ran while one was open for 10% -> 8% of each run, Pallas kernels for 35% -> 42%
where the time goes in v3:
time: 457 us; the launch traced here: 450 us
  Pallas kernels  188 us (41%)
  waiting for transfers between devices  155 us (34%)
  starting transfers between devices  41.4 us (9%)
  other arithmetic  37.3 us (8%)
  between operations  14.7 us (3%)
  local copies, waits for them, and re-layouts  13.3 us (3%)
    pallas_call x4, Pallas kernels, experts(): pl.pallas_call(functools.partial(expert_kernel, outer, micro, e), grid_sp...  124 us
    ppermute x18, waiting for transfers between devices, onward(): lax.ppermute(v, 'z', [(i, (i + steps) % count) for i in range(count)])  95.3 us
    pallas_call x2, Pallas kernels, attention_backward(): pl.pallas_call(functools.partial(attention_backward_kernel, outer, last),...  37.7 us
    ppermute x15, waiting for transfers between devices, across(): return lax.ppermute(v, axis, [(0, 1), (1, 0)])  27.8 us
    pallas_call x2, Pallas kernels, attention_forward(): pl.pallas_call(functools.partial(attention_forward_kernel, micro, outer),...  26.7 us
    ppermute x18, starting transfers between devices, onward(): lax.ppermute(v, 'z', [(i, (i + steps) % count) for i in range(count)])  20 us
    all_to_all x1, waiting for transfers between devices, shards(): lax.all_to_all(sent.reshape(PLANE, OWN, *sent.shape[1:]), PLANE_AXES, spl...  15 us
    ppermute x15, starting transfers between devices, across(): return lax.ppermute(v, axis, [(0, 1), (1, 0)])  12 us
  transfers between devices with their start and end apart: 40, of which 21 were waited for; matrix products, arithmetic and copies ran while one was open for 8% of the time, Pallas kernels for 42%

profile of v3, /device:TPU:0, one launch (start us, length us, event | category | flops | bytes accessed | tf_op | source)
XLA Modules:
  0.0 449.6 jit_solution(8240414649417919570)
XLA Ops:
  9.9 5.3 %all-to-all-start = ((bf16[8,2,48,1024]{3,2,1,0:T(8,128)(2,1)}), bf16[8,2,48,1024]{3,2,1,0:T(8,128)(2,1)S(1)}, u32[]{:S(2)}, u32[]{:S(2)}) async-start(bf16[8,2,48,1024]{3,2,1,0:T(8,128)(2,1)} %bitcast.4), calls=%async_computation | async-start | bytes 3145728 | tf_op jit(solution)/shard_map/all_to_all | solution.py:582
  21.3 15.0 %all-to-all-done = bf16[8,2,48,1024]{3,2,1,0:T(8,128)(2,1)S(1)} async-done(((bf16[8,2,48,1024]{3,2,1,0:T(8,128)(2,1)}), bf16[8,2,48,1024]{3,2,1,0:T(8,128)(2,1)S(1)}, u32[]{:S(2)}, u32[]{:S(2)}) %all-to-all-start) | async-done | bytes 1572896 | tf_op jit(solution)/shard_map/all_to_all | solution.py:582
  43.4 15.1 %collective-permute-done.3.refs_7_.refs_5_ = bf16[384,1024]{1,0:T(8,128)(2,1)} collective-permute-done((bf16[384,1024]{1,0:T(8,128)(2,1)S(1)}, bf16[384,1024]{1,0:T(8,128)(2,1)}, u32[]{:S(2)}, u32[]{:S(2)}) %collective-permute-start.3) | collective-permute-done | bytes 786464 | tf_op jit(solution)/shard_map/ppermute | solution.py:525
  63.2 15.4 %collective-permute-done.4.refs_8_.refs_6_ = bf16[384,1024]{1,0:T(8,128)(2,1)} collective-permute-done((bf16[384,1024]{1,0:T(8,128)(2,1)}, bf16[384,1024]{1,0:T(8,128)(2,1)}, u32[]{:S(2)}, u32[]{:S(2)}) %collective-permute-start.4) | collective-permute-done | bytes 786464 | tf_op jit(solution)/shard_map/ppermute | solution.py:525
  78.6 6.8 %all-gather.4.cloned.1.call-done.w_ref = bf16[1024,3200]{1,0:T(8,128)(2,1)} async-done(((bf16[128,3200]{1,0:T(8,128)(2,1)}), bf16[1024,3200]{1,0:T(8,128)(2,1)}) %all-gather.4.cloned.1.call-update) | async-done | bytes 6553616 | tf_op jit(solution)/shard_map/all_gather | solution.py:504
  88.9 14.2 %attention_forward_0.1 = (bf16[256,1024]{1,0:T(8,128)(2,1)}, bf16[256,1024]{1,0:T(8,128)(2,1)}, bf16[256,1024]{1,0:T(8,128)(2,1)}, bf16[256,1024]{1,0:T(8,128)(2...) custom-call(s32[2]{0:T(128)} %pad_add_fusion.1.place_ref.refs_0_, ...), custom_call_target="tpu_custom_call" | custom-call | flops 13799999488 | bytes 1048576 | tf_op jit(solution)/shard_map/attention_forward_0/pallas_call | solution.py:384
  103.1 5.5 %collective-permute-done.7.refs_9_.refs_7_ = bf16[384,1024]{1,0:T(8,128)(2,1)} collective-permute-done((bf16[384,1024]{1,0:T(8,128)(2,1)}, bf16[384,1024]{1,0:T(8,128)(2,1)}, u32[]{:S(2)}, u32[]{:S(2)}) %collective-permute-start.7) | collective-permute-done | bytes 786464 | tf_op jit(solution)/shard_map/ppermute | solution.py:525
  108.8 20.0 %collective-permute-done.8.refs_7_.refs_5_ = bf16[384,1024]{1,0:T(8,128)(2,1)S(1)} collective-permute-done((bf16[384,1024]{1,0:T(8,128)(2,1)S(1)}, bf16[384,1024]{1,0:T(8,128)(2,1)S(1)}, u32[]{:S(2)}, u32[]{:S(2)}) %collective-permute-start.8) | collective-permute-done | bytes 786464 | tf_op jit(solution)/shard_map/ppermute | solution.py:525
  131.4 12.5 %attention_forward_1.1 = (bf16[256,2176]{1,0:T(8,128)(2,1)}, bf16[256,1024]{1,0:T(8,128)(2,1)}, bf16[256,1024]{1,0:T(8,128)(2,1)}, bf16[256,1024]{1,0:T(8,128)(2...) custom-call(s32[2]{0:T(128)} %pad_add_fusion.1.place_ref.refs_0_, s32[2,4]{1,0:T(2,128)} %lens_ref.3, ...), custom_call_target="tpu_custom_call" | custom-call | flops 13799999488 | bytes 1048576 | tf_op jit(solution)/shard_map/attention_forward_1/pallas_call | solution.py:384
  143.9 4.5 %collective-permute-done.11.refs_8_.refs_6_ = bf16[384,1024]{1,0:T(8,128)(2,1)} collective-permute-done((bf16[384,1024]{1,0:T(8,128)(2,1)S(1)}, bf16[384,1024]{1,0:T(8,128)(2,1)}, u32[]{:S(2)}, u32[]{:S(2)}) %collective-permute-start.11) | collective-permute-done | bytes 786464 | tf_op jit(solution)/shard_map/ppermute | solution.py:525
  156.0 30.6 %experts_0_0.1 = (bf16[2048,2176]{1,0:T(8,128)(2,1)}, f32[1024,1024]{1,0:T(8,128)}, f32[512,1024]{1,0:T(8,128)}) custom-call(s32[2]{0:T(128)} %pad_add_fusion.1.place_ref.refs_0_, bf16[1024,1152]{1,0:T(8,128)(2,1)} %copy-done.17, bf16[1024,1152]{1,0:T(8,128)(2,1)} %copy-done.25, bf16[2048,1024]{1,0:T(8,128)(2,1)} %all-gather.6.cloned.1.call-done.refs_3_.refs_4_, ...), custom_call_target="tpu_custom_call" | custom-call | flops 32199999488 | bytes 1048576 | tf_op jit(solution)/shard_map/experts_0_0/pallas_call | solution.py:443
  187.6 30.2 %experts_0_1.1 = (bf16[2048,2176]{1,0:T(8,128)(2,1)}, f32[1024,1024]{1,0:T(8,128)}, f32[512,1024]{1,0:T(8,128)}) custom-call(s32[2]{0:T(128)} %pad_add_fusion.1.place_ref.refs_0_, bf16[1024,1152]{1,0:T(8,128)(2,1)} %copy-done.17, bf16[1024,1152]{1,0:T(8,128)(2,1)} %copy-done.25, bf16[2048,1024]{1,0:T(8,128)(2,1)} %all-gather.6.cloned.1.call-done.refs_3_.refs_4_, ...), custom_call_target="tpu_custom_call" | custom-call | flops 32199999488 | bytes 1048576 | tf_op jit(solution)/shard_map/experts_0_1/pallas_call | solution.py:443
  218.1 30.6 %experts_1_0.1 = (bf16[2048,2176]{1,0:T(8,128)(2,1)}, bf16[384,1024]{1,0:T(8,128)(2,1)}, bf16[384,1024]{1,0:T(8,128)(2,1)}, bf16[384,1024]{1,0:T(8,128)(2,1)}, bf16[384,1024]{1,0:T(8,128)(2,1)}) custom-call(s32[2]{0:T(128)} %pad_add_fusion.1.place_ref.refs_0_, bf16[2048,2176]{1,0:T(8,128)(2,1)} %all-gather.8.cloned.1.call-done.refs_1_.refs_2_, ...), custom_call_target="tpu_custom_call" | custom-call | flops 32199999488 | bytes 1048576 | tf_op jit(solution)/shard_map/experts_1_0/pallas_call | solution.py:443
  248.7 32.1 %experts_1_1.1 = (bf16[2048,1024]{1,0:T(8,128)(2,1)}, bf16[1024,1152]{1,0:T(8,128)(2,1)}, bf16[1024,1152]{1,0:T(8,128)(2,1)}, bf16[384,1024]{1,0:T(8,128)(2,1)},...) custom-call(s32[2]{0:T(128)} %pad_add_fusion.1.place_ref.refs_0_, ...), custom_call_target="tpu_custom_call" | custom-call | flops 32199999488 | bytes 1048576 | tf_op jit(solution)/shard_map/experts_1_1/pallas_call | solution.py:443
  294.5 15.3 %attention_backward_0.1 = (f32[256,1024]{1,0:T(8,128)}, bf16[256,1024]{1,0:T(8,128)(2,1)}, bf16[256,1024]{1,0:T(8,128)(2,1)}, bf16[256,1024]{1,0:T(8,128)(2,1)},...) custom-call(s32[2]{0:T(128)} %pad_add_fusion.1.place_ref.refs_0_, ...), custom_call_target="tpu_custom_call" | custom-call | flops 14949999616 | bytes 1048576 | tf_op jit(solution)/shard_map/attention_backward_0/pallas_call | solution.py:475
  318.1 5.4 %collective-permute-done.19 = bf16[128,1152]{1,0:T(8,128)(2,1)S(1)} collective-permute-done((bf16[128,1152]{1,0:T(8,128)(2,1)S(1)}, bf16[128,1152]{1,0:T(8,128)(2,1)S(1)}, u32[]{:S(2)}, u32[]{:S(2)}) %collective-permute-start.19) | collective-permute-done | bytes 294944 | tf_op jit(solution)/shard_map/ppermute | solution.py:520
  326.2 6.0 %collective-permute-done.21 = bf16[384,1024]{1,0:T(8,128)(2,1)S(1)} collective-permute-done((bf16[384,1024]{1,0:T(8,128)(2,1)S(1)}, bf16[384,1024]{1,0:T(8,128)(2,1)S(1)}, u32[]{:S(2)}, u32[]{:S(2)}) %collective-permute-start.21) | collective-permute-done | bytes 786464 | tf_op jit(solution)/shard_map/ppermute | solution.py:525
  334.6 22.4 %attention_backward_1.1 = (f32[256,1024]{1,0:T(8,128)}, bf16[4,4,32,3200]{3,2,1,0:T(8,128)(2,1)}, bf16[4,4,32,3200]{3,2,1,0:T(8,128)(2,1)}) custom-call(s32[2]{0:T(128)} %pad_add_fusion.1.place_ref.refs_0_, bf16[512,1024]{1,0:T(8,128)(2,1)} %refs_1_.3, bf16[512,1152]{1,0:T(8,128)(2,1)} %pad_maximum_fusion.3.cot_ref.refs_2_, ...), custom_call_target="tpu_custom_call" | custom-call | flops 20700000256 | bytes 1048576 | tf_op jit(solution)/shard_map/attention_backward_1/pallas_call | solution.py:475
  369.6 13.6 %collective-permute-done.26 = bf16[384,1024]{1,0:T(8,128)(2,1)S(1)} collective-permute-done((bf16[384,1024]{1,0:T(8,128)(2,1)S(1)}, bf16[384,1024]{1,0:T(8,128)(2,1)S(1)}, u32[]{:S(2)}, u32[]{:S(2)}) %collective-permute-start.26) | collective-permute-done | bytes 786464 | tf_op jit(solution)/shard_map/ppermute | solution.py:525
  383.2 4.4 collective-permute-done.24
  393.7 6.4 %collective-permute-done.27 = bf16[4,32,1536]{2,1,0:T(8,128)(2,1)S(1)} collective-permute-done((bf16[4,32,1536]{2,1,0:T(8,128)(2,1)S(1)}, bf16[4,32,1536]{2,1,0:T(8,128)(2,1)S(1)}, u32[]{:S(2)}, u32[]{:S(2)}) %collective-permute-start.27) | collective-permute-done | bytes 393248 | tf_op jit(solution)/shard_map/ppermute | solution.py:520
  400.2 8.4 %collective-permute-done.29 = bf16[384,1024]{1,0:T(8,128)(2,1)S(1)} collective-permute-done((bf16[384,1024]{1,0:T(8,128)(2,1)S(1)}, bf16[384,1024]{1,0:T(8,128)(2,1)S(1)}, u32[]{:S(2)}, u32[]{:S(2)}) %collective-permute-start.29) | collective-permute-done | bytes 786464 | tf_op jit(solution)/shard_map/ppermute | solution.py:525
  420.3 6.2 %collective-permute-done.31 = bf16[32,3200]{1,0:T(8,128)(2,1)} collective-permute-done((bf16[32,3200]{1,0:T(8,128)(2,1)}, bf16[32,3200]{1,0:T(8,128)(2,1)}, u32[]{:S(2)}, u32[]{:S(2)}) %collective-permute-start.31) | collective-permute-done | bytes 204832 | tf_op jit(solution)/shard_map/ppermute | solution.py:525
  429.9 9.9 %all-to-all-done.1 = bf16[8,2,48,1024]{3,2,1,0:T(8,128)(2,1)S(1)} async-done(((bf16[8,2,48,1024]{3,2,1,0:T(8,128)(2,1)}), bf16[8,2,48,1024]{3,2,1,0:T(8,128)(2,1)S(1)}, u32[]{:S(2)}, u32[]{:S(2)}) %all-to-all-start.1) | async-done | bytes 1572896 | tf_op jit(solution)/shard_map/all_to_all | solution.py:653
  (200 shorter events, 98.8 us)
Async XLA Ops:
  9.9 26.3 %all-to-all-start = ((bf16[8,2,48,1024]{3,2,1,0:T(8,128)(2,1)}), bf16[8,2,48,1024]{3,2,1,0:T(8,128)(2,1)S(1)}, u32[]{:S(2)}, u32[]{:S(2)}) async-start(bf16[8,2,48,1024]{3,2,1,0:T(8,128)(2,1)} %bitcast.4), calls=%async_computation | async-start | bytes 3145728 | tf_op jit(solution)/shard_map/all_to_all | solution.py:582
  15.2 70.2 %all-gather.4.cloned.1.call-start = ((), (), s32[]{:S(2)}) async-start(), calls=%async_computation.4 | async-start | bytes 7372800 | tf_op jit(solution)/shard_map/all_gather | solution.py:504
  15.7 20.9 %collective-permute-start = (bf16[32,3200]{1,0:T(8,128)(2,1)S(1)}, bf16[32,3200]{1,0:T(8,128)(2,1)S(1)}, u32[]{:S(2)}, u32[]{:S(2)}) collective-permute-start(bf16[32,3200]{1,0:T(8,128)(2,1)S(1)} %concatenate.37), channel_id=1, source_target_pairs={{0,8},{8,16},{16,24},{24,0},{1,9},{9,17},{17,25},{25,1},{2,10},{10... | collective-permute-start | bytes 614408 | tf_op jit(solution)/shard_map/ppermute | solution.py:525
  17.3 19.2 %collective-permute-start.1 = (bf16[32,3200]{1,0:T(8,128)(2,1)S(1)}, bf16[32,3200]{1,0:T(8,128)(2,1)S(1)}, u32[]{:S(2)}, u32[]{:S(2)}) collective-permute-start(bf16[32,3200]{1,0:T(8,128)(2,1)S(1)} %concatenate.37), channel_id=1, source_target_pairs={{0,16},{8,24},{16,0},{24,8},{1,17},{9,25},{17,1},{25,9},{2,18},{10... | collective-permute-start | bytes 614408 | tf_op jit(solution)/shard_map/ppermute | solution.py:525
  37.6 117.1 %all-gather.6.cloned.1.call-start = ((), (), s32[]{:S(2)}) async-start(), calls=%async_computation.5 | async-start | bytes 4718592 | tf_op jit(solution)/shard_map/all_gather | solution.py:504
  37.7 20.8 %collective-permute-start.3 = (bf16[384,1024]{1,0:T(8,128)(2,1)S(1)}, bf16[384,1024]{1,0:T(8,128)(2,1)}, u32[]{:S(2)}, u32[]{:S(2)}) collective-permute-start(bf16[384,1024]{1,0:T(8,128)(2,1)S(1)} %get-tuple-element.94.refs_6_.refs_4_), channel_id=1, source_target_pairs={{0,8},{8,16},{16,24},{24,0},{1,9},{9,17},{17,25},{25,1},{2,10},{10... | collective-permute-start | bytes 2359304 | tf_op jit(solution)/shard_map/ppermute | solution.py:525
  58.5 20.0 %collective-permute-start.4 = (bf16[384,1024]{1,0:T(8,128)(2,1)}, bf16[384,1024]{1,0:T(8,128)(2,1)}, u32[]{:S(2)}, u32[]{:S(2)}) collective-permute-start(bf16[384,1024]{1,0:T(8,128)(2,1)} %collective-permute-done.3.refs_7_.refs_5_), channel_id=1, source_target_pairs={{0,8},{8,16},{16,24},{24,0},{1,9},{9,17},{17,25},{25,1},{2,10},{10... | collective-permute-start | bytes 2359304 | tf_op jit(solution)/shard_map/ppermute | solution.py:525
  87.4 21.3 %collective-permute-start.7 = (bf16[384,1024]{1,0:T(8,128)(2,1)}, bf16[384,1024]{1,0:T(8,128)(2,1)}, u32[]{:S(2)}, u32[]{:S(2)}) collective-permute-start(bf16[384,1024]{1,0:T(8,128)(2,1)} %collective-permute-done.4.refs_8_.refs_6_), channel_id=1, source_target_pairs={{0,8},{8,16},{16,24},{24,0},{1,9},{9,17},{17,25},{25,1},{2,10},{10... | collective-permute-start | bytes 2359304 | tf_op jit(solution)/shard_map/ppermute | solution.py:525
  108.7 109.4 %all-gather.8.cloned.1.call-start = ((), (), s32[]{:S(2)}) async-start(), calls=%async_computation.7 | async-start | bytes 10027008 | tf_op jit(solution)/shard_map/all_gather | solution.py:504
  108.8 20.1 %collective-permute-start.8 = (bf16[384,1024]{1,0:T(8,128)(2,1)S(1)}, bf16[384,1024]{1,0:T(8,128)(2,1)S(1)}, u32[]{:S(2)}, u32[]{:S(2)}) collective-permute-start(bf16[384,1024]{1,0:T(8,128)(2,1)S(1)} %get-tuple-element.103.refs_6_.refs_4_), channel_id=1, source_target_pairs={{0,8},{8,16},{16,24},{24,0},{1,9},{9,17},{17,25},{25,1},{2,10},{10... | collective-permute-start | bytes 2359304 | tf_op jit(solution)/shard_map/ppermute | solution.py:525
  128.9 19.5 %collective-permute-start.11 = (bf16[384,1024]{1,0:T(8,128)(2,1)S(1)}, bf16[384,1024]{1,0:T(8,128)(2,1)}, u32[]{:S(2)}, u32[]{:S(2)}) collective-permute-start(bf16[384,1024]{1,0:T(8,128)(2,1)S(1)} %collective-permute-done.8.refs_7_.refs_5_), channel_id=1, source_target_pairs={{0,8},{8,16},{16,24},{24,0},{1,9},{9,17},{17,25},{25,1},{2,10},{10... | collective-permute-start | bytes 2359304 | tf_op jit(solution)/shard_map/ppermute | solution.py:525
  129.2 19.2 %collective-permute-start.10 = (bf16[128,1152]{1,0:T(8,128)(2,1)S(1)}, bf16[128,1152]{1,0:T(8,128)(2,1)S(1)}, u32[]{:S(2)}, u32[]{:S(2)}) collective-permute-start(bf16[128,1152]{1,0:T(8,128)(2,1)S(1)} %slice.150), channel_id=1, source_target_pairs={{0,2},{2,0},{1,3},{3,1},{4,6},{6,4},{5,7},{7,5},{8,10},{10,8},{9,1... | collective-permute-start | bytes 884744 | tf_op jit(solution)/shard_map/ppermute | solution.py:520
  148.4 146.1 %reduce-scatter.3.cloned.1.call-start = ((), (), s32[]{:S(2)}) async-start(), calls=%async_computation.6 | async-start | bytes 10027008 | tf_op jit(solution)/shard_map/reduce_scatter | solution.py:508
  150.1 36.5 %collective-permute-start.13 = (bf16[384,1024]{1,0:T(8,128)(2,1)}, bf16[384,1024]{1,0:T(8,128)(2,1)S(1)}, u32[]{:S(2)}, u32[]{:S(2)}) collective-permute-start(bf16[384,1024]{1,0:T(8,128)(2,1)} %collective-permute-done.11.refs_8_.refs_6_), channel_id=1, source_target_pairs={{0,8},{8,16},{16,24},{24,0},{1,9},{9,17},{17,25},{25,1},{2,10},{10... | collective-permute-start | bytes 2359304 | tf_op jit(solution)/shard_map/ppermute | solution.py:525
  217.8 139.2 %reduce-scatter.5.cloned.1.call-start = ((), (), s32[]{:S(2)}) async-start(), calls=%async_computation.8 | async-start | bytes 4718592 | tf_op jit(solution)/shard_map/reduce_scatter | solution.py:508
  248.7 32.2 %collective-permute-start.14 = (bf16[384,1024]{1,0:T(8,128)(2,1)}, bf16[384,1024]{1,0:T(8,128)(2,1)S(1)}, u32[]{:S(2)}, u32[]{:S(2)}) collective-permute-start(bf16[384,1024]{1,0:T(8,128)(2,1)} %get-tuple-element.127), channel_id=1, source_target_pairs={{0,8},{8,16},{16,24},{24,0},{1,9},{9,17},{17,25},{25,1},{2,10},{10... | collective-permute-start | bytes 2359304 | tf_op jit(solution)/shard_map/ppermute | solution.py:525
  285.6 24.2 %collective-permute-start.18 = (bf16[384,1024]{1,0:T(8,128)(2,1)}, bf16[384,1024]{1,0:T(8,128)(2,1)S(1)}, u32[]{:S(2)}, u32[]{:S(2)}) collective-permute-start(bf16[384,1024]{1,0:T(8,128)(2,1)} %add_convert_fusion.9), channel_id=1, source_target_pairs={{0,8},{8,16},{16,24},{24,0},{1,9},{9,17},{17,25},{25,1},{2,10},{10... | collective-permute-start | bytes 2359304 | tf_op jit(solution)/shard_map/ppermute | solution.py:525
  309.9 22.3 %collective-permute-start.21 = (bf16[384,1024]{1,0:T(8,128)(2,1)S(1)}, bf16[384,1024]{1,0:T(8,128)(2,1)S(1)}, u32[]{:S(2)}, u32[]{:S(2)}) collective-permute-start(bf16[384,1024]{1,0:T(8,128)(2,1)S(1)} %copy-done.27), channel_id=1, source_target_pairs={{0,8},{8,16},{16,24},{24,0},{1,9},{9,17},{17,25},{25,1},{2,10},{10... | collective-permute-start | bytes 2359304 | tf_op jit(solution)/shard_map/ppermute | solution.py:525
  313.8 45.7 %collective-permute-start.22 = (bf16[384,1024]{1,0:T(8,128)(2,1)}, bf16[384,1024]{1,0:T(8,128)(2,1)}, u32[]{:S(2)}, u32[]{:S(2)}) collective-permute-start(bf16[384,1024]{1,0:T(8,128)(2,1)} %add_convert_fusion.8), channel_id=1, source_target_pairs={{0,8},{8,16},{16,24},{24,0},{1,9},{9,17},{17,25},{25,1},{2,10},{10... | collective-permute-start | bytes 2359304 | tf_op jit(solution)/shard_map/ppermute | solution.py:525
  361.2 22.0 %collective-permute-start.26 = (bf16[384,1024]{1,0:T(8,128)(2,1)S(1)}, bf16[384,1024]{1,0:T(8,128)(2,1)S(1)}, u32[]{:S(2)}, u32[]{:S(2)}) collective-permute-start(bf16[384,1024]{1,0:T(8,128)(2,1)S(1)} %add_convert_fusion.7), channel_id=1, source_target_pairs={{0,8},{8,16},{16,24},{24,0},{1,9},{9,17},{17,25},{25,1},{2,10},{10... | collective-permute-start | bytes 2359304 | tf_op jit(solution)/shard_map/ppermute | solution.py:525
  366.6 21.1 %collective-permute-start.25 = (bf16[4,2,32,1664]{3,2,1,0:T(8,128)(2,1)S(1)}, bf16[4,2,32,1664]{3,2,1,0:T(8,128)(2,1)S(1)}, u32[]{:S(2)}, u32[]{:S(2)}) collective-permute-start(bf16[4,2,32,1664]{3,2,1,0:T(8,128)(2,1)S(1)} %slice.203), channel_id=1, source_target_pairs={{0,4},{4,0},{1,5},{5,1},{2,6},{6,2},{3,7},{7,3},{8,12},{12,8},{9,1... | collective-permute-start | bytes 2555912 | tf_op jit(solution)/shard_map/ppermute | solution.py:520
  368.2 19.4 %collective-permute-start.24 = (bf16[4,2,32,1536]{3,2,0,1:T(8,128)(2,1)S(1)}, bf16[4,2,32,1536]{3,2,0,1:T(8,128)(2,1)S(1)}, u32[]{:S(2)}, u32[]{:S(2)}) collective-permute-start(bf16[4,2,32,1536]{3,2,0,1:T(8,128)(2,1)S(1)} %copy.69), channel_id=1, source_target_pairs={{0,2},{2,0},{1,3},{3,1},{4,6},{6,4},{5,7},{7,5},{8,10},{10,8},{9,1... | collective-permute-start | bytes 2359304 | tf_op jit(solution)/shard_map/ppermute | solution.py:520
  388.0 20.6 %collective-permute-start.29 = (bf16[384,1024]{1,0:T(8,128)(2,1)S(1)}, bf16[384,1024]{1,0:T(8,128)(2,1)S(1)}, u32[]{:S(2)}, u32[]{:S(2)}) collective-permute-start(bf16[384,1024]{1,0:T(8,128)(2,1)S(1)} %add_convert_fusion.5), channel_id=1, source_target_pairs={{0,8},{8,16},{16,24},{24,0},{1,9},{9,17},{17,25},{25,1},{2,10},{10... | collective-permute-start | bytes 2359304 | tf_op jit(solution)/shard_map/ppermute | solution.py:525
  415.2 24.7 %all-to-all-start.1 = ((bf16[8,2,48,1024]{3,2,1,0:T(8,128)(2,1)}), bf16[8,2,48,1024]{3,2,1,0:T(8,128)(2,1)S(1)}, u32[]{:S(2)}, u32[]{:S(2)}) async-start(bf16[8,2,48,1024]{3,2,1,0:T(8,128)(2,1)} %copy_bitcast_fusion), calls=%async_computation.3 | async-start | bytes 3145728 | tf_op jit(solution)/shard_map/all_to_all | solution.py:653
  (46 other events, 473.4 us)
Sparse Core Ops, SparseCore 0:
  37.7 47.6 all-gather.3
  108.8 41.1 all-gather.5
  151.9 59.2 all-gather.7
  218.0 71.4 reduce-scatter.2
  292.6 55.2 reduce-scatter.4

commit v4 on v3

--- a/solution.py
+++ b/solution.py
@@ -195,9 +195,14 @@
     cot = jnp.concatenate([ref[:, :D] for ref in cots], axis=0)
     hot = jnp.concatenate([ref[:, D:DMID] for ref in cots], axis=0).astype(F32)
     lane = lane_of(nm.shape[0])
-    gates = masked_gates(dot(nm, wr_ref[...]), hot > 0.5)
     expert = place_ref[0] * OWN + e
-    combine = jnp.sum(jnp.where(lane == expert, gates, 0.0), axis=1, keepdims=True)
+    if e:
+        handed = partial_ref[:, D:DMID].astype(F32)
+        mine = (lane == expert + 2 * E) | (lane == expert + 3 * E)
+        combine = jnp.sum(jnp.where(mine, handed, 0.0), axis=1, keepdims=True)
+    else:
+        gates = masked_gates(dot(nm, wr_ref[...]), hot > 0.5)
+        combine = jnp.sum(jnp.where(lane == expert, gates, 0.0), axis=1, keepdims=True)
     gateup = dot(nm, w_gu[...])
     gate, up = gateup[:, :FF], gateup[:, FF:]
     s = 1.0 / (1.0 + jnp.exp(-gate))
@@ -218,8 +223,11 @@
     extra = jnp.where(lane == expert, high, 0.0) + jnp.where(lane == expert + E, d_combine - high, 0.0)
     if e:
         d_mid = d_mid + partial_ref[:, :D].astype(F32)
-        extra = extra + partial_ref[:, D:DMID].astype(F32)
+        extra = extra + jnp.where(lane < 2 * E, handed, 0.0)
         out = out + partial_ref[:, DMID:].astype(F32)
+    else:
+        high = gates.astype(BF).astype(F32)
+        extra = extra + pltpu.roll(high, 2 * E, 1) + pltpu.roll(gates - high, 3 * E, 1)
     d_mid = jnp.concatenate([d_mid.astype(BF), extra.astype(BF)], axis=1)
     out = out.astype(BF)
     if not e:
@@ -279,6 +287,26 @@
     d_resid = cot + inverse * u - resid * (inverse * inverse * inverse) * mean_rows(u * resid)
     gain_mid_grad = jnp.sum(d_mid * resid * inverse, axis=0, keepdims=True)
     d_branch = d_resid.astype(BF)
+    both = lambda k, value: jnp.concatenate([old[k][...], value], axis=0)
+    leaving = []
+
+    def leave(k, part):
+        grad_ref, sems = refs
+        share = D // outer // PLANE
+        for s in range(outer):
+            z = lax.rem(place_ref[1] + s, outer)
+            for q in range(PLANE // 2):
+                for other in range(2):
+                    device = lax.bitwise_xor(place_ref[0], 2 * q + other)
+                    at = pl.ds(pl.multiple_of((z * PLANE + device) * share, share), share)
+                    sem = sems.at[k, s * PLANE + 2 * q + other]
+                    copy = pltpu.make_async_copy(grad_ref.at[at, part], kept[other].at[s, q, :, part], sem)
+                    copy.start()
+                    leaving.append(copy)
+
+    if last:
+        refs[0][:, 2 * D : 3 * D] = dot(both(6, mixed_ref[...]), both(3, d_branch), 0, 0).astype(BF)
+        leave(0, slice(2 * D, 3 * D))
     d_mixed = dot(d_branch, w_ref[:, 2 * D : 3 * D], 1, 1).astype(BF)
 
     cosine, sine = cos_ref[...], sin_ref[...]
@@ -319,6 +347,11 @@
     x = tok_ref[...].astype(F32)
     inverse = lax.rsqrt(mean_rows(x * x) + EPS)
     normed = (x * inverse * gain_in).astype(BF)
+    if last:
+        normed_two = both(0, normed)
+        refs[0][:, : D] = dot(normed_two, both(1, d_q), 0, 0).astype(BF)
+        refs[0][:, D : 2 * D] = dot(normed_two, both(2, d_kv), 0, 0).astype(BF)
+        leave(1, slice(0, 2 * D))
     d_in = dot(d_q, w_ref[:, :D], 1, 1) + dot(d_kv, w_ref[:, D : 2 * D], 1, 1)
     v = d_in * gain_in
     rows_ref[...] = d_resid + inverse * v - x * (inverse * inverse * inverse) * mean_rows(v * x)
@@ -328,27 +361,10 @@
         for ref, value in zip(kept, (normed, d_q, d_kv, d_branch, d_logits, gains)):
             ref[...] = value
         return
-    both = lambda k, value: jnp.concatenate([old[k][...], value], axis=0)
-    grad_ref, sems = refs
-    normed_two = both(0, normed)
-    grad_ref[:, :D] = dot(normed_two, both(1, d_q), 0, 0).astype(BF)
-    grad_ref[:, D : 2 * D] = dot(normed_two, both(2, d_kv), 0, 0).astype(BF)
-    grad_ref[:, 2 * D : 3 * D] = dot(both(6, mixed_ref[...]), both(3, d_branch), 0, 0).astype(BF)
     gains = jnp.concatenate([jnp.zeros((E, D), F32), gains + old[5][...], jnp.zeros((LANES - E - 8, D), F32)], axis=0)
-    grad_ref[:, 3 * D :] = (dot(both(7, nm), both(4, d_logits), 0, 0) + gains.T).astype(BF)
-    share = D // outer // PLANE
-    copies = []
-    for s in range(outer):
-        z = lax.rem(place_ref[1] + s, outer)
-        for q in range(PLANE // 2):
-            for other in range(2):
-                device = lax.bitwise_xor(place_ref[0], 2 * q + other)
-                at = pl.ds(pl.multiple_of((z * PLANE + device) * share, share), share)
-                sem = sems.at[s * PLANE + 2 * q + other]
-                copies.append(pltpu.make_async_copy(grad_ref.at[at], kept[other].at[s, q], sem))
-    for copy in copies:
-        copy.start()
-    for copy in copies:
+    refs[0][:, 3 * D :] = (dot(both(7, nm), both(4, d_logits), 0, 0) + gains.T).astype(BF)
+    leave(2, slice(3 * D, WIDE))
+    for copy in leaving:
         copy.wait()
 
 
@@ -471,7 +487,7 @@
         share = D // outer // PLANE
         kept = [jax.ShapeDtypeStruct((outer, PLANE // 2, share, WIDE), BF)] * 2
         kept_specs = [any_ref] * 2
-        scratch = [pltpu.VMEM((D, WIDE), BF), pltpu.SemaphoreType.DMA((outer * PLANE,))]
+        scratch = [pltpu.VMEM((D, WIDE), BF), pltpu.SemaphoreType.DMA((3, outer * PLANE))]
     return pl.pallas_call(
         functools.partial(attention_backward_kernel, outer, last),
         grid_spec=pltpu.PrefetchScalarGridSpec(
@@ -604,13 +620,13 @@
     *saved_0, packed = attention_forward(0, outer, place, lengths, tokens, cot, packed, cosine, sine)
     nm_0, from_x, from_y, homes[0][-1] = tie(saved_0[0], from_x, from_y, ring(0))
     nm_0 = gather(nm_0, PLANE_AXES)
-    packed, homes[1][-1] = tie(packed, ring(1, max(outer - 3, 0)))
     corner_a, corner_b = across(from_x[: MB // 2], "y"), across(from_y[MB // 2 :], "x")
+    packed, corner_a, corner_b, homes[1][-1] = tie(packed, corner_a, corner_b, ring(1, max(outer - 3, 0)))
+    cot_same = jnp.concatenate([cot_0, from_x, from_y, corner_a, corner_b], axis=0)
+    cot_other = across(cot_same, "c")
     saved_1 = attention_forward(1, outer, place, lengths, tokens, cot, packed, cosine, sine)
-    nm_1, corner_a, corner_b, homes[1][-1] = tie(saved_1[0], corner_a, corner_b, ring(1))
-    cot_same = jnp.concatenate([cot_0, from_x, from_y, corner_a, corner_b], axis=0)
+    nm_1, cot_other, homes[1][-1] = tie(saved_1[0], cot_other, ring(1))
     nm_1 = gather(nm_1, PLANE_AXES)
-    cot_other = across(cot_same, "c")
     ring(1, outer - len(homes[1]))
 
     rows = [cot_same, cot_other, nm_0, nm_0]
@@ -635,13 +651,16 @@
     early = rows_0, pass_on(0, 2, outer - 1)
     moved[1] = after(moved[1], rows_0)
     d_mid_1, (rows_0, moved[0]), moved[1] = sum_to_owners(same_1, other_1, early, pass_on(1, 1, outer - 2))
+    summed_0, out_1 = both_0[:, DMID:], scatter_sum(out_1, PLANE_AXES)
+    d_mid_1, moved[1] = tie(d_mid_1, moved[1])
+    following = plus(turns[1][outer - 2], moved[1])
+    d_mid_1, following = tie(d_mid_1, following)
     rows_1, grads, grads_other = attention_backward(1, outer, place, tokens, cot, saved_1, d_mid_1, packed, cosine, sine, old)
-    out_sums = both_0[:, DMID:], scatter_sum(out_1, PLANE_AXES)
+    grads, grads_other, moved[0], out_1 = tie(grads, grads_other, pass_on(0, outer - 1, outer), out_1)
+    out_sums = summed_0, out_1
     output = [(saved[4] + part.astype(F32)).astype(BF) for saved, part in zip((saved_0, saved_1), out_sums)]
-    grads, grads_other, moved[0], output[1] = tie(grads, grads_other, pass_on(0, outer - 1, outer), output[1])
-
     beside = (
-        (lambda: pass_on(1, outer - 2, outer - 1), lambda v: moved.__setitem__(1, v)),
+        (lambda: onward(following), lambda v: moved.__setitem__(1, v)),
         (lambda: pass_on(1, outer - 1, outer), lambda v: moved.__setitem__(1, v)),
     )
     grads = sum_weights(grads, grads_other, beside)
@@ -651,7 +670,7 @@
         [up.reshape(OWN, PLANE, share, D), down.reshape(OWN, PLANE, share // 2, D)], axis=2
     ).transpose(1, 0, 2, 3)
     home = lax.all_to_all(home, PLANE_AXES, split_axis=0, concat_axis=0, tiled=True)
-    home = home.reshape(E, -1, D).astype(F32)
+    home = home.reshape(E, -1, D)
     return (
         jnp.concatenate(output, axis=0),
         jnp.concatenate([rows_0, rows_1], axis=0),
@@ -661,8 +680,8 @@
         grads[:, 2 * D : 3 * D],
         grads[:, 3 * D + E + 1],
         grads[:, 3 * D : 3 * D + E],
-        home[:, :share],
-        home[:, share:],
+        home[:, :share].astype(F32),
+        home[:, share:].astype(F32),
     )
 
 

time: 457 us -> 447 us (0.978)
  local copies, waits for them, and re-layouts: 13.3 us -> 7.58 us
    ppermute x18, waiting for transfers between devices: 95.3 us -> 100 us  [onward(): lax.ppermute(v, 'z', [(i, (i + steps) % count) for i in range(count)])]
  transfers between devices with their start and end apart: 40 -> 40, of which waited for: 21 -> 18; matrix products, arithmetic and copies ran while one was open for 8% -> 7% of each run, Pallas kernels for 42% -> 42%
where the time goes in v4:
time: 447 us; the launch traced here: 440 us
  Pallas kernels  184 us (41%)
  waiting for transfers between devices  155 us (35%)
  starting transfers between devices  42.9 us (10%)
  other arithmetic  35.1 us (8%)
  between operations  14.7 us (3%)
  local copies, waits for them, and re-layouts  7.58 us (2%)
    pallas_call x4, Pallas kernels, experts(): pl.pallas_call(functools.partial(expert_kernel, outer, micro, e), grid_sp...  122 us
    ppermute x18, waiting for transfers between devices, onward(): lax.ppermute(v, 'z', [(i, (i + steps) % count) for i in range(count)])  100 us
    pallas_call x2, Pallas kernels, attention_backward(): pl.pallas_call(functools.partial(attention_backward_kernel, outer, last),...  35.8 us
    pallas_call x2, Pallas kernels, attention_forward(): pl.pallas_call(functools.partial(attention_forward_kernel, micro, outer),...  26.7 us
    ppermute x15, waiting for transfers between devices, across(): return lax.ppermute(v, axis, [(0, 1), (1, 0)])  23.4 us
    ppermute x18, starting transfers between devices, onward(): lax.ppermute(v, 'z', [(i, (i + steps) % count) for i in range(count)])  20.1 us
    all_to_all x1, waiting for transfers between devices, shards(): lax.all_to_all(sent.reshape(PLANE, OWN, *sent.shape[1:]), PLANE_AXES, spl...  15 us
    ppermute x15, starting transfers between devices, across(): return lax.ppermute(v, axis, [(0, 1), (1, 0)])  13.5 us
  transfers between devices with their start and end apart: 40, of which 18 were waited for; matrix products, arithmetic and copies ran while one was open for 7% of the time, Pallas kernels for 42%

profile of v4, /device:TPU:0, one launch (start us, length us, event | category | flops | bytes accessed | tf_op | source)
XLA Modules:
  0.0 439.6 jit_solution(2800057475857736900)
XLA Ops:
  9.9 5.3 %all-to-all-start = ((bf16[8,2,48,1024]{3,2,1,0:T(8,128)(2,1)}), bf16[8,2,48,1024]{3,2,1,0:T(8,128)(2,1)S(1)}, u32[]{:S(2)}, u32[]{:S(2)}) async-start(bf16[8,2,48,1024]{3,2,1,0:T(8,128)(2,1)} %bitcast.4), calls=%async_computation | async-start | bytes 3145728 | tf_op jit(solution)/shard_map/all_to_all | solution.py:598
  21.3 15.0 %all-to-all-done = bf16[8,2,48,1024]{3,2,1,0:T(8,128)(2,1)S(1)} async-done(((bf16[8,2,48,1024]{3,2,1,0:T(8,128)(2,1)}), bf16[8,2,48,1024]{3,2,1,0:T(8,128)(2,1)S(1)}, u32[]{:S(2)}, u32[]{:S(2)}) %all-to-all-start) | async-done | bytes 1572896 | tf_op jit(solution)/shard_map/all_to_all | solution.py:598
  43.4 15.1 %collective-permute-done.3.refs_7_.refs_5_ = bf16[384,1024]{1,0:T(8,128)(2,1)} collective-permute-done((bf16[384,1024]{1,0:T(8,128)(2,1)S(1)}, bf16[384,1024]{1,0:T(8,128)(2,1)}, u32[]{:S(2)}, u32[]{:S(2)}) %collective-permute-start.3) | collective-permute-done | bytes 786464 | tf_op jit(solution)/shard_map/ppermute | solution.py:541
  63.2 15.4 %collective-permute-done.4.refs_8_.refs_6_ = bf16[384,1024]{1,0:T(8,128)(2,1)} collective-permute-done((bf16[384,1024]{1,0:T(8,128)(2,1)}, bf16[384,1024]{1,0:T(8,128)(2,1)}, u32[]{:S(2)}, u32[]{:S(2)}) %collective-permute-start.4) | collective-permute-done | bytes 786464 | tf_op jit(solution)/shard_map/ppermute | solution.py:541
  78.6 6.8 %all-gather.4.cloned.1.call-done.w_ref = bf16[1024,3200]{1,0:T(8,128)(2,1)} async-done(((bf16[128,3200]{1,0:T(8,128)(2,1)}), bf16[1024,3200]{1,0:T(8,128)(2,1)}) %all-gather.4.cloned.1.call-update) | async-done | bytes 6553616 | tf_op jit(solution)/shard_map/all_gather | solution.py:520
  88.9 14.2 %attention_forward_0.1 = (bf16[256,1024]{1,0:T(8,128)(2,1)}, bf16[256,1024]{1,0:T(8,128)(2,1)}, bf16[256,1024]{1,0:T(8,128)(2,1)}, bf16[256,1024]{1,0:T(8,128)(2...) custom-call(s32[2]{0:T(128)} %pad_add_fusion.1.place_ref.refs_0_, ...), custom_call_target="tpu_custom_call" | custom-call | flops 13799999488 | bytes 1048576 | tf_op jit(solution)/shard_map/attention_forward_0/pallas_call | solution.py:400
  103.1 5.4 %collective-permute-done.7.refs_9_.refs_7_ = bf16[384,1024]{1,0:T(8,128)(2,1)S(1)} collective-permute-done((bf16[384,1024]{1,0:T(8,128)(2,1)}, bf16[384,1024]{1,0:T(8,128)(2,1)S(1)}, u32[]{:S(2)}, u32[]{:S(2)}) %collective-permute-start.7) | collective-permute-done | bytes 786464 | tf_op jit(solution)/shard_map/ppermute | solution.py:541
  111.2 17.7 %collective-permute-done.10.refs_7_.refs_5_ = bf16[384,1024]{1,0:T(8,128)(2,1)} collective-permute-done((bf16[384,1024]{1,0:T(8,128)(2,1)S(1)}, bf16[384,1024]{1,0:T(8,128)(2,1)}, u32[]{:S(2)}, u32[]{:S(2)}) %collective-permute-start.10) | collective-permute-done | bytes 786464 | tf_op jit(solution)/shard_map/ppermute | solution.py:541
  129.6 12.5 %attention_forward_1.1 = (bf16[256,2176]{1,0:T(8,128)(2,1)}, bf16[256,1024]{1,0:T(8,128)(2,1)}, bf16[256,1024]{1,0:T(8,128)(2,1)}, bf16[256,1024]{1,0:T(8,128)(2...) custom-call(s32[2]{0:T(128)} %pad_add_fusion.1.place_ref.refs_0_, s32[2,4]{1,0:T(2,128)} %lens_ref.3, ...), custom_call_target="tpu_custom_call" | custom-call | flops 13799999488 | bytes 1048576 | tf_op jit(solution)/shard_map/attention_forward_1/pallas_call | solution.py:400
  142.1 9.4 %collective-permute-done.12.refs_8_.refs_6_ = bf16[384,1024]{1,0:T(8,128)(2,1)S(1)} collective-permute-done((bf16[384,1024]{1,0:T(8,128)(2,1)}, bf16[384,1024]{1,0:T(8,128)(2,1)S(1)}, u32[]{:S(2)}, u32[]{:S(2)}) %collective-permute-start.12) | collective-permute-done | bytes 786464 | tf_op jit(solution)/shard_map/ppermute | solution.py:541
  152.9 30.9 %experts_0_0.1 = (bf16[2048,2176]{1,0:T(8,128)(2,1)}, f32[1024,1024]{1,0:T(8,128)}, f32[512,1024]{1,0:T(8,128)}) custom-call(s32[2]{0:T(128)} %pad_add_fusion.1.place_ref.refs_0_, bf16[1024,1152]{1,0:T(8,128)(2,1)} %copy-done.16, bf16[1024,1152]{1,0:T(8,128)(2,1)} %copy-done.24, bf16[2048,1024]{1,0:T(8,128)(2,1)} %all-gather.6.cloned.1.call-done.refs_3_.refs_4_, ...), custom_call_target="tpu_custom_call" | custom-call | flops 32199999488 | bytes 1048576 | tf_op jit(solution)/shard_map/experts_0_0/pallas_call | solution.py:459
  183.8 29.3 %experts_0_1.1 = (bf16[2048,2176]{1,0:T(8,128)(2,1)}, f32[1024,1024]{1,0:T(8,128)}, f32[512,1024]{1,0:T(8,128)}) custom-call(s32[2]{0:T(128)} %pad_add_fusion.1.place_ref.refs_0_, bf16[1024,1152]{1,0:T(8,128)(2,1)} %copy-done.16, bf16[1024,1152]{1,0:T(8,128)(2,1)} %copy-done.24, bf16[2048,1024]{1,0:T(8,128)(2,1)} %all-gather.6.cloned.1.call-done.refs_3_.refs_4_, ...), custom_call_target="tpu_custom_call" | custom-call | flops 32199999488 | bytes 1048576 | tf_op jit(solution)/shard_map/experts_0_1/pallas_call | solution.py:459
  213.4 30.2 %experts_1_0.1 = (bf16[2048,2176]{1,0:T(8,128)(2,1)}, bf16[384,1024]{1,0:T(8,128)(2,1)}, bf16[384,1024]{1,0:T(8,128)(2,1)}, bf16[384,1024]{1,0:T(8,128)(2,1)}, bf16[384,1024]{1,0:T(8,128)(2,1)}) custom-call(s32[2]{0:T(128)} %pad_add_fusion.1.place_ref.refs_0_, bf16[2048,2176]{1,0:T(8,128)(2,1)} %all-gather.8.cloned.1.call-done.refs_1_.refs_2_, ...), custom_call_target="tpu_custom_call" | custom-call | flops 32199999488 | bytes 1048576 | tf_op jit(solution)/shard_map/experts_1_0/pallas_call | solution.py:459
  243.7 31.1 %experts_1_1.1 = (bf16[2048,1024]{1,0:T(8,128)(2,1)}, bf16[1024,1152]{1,0:T(8,128)(2,1)}, bf16[1024,1152]{1,0:T(8,128)(2,1)}, bf16[384,1024]{1,0:T(8,128)(2,1)},...) custom-call(s32[2]{0:T(128)} %pad_add_fusion.1.place_ref.refs_0_, ...), custom_call_target="tpu_custom_call" | custom-call | flops 32199999488 | bytes 1048576 | tf_op jit(solution)/shard_map/experts_1_1/pallas_call | solution.py:459
  287.2 14.5 %attention_backward_0.1 = (f32[256,1024]{1,0:T(8,128)}, bf16[256,1024]{1,0:T(8,128)(2,1)}, bf16[256,1024]{1,0:T(8,128)(2,1)}, bf16[256,1024]{1,0:T(8,128)(2,1)},...) custom-call(s32[2]{0:T(128)} %pad_add_fusion.1.place_ref.refs_0_, ...), custom_call_target="tpu_custom_call" | custom-call | flops 14949999616 | bytes 1048576 | tf_op jit(solution)/shard_map/attention_backward_0/pallas_call | solution.py:491
  309.9 14.4 %collective-permute-done.21 = bf16[384,1024]{1,0:T(8,128)(2,1)S(1)} collective-permute-done((bf16[384,1024]{1,0:T(8,128)(2,1)}, bf16[384,1024]{1,0:T(8,128)(2,1)S(1)}, u32[]{:S(2)}, u32[]{:S(2)}) %collective-permute-start.21) | collective-permute-done | bytes 786464 | tf_op jit(solution)/shard_map/ppermute | solution.py:541
  326.7 21.2 %attention_backward_1.1 = (f32[256,1024]{1,0:T(8,128)}, bf16[4,4,32,3200]{3,2,1,0:T(8,128)(2,1)}, bf16[4,4,32,3200]{3,2,1,0:T(8,128)(2,1)}) custom-call(s32[2]{0:T(128)} %pad_add_fusion.1.place_ref.refs_0_, bf16[512,1024]{1,0:T(8,128)(2,1)} %refs_1_.3, bf16[512,1152]{1,0:T(8,128)(2,1)} %pad_maximum_fusion.3.cot_ref.refs_2_, ...), custom_call_target="tpu_custom_call" | custom-call | flops 20700000256 | bytes 1048576 | tf_op jit(solution)/shard_map/attention_backward_1/pallas_call | solution.py:491
  348.6 5.6 %collective-permute-done.23 = bf16[4,4,32,3200]{3,2,1,0:T(8,128)(2,1)S(1)} collective-permute-done((bf16[4,4,32,3200]{3,2,1,0:T(8,128)(2,1)}, bf16[4,4,32,3200]{3,2,1,0:T(8,128)(2,1)S(1)}, u32[]{:S(2)}, u32[]{:S(2)}) %collective-permute-start.23) | collective-permute-done | bytes 3276832 | tf_op jit(solution)/shard_map/ppermute | solution.py:536
  362.1 7.9 %collective-permute-done.26 = bf16[384,1024]{1,0:T(8,128)(2,1)S(1)} collective-permute-done((bf16[384,1024]{1,0:T(8,128)(2,1)S(1)}, bf16[384,1024]{1,0:T(8,128)(2,1)S(1)}, u32[]{:S(2)}, u32[]{:S(2)}) %collective-permute-start.26) | collective-permute-done | bytes 786464 | tf_op jit(solution)/shard_map/ppermute | solution.py:541
  370.0 8.0 %collective-permute-done.24 = bf16[4,2,32,1536]{3,2,0,1:T(8,128)(2,1)S(1)} collective-permute-done((bf16[4,2,32,1536]{3,2,0,1:T(8,128)(2,1)S(1)}, bf16[4,2,32,1536]{3,2,0,1:T(8,128)(2,1)S(1)}, u32[]{:S(2)}, u32[]{:S(2)}) %collective-permute-start.24) | collective-permute-done | bytes 786464 | tf_op jit(solution)/shard_map/ppermute | solution.py:536
  382.5 8.6 %collective-permute-done.27 = bf16[4,32,1536]{2,1,0:T(8,128)(2,1)S(1)} collective-permute-done((bf16[4,32,1536]{2,1,0:T(8,128)(2,1)S(1)}, bf16[4,32,1536]{2,1,0:T(8,128)(2,1)S(1)}, u32[]{:S(2)}, u32[]{:S(2)}) %collective-permute-start.27) | collective-permute-done | bytes 393248 | tf_op jit(solution)/shard_map/ppermute | solution.py:536
  391.2 7.9 %collective-permute-done.29 = bf16[384,1024]{1,0:T(8,128)(2,1)S(1)} collective-permute-done((bf16[384,1024]{1,0:T(8,128)(2,1)S(1)}, bf16[384,1024]{1,0:T(8,128)(2,1)S(1)}, u32[]{:S(2)}, u32[]{:S(2)}) %collective-permute-start.29) | collective-permute-done | bytes 786464 | tf_op jit(solution)/shard_map/ppermute | solution.py:541
  410.8 6.2 %collective-permute-done.31 = bf16[32,3200]{1,0:T(8,128)(2,1)} collective-permute-done((bf16[32,3200]{1,0:T(8,128)(2,1)}, bf16[32,3200]{1,0:T(8,128)(2,1)}, u32[]{:S(2)}, u32[]{:S(2)}) %collective-permute-start.31) | collective-permute-done | bytes 204832 | tf_op jit(solution)/shard_map/ppermute | solution.py:541
  420.4 9.8 %all-to-all-done.1 = bf16[8,2,48,1024]{3,2,1,0:T(8,128)(2,1)S(1)} async-done(((bf16[8,2,48,1024]{3,2,1,0:T(8,128)(2,1)}), bf16[8,2,48,1024]{3,2,1,0:T(8,128)(2,1)S(1)}, u32[]{:S(2)}, u32[]{:S(2)}) %all-to-all-start.1) | async-done | bytes 1572896 | tf_op jit(solution)/shard_map/all_to_all | solution.py:672
  (195 shorter events, 82.1 us)
Async XLA Ops:
  9.9 26.3 %all-to-all-start = ((bf16[8,2,48,1024]{3,2,1,0:T(8,128)(2,1)}), bf16[8,2,48,1024]{3,2,1,0:T(8,128)(2,1)S(1)}, u32[]{:S(2)}, u32[]{:S(2)}) async-start(bf16[8,2,48,1024]{3,2,1,0:T(8,128)(2,1)} %bitcast.4), calls=%async_computation | async-start | bytes 3145728 | tf_op jit(solution)/shard_map/all_to_all | solution.py:598
  15.2 70.2 %all-gather.4.cloned.1.call-start = ((), (), s32[]{:S(2)}) async-start(), calls=%async_computation.4 | async-start | bytes 7372800 | tf_op jit(solution)/shard_map/all_gather | solution.py:520
  15.7 20.9 %collective-permute-start = (bf16[32,3200]{1,0:T(8,128)(2,1)S(1)}, bf16[32,3200]{1,0:T(8,128)(2,1)S(1)}, u32[]{:S(2)}, u32[]{:S(2)}) collective-permute-start(bf16[32,3200]{1,0:T(8,128)(2,1)S(1)} %concatenate.37), channel_id=1, source_target_pairs={{0,8},{8,16},{16,24},{24,0},{1,9},{9,17},{17,25},{25,1},{2,10},{10... | collective-permute-start | bytes 614408 | tf_op jit(solution)/shard_map/ppermute | solution.py:541
  37.6 114.0 %all-gather.6.cloned.1.call-start = ((), (), s32[]{:S(2)}) async-start(), calls=%async_computation.5 | async-start | bytes 4718592 | tf_op jit(solution)/shard_map/all_gather | solution.py:520
  37.7 20.8 %collective-permute-start.3 = (bf16[384,1024]{1,0:T(8,128)(2,1)S(1)}, bf16[384,1024]{1,0:T(8,128)(2,1)}, u32[]{:S(2)}, u32[]{:S(2)}) collective-permute-start(bf16[384,1024]{1,0:T(8,128)(2,1)S(1)} %get-tuple-element.99.refs_6_.refs_4_), channel_id=1, source_target_pairs={{0,8},{8,16},{16,24},{24,0},{1,9},{9,17},{17,25},{25,1},{2,10},{10... | collective-permute-start | bytes 2359304 | tf_op jit(solution)/shard_map/ppermute | solution.py:541
  58.5 20.0 %collective-permute-start.4 = (bf16[384,1024]{1,0:T(8,128)(2,1)}, bf16[384,1024]{1,0:T(8,128)(2,1)}, u32[]{:S(2)}, u32[]{:S(2)}) collective-permute-start(bf16[384,1024]{1,0:T(8,128)(2,1)} %collective-permute-done.3.refs_7_.refs_5_), channel_id=1, source_target_pairs={{0,8},{8,16},{16,24},{24,0},{1,9},{9,17},{17,25},{25,1},{2,10},{10... | collective-permute-start | bytes 2359304 | tf_op jit(solution)/shard_map/ppermute | solution.py:541
  87.4 21.2 %collective-permute-start.7 = (bf16[384,1024]{1,0:T(8,128)(2,1)}, bf16[384,1024]{1,0:T(8,128)(2,1)S(1)}, u32[]{:S(2)}, u32[]{:S(2)}) collective-permute-start(bf16[384,1024]{1,0:T(8,128)(2,1)} %collective-permute-done.4.refs_8_.refs_6_), channel_id=1, source_target_pairs={{0,8},{8,16},{16,24},{24,0},{1,9},{9,17},{17,25},{25,1},{2,10},{10... | collective-permute-start | bytes 2359304 | tf_op jit(solution)/shard_map/ppermute | solution.py:541
  108.6 104.8 %all-gather.8.cloned.1.call-start = ((), (), s32[]{:S(2)}) async-start(), calls=%async_computation.7 | async-start | bytes 10027008 | tf_op jit(solution)/shard_map/all_gather | solution.py:520
  108.7 20.2 %collective-permute-start.10 = (bf16[384,1024]{1,0:T(8,128)(2,1)S(1)}, bf16[384,1024]{1,0:T(8,128)(2,1)}, u32[]{:S(2)}, u32[]{:S(2)}) collective-permute-start(bf16[384,1024]{1,0:T(8,128)(2,1)S(1)} %get-tuple-element.108.refs_6_.refs_4_), channel_id=1, source_target_pairs={{0,8},{8,16},{16,24},{24,0},{1,9},{9,17},{17,25},{25,1},{2,10},{10... | collective-permute-start | bytes 2359304 | tf_op jit(solution)/shard_map/ppermute | solution.py:541
  108.8 20.1 %collective-permute-start.8 = (bf16[128,1152]{1,0:T(8,128)(2,1)S(1)}, bf16[128,1152]{1,0:T(8,128)(2,1)S(1)}, u32[]{:S(2)}, u32[]{:S(2)}) collective-permute-start(bf16[128,1152]{1,0:T(8,128)(2,1)S(1)} %slice.149), channel_id=1, source_target_pairs={{0,4},{4,0},{1,5},{5,1},{2,6},{6,2},{3,7},{7,3},{8,12},{12,8},{9,1... | collective-permute-start | bytes 884744 | tf_op jit(solution)/shard_map/ppermute | solution.py:536
  129.0 22.5 %collective-permute-start.11 = (bf16[1024,1152]{1,0:T(8,128)(2,1)S(1)}, bf16[1024,1152]{1,0:T(8,128)(2,1)S(1)}, u32[]{:S(2)}, u32[]{:S(2)}) collective-permute-start(bf16[1024,1152]{1,0:T(8,128)(2,1)S(1)} %constant_dynamic-update-slice_fusion.refs_1_), channel_id=1, source_target_pairs={{0,1},{1,0},{2,3},{3,2},{4,5},{5,4},{6,7},{7,6},{8,9},{9,8},{10,11... | collective-permute-start | bytes 7077896 | tf_op jit(solution)/shard_map/ppermute | solution.py:536
  129.0 22.4 %collective-permute-start.12 = (bf16[384,1024]{1,0:T(8,128)(2,1)}, bf16[384,1024]{1,0:T(8,128)(2,1)S(1)}, u32[]{:S(2)}, u32[]{:S(2)}) collective-permute-start(bf16[384,1024]{1,0:T(8,128)(2,1)} %collective-permute-done.10.refs_7_.refs_5_), channel_id=1, source_target_pairs={{0,8},{8,16},{16,24},{24,0},{1,9},{9,17},{17,25},{25,1},{2,10},{10... | collective-permute-start | bytes 2359304 | tf_op jit(solution)/shard_map/ppermute | solution.py:541
  151.5 135.7 %reduce-scatter.3.cloned.1.call-start = ((), (), s32[]{:S(2)}) async-start(), calls=%async_computation.6 | async-start | bytes 10027008 | tf_op jit(solution)/shard_map/reduce_scatter | solution.py:524
  151.5 32.3 %collective-permute-start.13 = (bf16[384,1024]{1,0:T(8,128)(2,1)S(1)}, bf16[384,1024]{1,0:T(8,128)(2,1)}, u32[]{:S(2)}, u32[]{:S(2)}) collective-permute-start(bf16[384,1024]{1,0:T(8,128)(2,1)S(1)} %collective-permute-done.12.refs_8_.refs_6_), channel_id=1, source_target_pairs={{0,8},{8,16},{16,24},{24,0},{1,9},{9,17},{17,25},{25,1},{2,10},{10... | collective-permute-start | bytes 2359304 | tf_op jit(solution)/shard_map/ppermute | solution.py:541
  213.2 134.8 %reduce-scatter.5.cloned.1.call-start = ((), (), s32[]{:S(2)}) async-start(), calls=%async_computation.8 | async-start | bytes 4718592 | tf_op jit(solution)/shard_map/reduce_scatter | solution.py:524
  243.7 31.2 %collective-permute-start.14 = (bf16[384,1024]{1,0:T(8,128)(2,1)}, bf16[384,1024]{1,0:T(8,128)(2,1)}, u32[]{:S(2)}, u32[]{:S(2)}) collective-permute-start(bf16[384,1024]{1,0:T(8,128)(2,1)} %get-tuple-element.133), channel_id=1, source_target_pairs={{0,8},{8,16},{16,24},{24,0},{1,9},{9,17},{17,25},{25,1},{2,10},{10... | collective-permute-start | bytes 2359304 | tf_op jit(solution)/shard_map/ppermute | solution.py:541
  278.5 25.6 %collective-permute-start.18 = (bf16[384,1024]{1,0:T(8,128)(2,1)}, bf16[384,1024]{1,0:T(8,128)(2,1)S(1)}, u32[]{:S(2)}, u32[]{:S(2)}) collective-permute-start(bf16[384,1024]{1,0:T(8,128)(2,1)} %add_convert_fusion.9), channel_id=1, source_target_pairs={{0,8},{8,16},{16,24},{24,0},{1,9},{9,17},{17,25},{25,1},{2,10},{10... | collective-permute-start | bytes 2359304 | tf_op jit(solution)/shard_map/ppermute | solution.py:541
  284.4 19.7 %collective-permute-start.17 = (bf16[2,128,1152]{2,1,0:T(8,128)(2,1)}, bf16[2,128,1152]{2,1,0:T(8,128)(2,1)}, u32[]{:S(2)}, u32[]{:S(2)}) collective-permute-start(bf16[2,128,1152]{2,1,0:T(8,128)(2,1)} %pad_maximum_fusion.9), channel_id=1, source_target_pairs={{0,4},{4,0},{1,5},{5,1},{2,6},{6,2},{3,7},{7,3},{8,12},{12,8},{9,1... | collective-permute-start | bytes 1769480 | tf_op jit(solution)/shard_map/ppermute | solution.py:536
  301.7 22.5 %collective-permute-start.21 = (bf16[384,1024]{1,0:T(8,128)(2,1)}, bf16[384,1024]{1,0:T(8,128)(2,1)S(1)}, u32[]{:S(2)}, u32[]{:S(2)}) collective-permute-start(bf16[384,1024]{1,0:T(8,128)(2,1)} %get-tuple-element.145), channel_id=1, source_target_pairs={{0,8},{8,16},{16,24},{24,0},{1,9},{9,17},{17,25},{25,1},{2,10},{10... | collective-permute-start | bytes 2359304 | tf_op jit(solution)/shard_map/ppermute | solution.py:541
  307.9 40.0 %collective-permute-start.22 = (bf16[384,1024]{1,0:T(8,128)(2,1)S(1)}, bf16[384,1024]{1,0:T(8,128)(2,1)S(1)}, u32[]{:S(2)}, u32[]{:S(2)}) collective-permute-start(bf16[384,1024]{1,0:T(8,128)(2,1)S(1)} %add_convert_fusion.7), channel_id=1, source_target_pairs={{0,8},{8,16},{16,24},{24,0},{1,9},{9,17},{17,25},{25,1},{2,10},{10... | collective-permute-start | bytes 2359304 | tf_op jit(solution)/shard_map/ppermute | solution.py:541
  348.1 21.9 %collective-permute-start.26 = (bf16[384,1024]{1,0:T(8,128)(2,1)S(1)}, bf16[384,1024]{1,0:T(8,128)(2,1)S(1)}, u32[]{:S(2)}, u32[]{:S(2)}) collective-permute-start(bf16[384,1024]{1,0:T(8,128)(2,1)S(1)} %add_convert_fusion.8), channel_id=1, source_target_pairs={{0,8},{8,16},{16,24},{24,0},{1,9},{9,17},{17,25},{25,1},{2,10},{10... | collective-permute-start | bytes 2359304 | tf_op jit(solution)/shard_map/ppermute | solution.py:541
  357.1 21.1 %collective-permute-start.25 = (bf16[4,2,32,1664]{3,2,1,0:T(8,128)(2,1)S(1)}, bf16[4,2,32,1664]{3,2,1,0:T(8,128)(2,1)S(1)}, u32[]{:S(2)}, u32[]{:S(2)}) collective-permute-start(bf16[4,2,32,1664]{3,2,1,0:T(8,128)(2,1)S(1)} %slice.203), channel_id=1, source_target_pairs={{0,4},{4,0},{1,5},{5,1},{2,6},{6,2},{3,7},{7,3},{8,12},{12,8},{9,1... | collective-permute-start | bytes 2555912 | tf_op jit(solution)/shard_map/ppermute | solution.py:536
  378.5 20.6 %collective-permute-start.29 = (bf16[384,1024]{1,0:T(8,128)(2,1)S(1)}, bf16[384,1024]{1,0:T(8,128)(2,1)S(1)}, u32[]{:S(2)}, u32[]{:S(2)}) collective-permute-start(bf16[384,1024]{1,0:T(8,128)(2,1)S(1)} %add_convert_fusion.5), channel_id=1, source_target_pairs={{0,8},{8,16},{16,24},{24,0},{1,9},{9,17},{17,25},{25,1},{2,10},{10... | collective-permute-start | bytes 2359304 | tf_op jit(solution)/shard_map/ppermute | solution.py:541
  405.7 24.5 %all-to-all-start.1 = ((bf16[8,2,48,1024]{3,2,1,0:T(8,128)(2,1)}), bf16[8,2,48,1024]{3,2,1,0:T(8,128)(2,1)S(1)}, u32[]{:S(2)}, u32[]{:S(2)}) async-start(bf16[8,2,48,1024]{3,2,1,0:T(8,128)(2,1)} %copy_bitcast_fusion), calls=%async_computation.3 | async-start | bytes 3145728 | tf_op jit(solution)/shard_map/all_to_all | solution.py:672
  (44 other events, 530.1 us)
Sparse Core Ops, SparseCore 0:
  37.7 47.6 all-gather.3
  108.7 35.2 all-gather.5
  151.6 53.8 all-gather.7
  213.3 72.8 reduce-scatter.2
  289.4 51.2 reduce-scatter.4

commit v5 on v4

--- a/solution.py
+++ b/solution.py
@@ -559,7 +559,8 @@
     first, second = total[..., :cut], total[..., cut:]
     got_x, got_y = both(0, across(first[:, 1::2], "x"), across(second[:, 2:], "y"))
     first, second = plus(first[:, ::2], got_x), plus(second[:, :2], got_y)
-    got_y, got_x = both(1, across(first[:, 1], "y"), across(second[:, 1], "x"))
+    beside[1][1](beside[1][0]())
+    got_y, got_x = across(first[:, 1], "y"), across(second[:, 1], "x")
     total = jnp.concatenate([plus(first[:, 0], got_y), plus(second[:, 0], got_x)], axis=-1)
     terms = [total[0]] + [onward(total[s], s) for s in range(1, outer)]
     return sum(term.astype(F32) for term in terms)
@@ -650,17 +651,17 @@
     old = old + [saved_0[3], saved_0[0]]
     early = rows_0, pass_on(0, 2, outer - 1)
     moved[1] = after(moved[1], rows_0)
-    d_mid_1, (rows_0, moved[0]), moved[1] = sum_to_owners(same_1, other_1, early, pass_on(1, 1, outer - 2))
+    d_mid_1, (rows_0, moved[0]), _ = sum_to_owners(same_1, other_1, early, rows_0)
+    pass_on(1, 1, outer - 2)
     summed_0, out_1 = both_0[:, DMID:], scatter_sum(out_1, PLANE_AXES)
-    d_mid_1, moved[1] = tie(d_mid_1, moved[1])
-    following = plus(turns[1][outer - 2], moved[1])
-    d_mid_1, following = tie(d_mid_1, following)
     rows_1, grads, grads_other = attention_backward(1, outer, place, tokens, cot, saved_1, d_mid_1, packed, cosine, sine, old)
-    grads, grads_other, moved[0], out_1 = tie(grads, grads_other, pass_on(0, outer - 1, outer), out_1)
+    grads, grads_other, moved[0], moved[1], out_1 = tie(
+        grads, grads_other, pass_on(0, outer - 1, outer), moved[1], out_1
+    )
     out_sums = summed_0, out_1
     output = [(saved[4] + part.astype(F32)).astype(BF) for saved, part in zip((saved_0, saved_1), out_sums)]
     beside = (
-        (lambda: onward(following), lambda v: moved.__setitem__(1, v)),
+        (lambda: pass_on(1, outer - 2, outer - 1), lambda v: moved.__setitem__(1, v)),
         (lambda: pass_on(1, outer - 1, outer), lambda v: moved.__setitem__(1, v)),
     )
     grads = sum_weights(grads, grads_other, beside)

time: 447 us -> 440 us (0.984)
  waiting for transfers between devices: 155 us -> 145 us
    ppermute x18, waiting for transfers between devices: 100 us -> 86.7 us  [onward(): lax.ppermute(v, 'z', [(i, (i + steps) % count) for i in range(count)])]
  transfers between devices with their start and end apart: 40 -> 40, of which waited for: 18 -> 21; matrix products, arithmetic and copies ran while one was open for 7% -> 8% of each run, Pallas kernels for 42% -> 43%
where the time goes in v5:
time: 440 us; the launch traced here: 432 us
  Pallas kernels  184 us (42%)
  waiting for transfers between devices  145 us (33%)
  starting transfers between devices  43.5 us (10%)
  other arithmetic  36.2 us (8%)
  between operations  14.7 us (3%)
  local copies, waits for them, and re-layouts  9.09 us (2%)
    pallas_call x4, Pallas kernels, experts(): pl.pallas_call(functools.partial(expert_kernel, outer, micro, e), grid_sp...  122 us
    ppermute x18, waiting for transfers between devices, onward(): lax.ppermute(v, 'z', [(i, (i + steps) % count) for i in range(count)])  86.7 us
    pallas_call x2, Pallas kernels, attention_backward(): pl.pallas_call(functools.partial(attention_backward_kernel, outer, last),...  35.7 us
    pallas_call x2, Pallas kernels, attention_forward(): pl.pallas_call(functools.partial(attention_forward_kernel, micro, outer),...  26.7 us
    ppermute x15, waiting for transfers between devices, across(): return lax.ppermute(v, axis, [(0, 1), (1, 0)])  24.4 us
    ppermute x18, starting transfers between devices, onward(): lax.ppermute(v, 'z', [(i, (i + steps) % count) for i in range(count)])  21.5 us
    all_to_all x1, waiting for transfers between devices, shards(): lax.all_to_all(sent.reshape(PLANE, OWN, *sent.shape[1:]), PLANE_AXES, spl...  15 us
    ppermute x15, starting transfers between devices, across(): return lax.ppermute(v, axis, [(0, 1), (1, 0)])  12.7 us
  transfers between devices with their start and end apart: 40, of which 21 were waited for; matrix products, arithmetic and copies ran while one was open for 8% of the time, Pallas kernels for 43%

profile of v5, /device:TPU:0, one launch (start us, length us, event | category | flops | bytes accessed | tf_op | source)
XLA Modules:
  0.0 432.3 jit_solution(16226226275308165823)
XLA Ops:
  9.9 5.3 %all-to-all-start = ((bf16[8,2,48,1024]{3,2,1,0:T(8,128)(2,1)}), bf16[8,2,48,1024]{3,2,1,0:T(8,128)(2,1)S(1)}, u32[]{:S(2)}, u32[]{:S(2)}) async-start(bf16[8,2,48,1024]{3,2,1,0:T(8,128)(2,1)} %bitcast.4), calls=%async_computation | async-start | bytes 3145728 | tf_op jit(solution)/shard_map/all_to_all | solution.py:599
  21.3 15.0 %all-to-all-done = bf16[8,2,48,1024]{3,2,1,0:T(8,128)(2,1)S(1)} async-done(((bf16[8,2,48,1024]{3,2,1,0:T(8,128)(2,1)}), bf16[8,2,48,1024]{3,2,1,0:T(8,128)(2,1)S(1)}, u32[]{:S(2)}, u32[]{:S(2)}) %all-to-all-start) | async-done | bytes 1572896 | tf_op jit(solution)/shard_map/all_to_all | solution.py:599
  43.4 15.1 %collective-permute-done.3.refs_7_.refs_5_ = bf16[384,1024]{1,0:T(8,128)(2,1)} collective-permute-done((bf16[384,1024]{1,0:T(8,128)(2,1)S(1)}, bf16[384,1024]{1,0:T(8,128)(2,1)}, u32[]{:S(2)}, u32[]{:S(2)}) %collective-permute-start.3) | collective-permute-done | bytes 786464 | tf_op jit(solution)/shard_map/ppermute | solution.py:541
  63.2 15.4 %collective-permute-done.4.refs_8_.refs_6_ = bf16[384,1024]{1,0:T(8,128)(2,1)} collective-permute-done((bf16[384,1024]{1,0:T(8,128)(2,1)}, bf16[384,1024]{1,0:T(8,128)(2,1)}, u32[]{:S(2)}, u32[]{:S(2)}) %collective-permute-start.4) | collective-permute-done | bytes 786464 | tf_op jit(solution)/shard_map/ppermute | solution.py:541
  78.6 6.8 %all-gather.4.cloned.1.call-done.w_ref = bf16[1024,3200]{1,0:T(8,128)(2,1)} async-done(((bf16[128,3200]{1,0:T(8,128)(2,1)}), bf16[1024,3200]{1,0:T(8,128)(2,1)}) %all-gather.4.cloned.1.call-update) | async-done | bytes 6553616 | tf_op jit(solution)/shard_map/all_gather | solution.py:520
  88.9 14.2 %attention_forward_0.1 = (bf16[256,1024]{1,0:T(8,128)(2,1)}, bf16[256,1024]{1,0:T(8,128)(2,1)}, bf16[256,1024]{1,0:T(8,128)(2,1)}, bf16[256,1024]{1,0:T(8,128)(2...) custom-call(s32[2]{0:T(128)} %pad_add_fusion.1.place_ref.refs_0_, ...), custom_call_target="tpu_custom_call" | custom-call | flops 13799999488 | bytes 1048576 | tf_op jit(solution)/shard_map/attention_forward_0/pallas_call | solution.py:400
  103.1 5.4 %collective-permute-done.7.refs_9_.refs_7_ = bf16[384,1024]{1,0:T(8,128)(2,1)S(1)} collective-permute-done((bf16[384,1024]{1,0:T(8,128)(2,1)}, bf16[384,1024]{1,0:T(8,128)(2,1)S(1)}, u32[]{:S(2)}, u32[]{:S(2)}) %collective-permute-start.7) | collective-permute-done | bytes 786464 | tf_op jit(solution)/shard_map/ppermute | solution.py:541
  111.2 17.7 %collective-permute-done.10.refs_7_.refs_5_ = bf16[384,1024]{1,0:T(8,128)(2,1)} collective-permute-done((bf16[384,1024]{1,0:T(8,128)(2,1)S(1)}, bf16[384,1024]{1,0:T(8,128)(2,1)}, u32[]{:S(2)}, u32[]{:S(2)}) %collective-permute-start.10) | collective-permute-done | bytes 786464 | tf_op jit(solution)/shard_map/ppermute | solution.py:541
  129.6 12.5 %attention_forward_1.1 = (bf16[256,2176]{1,0:T(8,128)(2,1)}, bf16[256,1024]{1,0:T(8,128)(2,1)}, bf16[256,1024]{1,0:T(8,128)(2,1)}, bf16[256,1024]{1,0:T(8,128)(2...) custom-call(s32[2]{0:T(128)} %pad_add_fusion.1.place_ref.refs_0_, s32[2,4]{1,0:T(2,128)} %lens_ref.3, ...), custom_call_target="tpu_custom_call" | custom-call | flops 13799999488 | bytes 1048576 | tf_op jit(solution)/shard_map/attention_forward_1/pallas_call | solution.py:400
  142.1 9.4 %collective-permute-done.12.refs_8_.refs_6_ = bf16[384,1024]{1,0:T(8,128)(2,1)S(1)} collective-permute-done((bf16[384,1024]{1,0:T(8,128)(2,1)}, bf16[384,1024]{1,0:T(8,128)(2,1)S(1)}, u32[]{:S(2)}, u32[]{:S(2)}) %collective-permute-start.12) | collective-permute-done | bytes 786464 | tf_op jit(solution)/shard_map/ppermute | solution.py:541
  152.9 30.9 %experts_0_0.1 = (bf16[2048,2176]{1,0:T(8,128)(2,1)}, f32[1024,1024]{1,0:T(8,128)}, f32[512,1024]{1,0:T(8,128)}) custom-call(s32[2]{0:T(128)} %pad_add_fusion.1.place_ref.refs_0_, bf16[1024,1152]{1,0:T(8,128)(2,1)} %copy-done.16, bf16[1024,1152]{1,0:T(8,128)(2,1)} %copy-done.24, bf16[2048,1024]{1,0:T(8,128)(2,1)} %all-gather.6.cloned.1.call-done.refs_3_.refs_4_, ...), custom_call_target="tpu_custom_call" | custom-call | flops 32199999488 | bytes 1048576 | tf_op jit(solution)/shard_map/experts_0_0/pallas_call | solution.py:459
  183.8 29.3 %experts_0_1.1 = (bf16[2048,2176]{1,0:T(8,128)(2,1)}, f32[1024,1024]{1,0:T(8,128)}, f32[512,1024]{1,0:T(8,128)}) custom-call(s32[2]{0:T(128)} %pad_add_fusion.1.place_ref.refs_0_, bf16[1024,1152]{1,0:T(8,128)(2,1)} %copy-done.16, bf16[1024,1152]{1,0:T(8,128)(2,1)} %copy-done.24, bf16[2048,1024]{1,0:T(8,128)(2,1)} %all-gather.6.cloned.1.call-done.refs_3_.refs_4_, ...), custom_call_target="tpu_custom_call" | custom-call | flops 32199999488 | bytes 1048576 | tf_op jit(solution)/shard_map/experts_0_1/pallas_call | solution.py:459
  213.4 30.2 %experts_1_0.1 = (bf16[2048,2176]{1,0:T(8,128)(2,1)}, bf16[384,1024]{1,0:T(8,128)(2,1)}, bf16[384,1024]{1,0:T(8,128)(2,1)}, bf16[384,1024]{1,0:T(8,128)(2,1)}, bf16[384,1024]{1,0:T(8,128)(2,1)}) custom-call(s32[2]{0:T(128)} %pad_add_fusion.1.place_ref.refs_0_, bf16[2048,2176]{1,0:T(8,128)(2,1)} %all-gather.8.cloned.1.call-done.refs_1_.refs_2_, ...), custom_call_target="tpu_custom_call" | custom-call | flops 32199999488 | bytes 1048576 | tf_op jit(solution)/shard_map/experts_1_0/pallas_call | solution.py:459
  243.7 31.1 %experts_1_1.1 = (bf16[2048,1024]{1,0:T(8,128)(2,1)}, bf16[1024,1152]{1,0:T(8,128)(2,1)}, bf16[1024,1152]{1,0:T(8,128)(2,1)}, bf16[384,1024]{1,0:T(8,128)(2,1)},...) custom-call(s32[2]{0:T(128)} %pad_add_fusion.1.place_ref.refs_0_, ...), custom_call_target="tpu_custom_call" | custom-call | flops 32199999488 | bytes 1048576 | tf_op jit(solution)/shard_map/experts_1_1/pallas_call | solution.py:459
  287.1 14.6 %attention_backward_0.1 = (f32[256,1024]{1,0:T(8,128)}, bf16[256,1024]{1,0:T(8,128)(2,1)}, bf16[256,1024]{1,0:T(8,128)(2,1)}, bf16[256,1024]{1,0:T(8,128)(2,1)},...) custom-call(s32[2]{0:T(128)} %pad_add_fusion.1.place_ref.refs_0_, ...), custom_call_target="tpu_custom_call" | custom-call | flops 14949999616 | bytes 1048576 | tf_op jit(solution)/shard_map/attention_backward_0/pallas_call | solution.py:491
  314.9 21.2 %attention_backward_1.1 = (f32[256,1024]{1,0:T(8,128)}, bf16[4,4,32,3200]{3,2,1,0:T(8,128)(2,1)}, bf16[4,4,32,3200]{3,2,1,0:T(8,128)(2,1)}) custom-call(s32[2]{0:T(128)} %pad_add_fusion.1.place_ref.refs_0_, bf16[512,1024]{1,0:T(8,128)(2,1)} %refs_1_.3, bf16[512,1152]{1,0:T(8,128)(2,1)} %pad_maximum_fusion.3.cot_ref.refs_2_, ...), custom_call_target="tpu_custom_call" | custom-call | flops 20700000256 | bytes 1048576 | tf_op jit(solution)/shard_map/attention_backward_1/pallas_call | solution.py:491
  336.1 6.6 %collective-permute-done.21 = bf16[384,1024]{1,0:T(8,128)(2,1)S(1)} collective-permute-done((bf16[384,1024]{1,0:T(8,128)(2,1)S(1)}, bf16[384,1024]{1,0:T(8,128)(2,1)S(1)}, u32[]{:S(2)}, u32[]{:S(2)}) %collective-permute-start.21) | collective-permute-done | bytes 786464 | tf_op jit(solution)/shard_map/ppermute | solution.py:541
  344.8 3.9 collective-permute-done.23
  358.6 7.5 %collective-permute-done.26 = bf16[384,1024]{1,0:T(8,128)(2,1)S(1)} collective-permute-done((bf16[384,1024]{1,0:T(8,128)(2,1)S(1)}, bf16[384,1024]{1,0:T(8,128)(2,1)S(1)}, u32[]{:S(2)}, u32[]{:S(2)}) %collective-permute-start.26) | collective-permute-done | bytes 786464 | tf_op jit(solution)/shard_map/ppermute | solution.py:541
  366.1 5.5 %collective-permute-done.24 = bf16[4,2,32,1536]{3,2,0,1:T(8,128)(2,1)S(1)} collective-permute-done((bf16[4,2,32,1536]{3,2,0,1:T(8,128)(2,1)S(1)}, bf16[4,2,32,1536]{3,2,0,1:T(8,128)(2,1)S(1)}, u32[]{:S(2)}, u32[]{:S(2)}) %collective-permute-start.24) | collective-permute-done | bytes 786464 | tf_op jit(solution)/shard_map/ppermute | solution.py:536
  377.7 7.0 %collective-permute-done.27 = bf16[4,32,1536]{2,1,0:T(8,128)(2,1)S(1)} collective-permute-done((bf16[4,32,1536]{2,1,0:T(8,128)(2,1)S(1)}, bf16[4,32,1536]{2,1,0:T(8,128)(2,1)S(1)}, u32[]{:S(2)}, u32[]{:S(2)}) %collective-permute-start.27) | collective-permute-done | bytes 393248 | tf_op jit(solution)/shard_map/ppermute | solution.py:536
  391.9 4.8 %collective-permute-done.32 = bf16[384,1024]{1,0:T(8,128)(2,1)S(1)} collective-permute-done((bf16[384,1024]{1,0:T(8,128)(2,1)S(1)}, bf16[384,1024]{1,0:T(8,128)(2,1)S(1)}, u32[]{:S(2)}, u32[]{:S(2)}) %collective-permute-start.32) | collective-permute-done | bytes 786464 | tf_op jit(solution)/shard_map/ppermute | solution.py:541
  403.0 4.8 %collective-permute-done.30 = bf16[32,3200]{1,0:T(8,128)(2,1)} collective-permute-done((bf16[32,3200]{1,0:T(8,128)(2,1)}, bf16[32,3200]{1,0:T(8,128)(2,1)}, u32[]{:S(2)}, u32[]{:S(2)}) %collective-permute-start.30) | collective-permute-done | bytes 204832 | tf_op jit(solution)/shard_map/ppermute | solution.py:541
  411.2 11.8 %all-to-all-done.1 = bf16[8,2,48,1024]{3,2,1,0:T(8,128)(2,1)S(1)} async-done(((bf16[8,2,48,1024]{3,2,1,0:T(8,128)(2,1)}), bf16[8,2,48,1024]{3,2,1,0:T(8,128)(2,1)S(1)}, u32[]{:S(2)}, u32[]{:S(2)}) %all-to-all-start.1) | async-done | bytes 1572896 | tf_op jit(solution)/shard_map/all_to_all | solution.py:673
  (195 shorter events, 91.7 us)
Async XLA Ops:
  9.9 26.3 %all-to-all-start = ((bf16[8,2,48,1024]{3,2,1,0:T(8,128)(2,1)}), bf16[8,2,48,1024]{3,2,1,0:T(8,128)(2,1)S(1)}, u32[]{:S(2)}, u32[]{:S(2)}) async-start(bf16[8,2,48,1024]{3,2,1,0:T(8,128)(2,1)} %bitcast.4), calls=%async_computation | async-start | bytes 3145728 | tf_op jit(solution)/shard_map/all_to_all | solution.py:599
  15.2 70.2 %all-gather.4.cloned.1.call-start = ((), (), s32[]{:S(2)}) async-start(), calls=%async_computation.4 | async-start | bytes 7372800 | tf_op jit(solution)/shard_map/all_gather | solution.py:520
  15.7 20.9 %collective-permute-start = (bf16[32,3200]{1,0:T(8,128)(2,1)S(1)}, bf16[32,3200]{1,0:T(8,128)(2,1)S(1)}, u32[]{:S(2)}, u32[]{:S(2)}) collective-permute-start(bf16[32,3200]{1,0:T(8,128)(2,1)S(1)} %concatenate.37), channel_id=1, source_target_pairs={{0,8},{8,16},{16,24},{24,0},{1,9},{9,17},{17,25},{25,1},{2,10},{10... | collective-permute-start | bytes 614408 | tf_op jit(solution)/shard_map/ppermute | solution.py:541
  37.6 114.0 %all-gather.6.cloned.1.call-start = ((), (), s32[]{:S(2)}) async-start(), calls=%async_computation.5 | async-start | bytes 4718592 | tf_op jit(solution)/shard_map/all_gather | solution.py:520
  37.7 20.8 %collective-permute-start.3 = (bf16[384,1024]{1,0:T(8,128)(2,1)S(1)}, bf16[384,1024]{1,0:T(8,128)(2,1)}, u32[]{:S(2)}, u32[]{:S(2)}) collective-permute-start(bf16[384,1024]{1,0:T(8,128)(2,1)S(1)} %get-tuple-element.92.refs_6_.refs_4_), channel_id=1, source_target_pairs={{0,8},{8,16},{16,24},{24,0},{1,9},{9,17},{17,25},{25,1},{2,10},{10... | collective-permute-start | bytes 2359304 | tf_op jit(solution)/shard_map/ppermute | solution.py:541
  58.5 20.0 %collective-permute-start.4 = (bf16[384,1024]{1,0:T(8,128)(2,1)}, bf16[384,1024]{1,0:T(8,128)(2,1)}, u32[]{:S(2)}, u32[]{:S(2)}) collective-permute-start(bf16[384,1024]{1,0:T(8,128)(2,1)} %collective-permute-done.3.refs_7_.refs_5_), channel_id=1, source_target_pairs={{0,8},{8,16},{16,24},{24,0},{1,9},{9,17},{17,25},{25,1},{2,10},{10... | collective-permute-start | bytes 2359304 | tf_op jit(solution)/shard_map/ppermute | solution.py:541
  87.4 21.2 %collective-permute-start.7 = (bf16[384,1024]{1,0:T(8,128)(2,1)}, bf16[384,1024]{1,0:T(8,128)(2,1)S(1)}, u32[]{:S(2)}, u32[]{:S(2)}) collective-permute-start(bf16[384,1024]{1,0:T(8,128)(2,1)} %collective-permute-done.4.refs_8_.refs_6_), channel_id=1, source_target_pairs={{0,8},{8,16},{16,24},{24,0},{1,9},{9,17},{17,25},{25,1},{2,10},{10... | collective-permute-start | bytes 2359304 | tf_op jit(solution)/shard_map/ppermute | solution.py:541
  108.6 104.8 %all-gather.8.cloned.1.call-start = ((), (), s32[]{:S(2)}) async-start(), calls=%async_computation.7 | async-start | bytes 10027008 | tf_op jit(solution)/shard_map/all_gather | solution.py:520
  108.7 20.2 %collective-permute-start.10 = (bf16[384,1024]{1,0:T(8,128)(2,1)S(1)}, bf16[384,1024]{1,0:T(8,128)(2,1)}, u32[]{:S(2)}, u32[]{:S(2)}) collective-permute-start(bf16[384,1024]{1,0:T(8,128)(2,1)S(1)} %get-tuple-element.101.refs_6_.refs_4_), channel_id=1, source_target_pairs={{0,8},{8,16},{16,24},{24,0},{1,9},{9,17},{17,25},{25,1},{2,10},{10... | collective-permute-start | bytes 2359304 | tf_op jit(solution)/shard_map/ppermute | solution.py:541
  108.8 20.1 %collective-permute-start.8 = (bf16[128,1152]{1,0:T(8,128)(2,1)S(1)}, bf16[128,1152]{1,0:T(8,128)(2,1)S(1)}, u32[]{:S(2)}, u32[]{:S(2)}) collective-permute-start(bf16[128,1152]{1,0:T(8,128)(2,1)S(1)} %slice.149), channel_id=1, source_target_pairs={{0,4},{4,0},{1,5},{5,1},{2,6},{6,2},{3,7},{7,3},{8,12},{12,8},{9,1... | collective-permute-start | bytes 884744 | tf_op jit(solution)/shard_map/ppermute | solution.py:536
  129.0 22.5 %collective-permute-start.11 = (bf16[1024,1152]{1,0:T(8,128)(2,1)S(1)}, bf16[1024,1152]{1,0:T(8,128)(2,1)S(1)}, u32[]{:S(2)}, u32[]{:S(2)}) collective-permute-start(bf16[1024,1152]{1,0:T(8,128)(2,1)S(1)} %constant_dynamic-update-slice_fusion.refs_1_), channel_id=1, source_target_pairs={{0,1},{1,0},{2,3},{3,2},{4,5},{5,4},{6,7},{7,6},{8,9},{9,8},{10,11... | collective-permute-start | bytes 7077896 | tf_op jit(solution)/shard_map/ppermute | solution.py:536
  129.0 22.4 %collective-permute-start.12 = (bf16[384,1024]{1,0:T(8,128)(2,1)}, bf16[384,1024]{1,0:T(8,128)(2,1)S(1)}, u32[]{:S(2)}, u32[]{:S(2)}) collective-permute-start(bf16[384,1024]{1,0:T(8,128)(2,1)} %collective-permute-done.10.refs_7_.refs_5_), channel_id=1, source_target_pairs={{0,8},{8,16},{16,24},{24,0},{1,9},{9,17},{17,25},{25,1},{2,10},{10... | collective-permute-start | bytes 2359304 | tf_op jit(solution)/shard_map/ppermute | solution.py:541
  151.5 135.7 %reduce-scatter.3.cloned.1.call-start = ((), (), s32[]{:S(2)}) async-start(), calls=%async_computation.6 | async-start | bytes 10027008 | tf_op jit(solution)/shard_map/reduce_scatter | solution.py:524
  151.5 32.3 %collective-permute-start.13 = (bf16[384,1024]{1,0:T(8,128)(2,1)S(1)}, bf16[384,1024]{1,0:T(8,128)(2,1)}, u32[]{:S(2)}, u32[]{:S(2)}) collective-permute-start(bf16[384,1024]{1,0:T(8,128)(2,1)S(1)} %collective-permute-done.12.refs_8_.refs_6_), channel_id=1, source_target_pairs={{0,8},{8,16},{16,24},{24,0},{1,9},{9,17},{17,25},{25,1},{2,10},{10... | collective-permute-start | bytes 2359304 | tf_op jit(solution)/shard_map/ppermute | solution.py:541
  213.2 129.5 %reduce-scatter.5.cloned.1.call-start = ((), (), s32[]{:S(2)}) async-start(), calls=%async_computation.8 | async-start | bytes 4718592 | tf_op jit(solution)/shard_map/reduce_scatter | solution.py:524
  243.6 31.2 %collective-permute-start.14 = (bf16[384,1024]{1,0:T(8,128)(2,1)}, bf16[384,1024]{1,0:T(8,128)(2,1)}, u32[]{:S(2)}, u32[]{:S(2)}) collective-permute-start(bf16[384,1024]{1,0:T(8,128)(2,1)} %get-tuple-element.126), channel_id=1, source_target_pairs={{0,8},{8,16},{16,24},{24,0},{1,9},{9,17},{17,25},{25,1},{2,10},{10... | collective-permute-start | bytes 2359304 | tf_op jit(solution)/shard_map/ppermute | solution.py:541
  278.4 23.3 %collective-permute-start.18 = (bf16[384,1024]{1,0:T(8,128)(2,1)}, bf16[384,1024]{1,0:T(8,128)(2,1)S(1)}, u32[]{:S(2)}, u32[]{:S(2)}) collective-permute-start(bf16[384,1024]{1,0:T(8,128)(2,1)} %add_convert_fusion.9), channel_id=1, source_target_pairs={{0,8},{8,16},{16,24},{24,0},{1,9},{9,17},{17,25},{25,1},{2,10},{10... | collective-permute-start | bytes 2359304 | tf_op jit(solution)/shard_map/ppermute | solution.py:541
  305.3 30.8 %collective-permute-start.22 = (bf16[384,1024]{1,0:T(8,128)(2,1)}, bf16[384,1024]{1,0:T(8,128)(2,1)}, u32[]{:S(2)}, u32[]{:S(2)}) collective-permute-start(bf16[384,1024]{1,0:T(8,128)(2,1)} %get-tuple-element.150), channel_id=1, source_target_pairs={{0,8},{8,16},{16,24},{24,0},{1,9},{9,17},{17,25},{25,1},{2,10},{10... | collective-permute-start | bytes 2359304 | tf_op jit(solution)/shard_map/ppermute | solution.py:541
  308.0 34.7 %collective-permute-start.21 = (bf16[384,1024]{1,0:T(8,128)(2,1)S(1)}, bf16[384,1024]{1,0:T(8,128)(2,1)S(1)}, u32[]{:S(2)}, u32[]{:S(2)}) collective-permute-start(bf16[384,1024]{1,0:T(8,128)(2,1)S(1)} %add_convert_fusion.8), channel_id=1, source_target_pairs={{0,8},{8,16},{16,24},{24,0},{1,9},{9,17},{17,25},{25,1},{2,10},{10... | collective-permute-start | bytes 2359304 | tf_op jit(solution)/shard_map/ppermute | solution.py:541
  344.1 22.0 %collective-permute-start.26 = (bf16[384,1024]{1,0:T(8,128)(2,1)S(1)}, bf16[384,1024]{1,0:T(8,128)(2,1)S(1)}, u32[]{:S(2)}, u32[]{:S(2)}) collective-permute-start(bf16[384,1024]{1,0:T(8,128)(2,1)S(1)} %add_convert_fusion.7), channel_id=1, source_target_pairs={{0,8},{8,16},{16,24},{24,0},{1,9},{9,17},{17,25},{25,1},{2,10},{10... | collective-permute-start | bytes 2359304 | tf_op jit(solution)/shard_map/ppermute | solution.py:541
  351.9 19.6 %collective-permute-start.24 = (bf16[4,2,32,1536]{3,2,0,1:T(8,128)(2,1)S(1)}, bf16[4,2,32,1536]{3,2,0,1:T(8,128)(2,1)S(1)}, u32[]{:S(2)}, u32[]{:S(2)}) collective-permute-start(bf16[4,2,32,1536]{3,2,0,1:T(8,128)(2,1)S(1)} %copy.69), channel_id=1, source_target_pairs={{0,2},{2,0},{1,3},{3,1},{4,6},{6,4},{5,7},{7,5},{8,10},{10,8},{9,1... | collective-permute-start | bytes 2359304 | tf_op jit(solution)/shard_map/ppermute | solution.py:536
  353.1 20.7 %collective-permute-start.25 = (bf16[4,2,32,1664]{3,2,1,0:T(8,128)(2,1)S(1)}, bf16[4,2,32,1664]{3,2,1,0:T(8,128)(2,1)S(1)}, u32[]{:S(2)}, u32[]{:S(2)}) collective-permute-start(bf16[4,2,32,1664]{3,2,1,0:T(8,128)(2,1)S(1)} %slice.203), channel_id=1, source_target_pairs={{0,4},{4,0},{1,5},{5,1},{2,6},{6,2},{3,7},{7,3},{8,12},{12,8},{9,1... | collective-permute-start | bytes 2555912 | tf_op jit(solution)/shard_map/ppermute | solution.py:536
  374.1 22.5 %collective-permute-start.32 = (bf16[384,1024]{1,0:T(8,128)(2,1)S(1)}, bf16[384,1024]{1,0:T(8,128)(2,1)S(1)}, u32[]{:S(2)}, u32[]{:S(2)}) collective-permute-start(bf16[384,1024]{1,0:T(8,128)(2,1)S(1)} %add_convert_fusion.4), channel_id=1, source_target_pairs={{0,8},{8,16},{16,24},{24,0},{1,9},{9,17},{17,25},{25,1},{2,10},{10... | collective-permute-start | bytes 2359304 | tf_op jit(solution)/shard_map/ppermute | solution.py:541
  398.4 24.5 %all-to-all-start.1 = ((bf16[8,2,48,1024]{3,2,1,0:T(8,128)(2,1)}), bf16[8,2,48,1024]{3,2,1,0:T(8,128)(2,1)S(1)}, u32[]{:S(2)}, u32[]{:S(2)}) async-start(bf16[8,2,48,1024]{3,2,1,0:T(8,128)(2,1)} %copy_bitcast_fusion), calls=%async_computation.3 | async-start | bytes 3145728 | tf_op jit(solution)/shard_map/all_to_all | solution.py:673
  (44 other events, 524.9 us)
Sparse Core Ops, SparseCore 0:
  37.7 47.6 all-gather.3
  108.7 35.2 all-gather.5
  151.6 53.8 all-gather.7
  213.3 72.8 reduce-scatter.2
  289.5 51.2 reduce-scatter.4

commit v6 on v5

--- a/solution.py
+++ b/solution.py
@@ -466,7 +466,7 @@
             scratch_shapes=scratch,
         ),
         out_shape=out_shape,
-        compiler_params=kernel_params(),
+        compiler_params=kernel_params(48 if not micro and not e else 58),
         cost_estimate=takes(28),
         name=f"experts_{micro}_{e}",
     )(place, *rows, packed, *homes, *partial, *carried)
@@ -498,7 +498,7 @@
             scratch_shapes=scratch,
         ),
         out_shape=[shaped(MB, D, F32)] + kept,
-        compiler_params=kernel_params(),
+        compiler_params=kernel_params(50 if last else 58),
         cost_estimate=takes(18 if last else 13),
         name=f"attention_backward_{micro}",
     )(place, *args)

time: 440 us -> 441 us (level)
  waiting for transfers between devices: 145 us -> 138 us
    ppermute x18, waiting for transfers between devices: 86.7 us -> 79.8 us  [onward(): lax.ppermute(v, 'z', [(i, (i + steps) % count) for i in range(count)])]
    unnamed x66 -> x102, local copies, waits for them, and re-layouts: 6.65 us -> 9.01 us
  transfers between devices with their start and end apart: 40 -> 40, of which waited for: 21 -> 21; matrix products, arithmetic and copies ran while one was open for 8% -> 9% of each run, Pallas kernels for 43% -> 42%
where the time goes in v6:
time: 441 us; the launch traced here: 433 us
  Pallas kernels  182 us (41%)
  waiting for transfers between devices  138 us (31%)
  starting transfers between devices  45.1 us (10%)
  other arithmetic  39.3 us (9%)
  between operations  14.9 us (3%)
  local copies, waits for them, and re-layouts  13.4 us (3%)
    pallas_call x4, Pallas kernels, experts(): pl.pallas_call(functools.partial(expert_kernel, outer, micro, e), grid_sp...  119 us
    ppermute x18, waiting for transfers between devices, onward(): lax.ppermute(v, 'z', [(i, (i + steps) % count) for i in range(count)])  79.8 us
    pallas_call x2, Pallas kernels, attention_backward(): pl.pallas_call(functools.partial(attention_backward_kernel, outer, last),...  35 us
    pallas_call x2, Pallas kernels, attention_forward(): pl.pallas_call(functools.partial(attention_forward_kernel, micro, outer),...  27.4 us
    ppermute x18, starting transfers between devices, onward(): lax.ppermute(v, 'z', [(i, (i + steps) % count) for i in range(count)])  23.4 us
    ppermute x15, waiting for transfers between devices, across(): return lax.ppermute(v, axis, [(0, 1), (1, 0)])  23.3 us
    all_to_all x1, waiting for transfers between devices, shards(): lax.all_to_all(sent.reshape(PLANE, OWN, *sent.shape[1:]), PLANE_AXES, spl...  15 us
    ppermute x15, starting transfers between devices, across(): return lax.ppermute(v, axis, [(0, 1), (1, 0)])  12.4 us
  transfers between devices with their start and end apart: 40, of which 21 were waited for; matrix products, arithmetic and copies ran while one was open for 9% of the time, Pallas kernels for 42%

profile of v6, /device:TPU:0, one launch (start us, length us, event | category | flops | bytes accessed | tf_op | source)
XLA Modules:
  0.0 432.5 jit_solution(18089940167170492468)
XLA Ops:
  9.9 5.3 %all-to-all-start = ((bf16[8,2,48,1024]{3,2,1,0:T(8,128)(2,1)}), bf16[8,2,48,1024]{3,2,1,0:T(8,128)(2,1)S(1)}, u32[]{:S(2)}, u32[]{:S(2)}) async-start(bf16[8,2,48,1024]{3,2,1,0:T(8,128)(2,1)} %bitcast.4), calls=%async_computation | async-start | bytes 3145728 | tf_op jit(solution)/shard_map/all_to_all | solution.py:599
  21.3 15.0 %all-to-all-done = bf16[8,2,48,1024]{3,2,1,0:T(8,128)(2,1)S(1)} async-done(((bf16[8,2,48,1024]{3,2,1,0:T(8,128)(2,1)}), bf16[8,2,48,1024]{3,2,1,0:T(8,128)(2,1)S(1)}, u32[]{:S(2)}, u32[]{:S(2)}) %all-to-all-start) | async-done | bytes 1572896 | tf_op jit(solution)/shard_map/all_to_all | solution.py:599
  44.9 14.5 %collective-permute-done.3.refs_7_.refs_5_ = bf16[384,1024]{1,0:T(8,128)(2,1)S(1)} collective-permute-done((bf16[384,1024]{1,0:T(8,128)(2,1)S(1)}, bf16[384,1024]{1,0:T(8,128)(2,1)S(1)}, u32[]{:S(2)}, u32[]{:S(2)}) %collective-permute-start.3) | collective-permute-done | bytes 786464 | tf_op jit(solution)/shard_map/ppermute | solution.py:541
  65.0 13.1 %collective-permute-done.4.refs_8_.refs_6_ = bf16[384,1024]{1,0:T(8,128)(2,1)S(1)} collective-permute-done((bf16[384,1024]{1,0:T(8,128)(2,1)S(1)}, bf16[384,1024]{1,0:T(8,128)(2,1)S(1)}, u32[]{:S(2)}, u32[]{:S(2)}) %collective-permute-start.4) | collective-permute-done | bytes 786464 | tf_op jit(solution)/shard_map/ppermute | solution.py:541
  78.0 8.3 %all-gather.4.cloned.1.call-done.w_ref = bf16[1024,3200]{1,0:T(8,128)(2,1)} async-done(((bf16[128,3200]{1,0:T(8,128)(2,1)}), bf16[1024,3200]{1,0:T(8,128)(2,1)}) %all-gather.4.cloned.1.call-update) | async-done | bytes 6553616 | tf_op jit(solution)/shard_map/all_gather | solution.py:520
  89.8 14.2 %attention_forward_0.1 = (bf16[256,1024]{1,0:T(8,128)(2,1)}, bf16[256,1024]{1,0:T(8,128)(2,1)}, bf16[256,1024]{1,0:T(8,128)(2,1)}, bf16[256,1024]{1,0:T(8,128)(2...) custom-call(s32[2]{0:T(128)} %pad_add_fusion.1.place_ref.refs_0_, ...), custom_call_target="tpu_custom_call" | custom-call | flops 13799999488 | bytes 1048576 | tf_op jit(solution)/shard_map/attention_forward_0/pallas_call | solution.py:400
  104.1 5.2 %collective-permute-done.7.refs_9_.refs_7_ = bf16[384,1024]{1,0:T(8,128)(2,1)S(1)} collective-permute-done((bf16[384,1024]{1,0:T(8,128)(2,1)S(1)}, bf16[384,1024]{1,0:T(8,128)(2,1)S(1)}, u32[]{:S(2)}, u32[]{:S(2)}) %collective-permute-start.7) | collective-permute-done | bytes 786464 | tf_op jit(solution)/shard_map/ppermute | solution.py:541
  115.1 14.7 %collective-permute-done.10.refs_7_.refs_5_ = bf16[384,1024]{1,0:T(8,128)(2,1)} collective-permute-done((bf16[384,1024]{1,0:T(8,128)(2,1)}, bf16[384,1024]{1,0:T(8,128)(2,1)}, u32[]{:S(2)}, u32[]{:S(2)}) %collective-permute-start.10) | collective-permute-done | bytes 786464 | tf_op jit(solution)/shard_map/ppermute | solution.py:541
  130.5 13.2 %attention_forward_1.1 = (bf16[256,2176]{1,0:T(8,128)(2,1)}, bf16[256,1024]{1,0:T(8,128)(2,1)}, bf16[256,1024]{1,0:T(8,128)(2,1)}, bf16[256,1024]{1,0:T(8,128)(2...) custom-call(s32[2]{0:T(128)} %pad_add_fusion.1.place_ref.refs_0_, s32[2,4]{1,0:T(2,128)} %lens_ref.3, ...), custom_call_target="tpu_custom_call" | custom-call | flops 13799999488 | bytes 1048576 | tf_op jit(solution)/shard_map/attention_forward_1/pallas_call | solution.py:400
  143.7 8.8 %collective-permute-done.12.refs_8_.refs_6_ = bf16[384,1024]{1,0:T(8,128)(2,1)} collective-permute-done((bf16[384,1024]{1,0:T(8,128)(2,1)}, bf16[384,1024]{1,0:T(8,128)(2,1)}, u32[]{:S(2)}, u32[]{:S(2)}) %collective-permute-start.12) | collective-permute-done | bytes 786464 | tf_op jit(solution)/shard_map/ppermute | solution.py:541
  152.7 28.7 %experts_0_0.1 = (bf16[2048,2176]{1,0:T(8,128)(2,1)}, f32[1024,1024]{1,0:T(8,128)}, f32[512,1024]{1,0:T(8,128)S(1)}) custom-call(s32[2]{0:T(128)S(1)} %copy-done.6, bf16[1024,1152]{1,0:T(8,128)(2,1)} %copy-done.36, bf16[1024,1152]{1,0:T(8,128)(2,1)} %collective-permute-done.11.refs_2_, bf16[2048,1024]{1,0:T(8,128)(2,1)} %all-gather.6.cloned.1.call-done.refs_3_.refs_4_, ...), custom_call_target="tpu_custom_call" | custom-call | flops 32199999488 | bytes 1048576 | tf_op jit(solution)/shard_map/experts_0_0/pallas_call | solution.py:459
  182.7 29.3 %experts_0_1.1 = (bf16[2048,2176]{1,0:T(8,128)(2,1)}, f32[1024,1024]{1,0:T(8,128)}, f32[512,1024]{1,0:T(8,128)}) custom-call(s32[2]{0:T(128)} %pad_add_fusion.1.place_ref.refs_0_, bf16[1024,1152]{1,0:T(8,128)(2,1)} %copy-done.36, bf16[1024,1152]{1,0:T(8,128)(2,1)} %collective-permute-done.11.refs_2_, ...), custom_call_target="tpu_custom_call" | custom-call | flops 32199999488 | bytes 1048576 | tf_op jit(solution)/shard_map/experts_0_1/pallas_call | solution.py:459
  212.3 30.2 %experts_1_0.1 = (bf16[2048,2176]{1,0:T(8,128)(2,1)}, bf16[384,1024]{1,0:T(8,128)(2,1)}, bf16[384,1024]{1,0:T(8,128)(2,1)}, bf16[384,1024]{1,0:T(8,128)(2,1)}, bf16[384,1024]{1,0:T(8,128)(2,1)}) custom-call(s32[2]{0:T(128)} %pad_add_fusion.1.place_ref.refs_0_, bf16[2048,2176]{1,0:T(8,128)(2,1)} %all-gather.8.cloned.1.call-done.refs_1_.refs_2_, ...), custom_call_target="tpu_custom_call" | custom-call | flops 32199999488 | bytes 1048576 | tf_op jit(solution)/shard_map/experts_1_0/pallas_call | solution.py:459
  242.5 31.1 %experts_1_1.1 = (bf16[2048,1024]{1,0:T(8,128)(2,1)}, bf16[1024,1152]{1,0:T(8,128)(2,1)}, bf16[1024,1152]{1,0:T(8,128)(2,1)}, bf16[384,1024]{1,0:T(8,128)(2,1)},...) custom-call(s32[2]{0:T(128)} %pad_add_fusion.1.place_ref.refs_0_, ...), custom_call_target="tpu_custom_call" | custom-call | flops 32199999488 | bytes 1048576 | tf_op jit(solution)/shard_map/experts_1_1/pallas_call | solution.py:459
  286.7 14.7 %attention_backward_0.1 = (f32[256,1024]{1,0:T(8,128)}, bf16[256,1024]{1,0:T(8,128)(2,1)}, bf16[256,1024]{1,0:T(8,128)(2,1)}, bf16[256,1024]{1,0:T(8,128)(2,1)},...) custom-call(s32[2]{0:T(128)} %pad_add_fusion.1.place_ref.refs_0_, ...), custom_call_target="tpu_custom_call" | custom-call | flops 14949999616 | bytes 1048576 | tf_op jit(solution)/shard_map/attention_backward_0/pallas_call | solution.py:491
  305.0 3.9 collective-permute-start.22
  315.4 20.3 %attention_backward_1.1 = (f32[256,1024]{1,0:T(8,128)}, bf16[4,4,32,3200]{3,2,1,0:T(8,128)(2,1)}, bf16[4,4,32,3200]{3,2,1,0:T(8,128)(2,1)}) custom-call(s32[2]{0:T(128)S(1)} %copy-done.7, bf16[512,1024]{1,0:T(8,128)(2,1)} %refs_1_.3, bf16[512,1152]{1,0:T(8,128)(2,1)} %pad_maximum_fusion.3.cot_ref.refs_2_, bf16[256,2176]{1,0:T(8,128)(2,1)} %get-tuple-element.118.refs_3_, ...), custom_call_target="tpu_custom_call" | custom-call | flops 20700000256 | bytes 1048576 | tf_op jit(solution)/shard_map/attention_backward_1/pallas_call | solution.py:491
  335.6 7.1 %collective-permute-done.21 = bf16[384,1024]{1,0:T(8,128)(2,1)S(1)} collective-permute-done((bf16[384,1024]{1,0:T(8,128)(2,1)S(1)}, bf16[384,1024]{1,0:T(8,128)(2,1)S(1)}, u32[]{:S(2)}, u32[]{:S(2)}) %collective-permute-start.21) | collective-permute-done | bytes 786464 | tf_op jit(solution)/shard_map/ppermute | solution.py:541
  359.1 7.1 %collective-permute-done.26 = bf16[384,1024]{1,0:T(8,128)(2,1)S(1)} collective-permute-done((bf16[384,1024]{1,0:T(8,128)(2,1)S(1)}, bf16[384,1024]{1,0:T(8,128)(2,1)S(1)}, u32[]{:S(2)}, u32[]{:S(2)}) %collective-permute-start.26) | collective-permute-done | bytes 786464 | tf_op jit(solution)/shard_map/ppermute | solution.py:541
  366.1 5.5 %collective-permute-done.24 = bf16[4,2,32,1536]{3,2,0,1:T(8,128)(2,1)S(1)} collective-permute-done((bf16[4,2,32,1536]{3,2,0,1:T(8,128)(2,1)S(1)}, bf16[4,2,32,1536]{3,2,0,1:T(8,128)(2,1)S(1)}, u32[]{:S(2)}, u32[]{:S(2)}) %collective-permute-start.24) | collective-permute-done | bytes 786464 | tf_op jit(solution)/shard_map/ppermute | solution.py:536
  378.6 7.4 %collective-permute-done.27 = bf16[4,32,1536]{2,1,0:T(8,128)(2,1)S(1)} collective-permute-done((bf16[4,32,1536]{2,1,0:T(8,128)(2,1)S(1)}, bf16[4,32,1536]{2,1,0:T(8,128)(2,1)S(1)}, u32[]{:S(2)}, u32[]{:S(2)}) %collective-permute-start.27) | collective-permute-done | bytes 393248 | tf_op jit(solution)/shard_map/ppermute | solution.py:536
  392.3 4.5 %collective-permute-done.32 = bf16[384,1024]{1,0:T(8,128)(2,1)S(1)} collective-permute-done((bf16[384,1024]{1,0:T(8,128)(2,1)S(1)}, bf16[384,1024]{1,0:T(8,128)(2,1)S(1)}, u32[]{:S(2)}, u32[]{:S(2)}) %collective-permute-start.32) | collective-permute-done | bytes 786464 | tf_op jit(solution)/shard_map/ppermute | solution.py:541
  403.2 4.8 %collective-permute-done.30 = bf16[32,3200]{1,0:T(8,128)(2,1)} collective-permute-done((bf16[32,3200]{1,0:T(8,128)(2,1)}, bf16[32,3200]{1,0:T(8,128)(2,1)}, u32[]{:S(2)}, u32[]{:S(2)}) %collective-permute-start.30) | collective-permute-done | bytes 204832 | tf_op jit(solution)/shard_map/ppermute | solution.py:541
  411.4 11.8 %all-to-all-done.1 = bf16[8,2,48,1024]{3,2,1,0:T(8,128)(2,1)S(1)} async-done(((bf16[8,2,48,1024]{3,2,1,0:T(8,128)(2,1)}), bf16[8,2,48,1024]{3,2,1,0:T(8,128)(2,1)S(1)}, u32[]{:S(2)}, u32[]{:S(2)}) %all-to-all-start.1) | async-done | bytes 1572896 | tf_op jit(solution)/shard_map/all_to_all | solution.py:673
  (231 shorter events, 99.2 us)
Async XLA Ops:
  9.9 26.3 %all-to-all-start = ((bf16[8,2,48,1024]{3,2,1,0:T(8,128)(2,1)}), bf16[8,2,48,1024]{3,2,1,0:T(8,128)(2,1)S(1)}, u32[]{:S(2)}, u32[]{:S(2)}) async-start(bf16[8,2,48,1024]{3,2,1,0:T(8,128)(2,1)} %bitcast.4), calls=%async_computation | async-start | bytes 3145728 | tf_op jit(solution)/shard_map/all_to_all | solution.py:599
  15.2 71.1 %all-gather.4.cloned.1.call-start = ((), (), s32[]{:S(2)}) async-start(), calls=%async_computation.4 | async-start | bytes 7372800 | tf_op jit(solution)/shard_map/all_gather | solution.py:520
  15.7 21.7 %collective-permute-start = (bf16[32,3200]{1,0:T(8,128)(2,1)S(1)}, bf16[32,3200]{1,0:T(8,128)(2,1)S(1)}, u32[]{:S(2)}, u32[]{:S(2)}) collective-permute-start(bf16[32,3200]{1,0:T(8,128)(2,1)S(1)} %concatenate.37), channel_id=1, source_target_pairs={{0,8},{8,16},{16,24},{24,0},{1,9},{9,17},{17,25},{25,1},{2,10},{10... | collective-permute-start | bytes 614408 | tf_op jit(solution)/shard_map/ppermute | solution.py:541
  17.3 20.1 %collective-permute-start.1 = (bf16[32,3200]{1,0:T(8,128)(2,1)S(1)}, bf16[32,3200]{1,0:T(8,128)(2,1)S(1)}, u32[]{:S(2)}, u32[]{:S(2)}) collective-permute-start(bf16[32,3200]{1,0:T(8,128)(2,1)S(1)} %concatenate.37), channel_id=1, source_target_pairs={{0,16},{8,24},{16,0},{24,8},{1,17},{9,25},{17,1},{25,9},{2,18},{10... | collective-permute-start | bytes 614408 | tf_op jit(solution)/shard_map/ppermute | solution.py:541
  39.7 113.0 %all-gather.6.cloned.1.call-start = ((), (), s32[]{:S(2)}) async-start(), calls=%async_computation.5 | async-start | bytes 4718592 | tf_op jit(solution)/shard_map/all_gather | solution.py:520
  39.8 19.5 %collective-permute-start.3 = (bf16[384,1024]{1,0:T(8,128)(2,1)S(1)}, bf16[384,1024]{1,0:T(8,128)(2,1)S(1)}, u32[]{:S(2)}, u32[]{:S(2)}) collective-permute-start(bf16[384,1024]{1,0:T(8,128)(2,1)S(1)} %get-tuple-element.92.refs_6_.refs_4_), channel_id=1, source_target_pairs={{0,8},{8,16},{16,24},{24,0},{1,9},{9,17},{17,25},{25,1},{2,10},{10... | collective-permute-start | bytes 2359304 | tf_op jit(solution)/shard_map/ppermute | solution.py:541
  59.4 18.7 %collective-permute-start.4 = (bf16[384,1024]{1,0:T(8,128)(2,1)S(1)}, bf16[384,1024]{1,0:T(8,128)(2,1)S(1)}, u32[]{:S(2)}, u32[]{:S(2)}) collective-permute-start(bf16[384,1024]{1,0:T(8,128)(2,1)S(1)} %collective-permute-done.3.refs_7_.refs_5_), channel_id=1, source_target_pairs={{0,8},{8,16},{16,24},{24,0},{1,9},{9,17},{17,25},{25,1},{2,10},{10... | collective-permute-start | bytes 2359304 | tf_op jit(solution)/shard_map/ppermute | solution.py:541
  88.3 20.9 %collective-permute-start.7 = (bf16[384,1024]{1,0:T(8,128)(2,1)S(1)}, bf16[384,1024]{1,0:T(8,128)(2,1)S(1)}, u32[]{:S(2)}, u32[]{:S(2)}) collective-permute-start(bf16[384,1024]{1,0:T(8,128)(2,1)S(1)} %collective-permute-done.4.refs_8_.refs_6_), channel_id=1, source_target_pairs={{0,8},{8,16},{16,24},{24,0},{1,9},{9,17},{17,25},{25,1},{2,10},{10... | collective-permute-start | bytes 2359304 | tf_op jit(solution)/shard_map/ppermute | solution.py:541
  109.3 102.9 %all-gather.8.cloned.1.call-start = ((), (), s32[]{:S(2)}) async-start(), calls=%async_computation.7 | async-start | bytes 10027008 | tf_op jit(solution)/shard_map/all_gather | solution.py:520
  109.4 20.4 %collective-permute-start.10 = (bf16[384,1024]{1,0:T(8,128)(2,1)}, bf16[384,1024]{1,0:T(8,128)(2,1)}, u32[]{:S(2)}, u32[]{:S(2)}) collective-permute-start(bf16[384,1024]{1,0:T(8,128)(2,1)} %get-tuple-element.101.refs_6_.refs_4_), channel_id=1, source_target_pairs={{0,8},{8,16},{16,24},{24,0},{1,9},{9,17},{17,25},{25,1},{2,10},{10... | collective-permute-start | bytes 2359304 | tf_op jit(solution)/shard_map/ppermute | solution.py:541
  129.9 22.6 %collective-permute-start.11 = (bf16[1024,1152]{1,0:T(8,128)(2,1)S(1)}, bf16[1024,1152]{1,0:T(8,128)(2,1)}, u32[]{:S(2)}, u32[]{:S(2)}) collective-permute-start(bf16[1024,1152]{1,0:T(8,128)(2,1)S(1)} %constant_dynamic-update-slice_fusion.refs_1_), channel_id=1, source_target_pairs={{0,1},{1,0},{2,3},{3,2},{4,5},{5,4},{6,7},{7,6},{8,9},{9,8},{10,11... | collective-permute-start | bytes 7077896 | tf_op jit(solution)/shard_map/ppermute | solution.py:536
  130.0 22.5 %collective-permute-start.12 = (bf16[384,1024]{1,0:T(8,128)(2,1)}, bf16[384,1024]{1,0:T(8,128)(2,1)}, u32[]{:S(2)}, u32[]{:S(2)}) collective-permute-start(bf16[384,1024]{1,0:T(8,128)(2,1)} %collective-permute-done.10.refs_7_.refs_5_), channel_id=1, source_target_pairs={{0,8},{8,16},{16,24},{24,0},{1,9},{9,17},{17,25},{25,1},{2,10},{10... | collective-permute-start | bytes 2359304 | tf_op jit(solution)/shard_map/ppermute | solution.py:541
  152.5 134.2 %reduce-scatter.3.cloned.1.call-start = ((), (), s32[]{:S(2)}) async-start(), calls=%async_computation.6 | async-start | bytes 10027008 | tf_op jit(solution)/shard_map/reduce_scatter | solution.py:524
  152.6 30.2 %collective-permute-start.13 = (bf16[384,1024]{1,0:T(8,128)(2,1)}, bf16[384,1024]{1,0:T(8,128)(2,1)}, u32[]{:S(2)}, u32[]{:S(2)}) collective-permute-start(bf16[384,1024]{1,0:T(8,128)(2,1)} %collective-permute-done.12.refs_8_.refs_6_), channel_id=1, source_target_pairs={{0,8},{8,16},{16,24},{24,0},{1,9},{9,17},{17,25},{25,1},{2,10},{10... | collective-permute-start | bytes 2359304 | tf_op jit(solution)/shard_map/ppermute | solution.py:541
  212.0 130.7 %reduce-scatter.5.cloned.1.call-start = ((), (), s32[]{:S(2)}) async-start(), calls=%async_computation.8 | async-start | bytes 4718592 | tf_op jit(solution)/shard_map/reduce_scatter | solution.py:524
  242.5 31.2 %collective-permute-start.14 = (bf16[384,1024]{1,0:T(8,128)(2,1)}, bf16[384,1024]{1,0:T(8,128)(2,1)S(1)}, u32[]{:S(2)}, u32[]{:S(2)}) collective-permute-start(bf16[384,1024]{1,0:T(8,128)(2,1)} %get-tuple-element.126), channel_id=1, source_target_pairs={{0,8},{8,16},{16,24},{24,0},{1,9},{9,17},{17,25},{25,1},{2,10},{10... | collective-permute-start | bytes 2359304 | tf_op jit(solution)/shard_map/ppermute | solution.py:541
  278.3 23.2 %collective-permute-start.18 = (bf16[384,1024]{1,0:T(8,128)(2,1)}, bf16[384,1024]{1,0:T(8,128)(2,1)S(1)}, u32[]{:S(2)}, u32[]{:S(2)}) collective-permute-start(bf16[384,1024]{1,0:T(8,128)(2,1)} %add_convert_fusion.9), channel_id=1, source_target_pairs={{0,8},{8,16},{16,24},{24,0},{1,9},{9,17},{17,25},{25,1},{2,10},{10... | collective-permute-start | bytes 2359304 | tf_op jit(solution)/shard_map/ppermute | solution.py:541
  305.0 30.6 %collective-permute-start.22 = (bf16[384,1024]{1,0:T(8,128)(2,1)S(1)}, bf16[384,1024]{1,0:T(8,128)(2,1)}, u32[]{:S(2)}, u32[]{:S(2)}) collective-permute-start(bf16[384,1024]{1,0:T(8,128)(2,1)S(1)} %copy-done.44), channel_id=1, source_target_pairs={{0,8},{8,16},{16,24},{24,0},{1,9},{9,17},{17,25},{25,1},{2,10},{10... | collective-permute-start | bytes 2359304 | tf_op jit(solution)/shard_map/ppermute | solution.py:541
  309.3 33.4 %collective-permute-start.21 = (bf16[384,1024]{1,0:T(8,128)(2,1)S(1)}, bf16[384,1024]{1,0:T(8,128)(2,1)S(1)}, u32[]{:S(2)}, u32[]{:S(2)}) collective-permute-start(bf16[384,1024]{1,0:T(8,128)(2,1)S(1)} %add_convert_fusion.8), channel_id=1, source_target_pairs={{0,8},{8,16},{16,24},{24,0},{1,9},{9,17},{17,25},{25,1},{2,10},{10... | collective-permute-start | bytes 2359304 | tf_op jit(solution)/shard_map/ppermute | solution.py:541
  344.2 22.0 %collective-permute-start.26 = (bf16[384,1024]{1,0:T(8,128)(2,1)S(1)}, bf16[384,1024]{1,0:T(8,128)(2,1)S(1)}, u32[]{:S(2)}, u32[]{:S(2)}) collective-permute-start(bf16[384,1024]{1,0:T(8,128)(2,1)S(1)} %add_convert_fusion.7), channel_id=1, source_target_pairs={{0,8},{8,16},{16,24},{24,0},{1,9},{9,17},{17,25},{25,1},{2,10},{10... | collective-permute-start | bytes 2359304 | tf_op jit(solution)/shard_map/ppermute | solution.py:541
  352.0 19.6 %collective-permute-start.24 = (bf16[4,2,32,1536]{3,2,0,1:T(8,128)(2,1)S(1)}, bf16[4,2,32,1536]{3,2,0,1:T(8,128)(2,1)S(1)}, u32[]{:S(2)}, u32[]{:S(2)}) collective-permute-start(bf16[4,2,32,1536]{3,2,0,1:T(8,128)(2,1)S(1)} %copy.69), channel_id=1, source_target_pairs={{0,2},{2,0},{1,3},{3,1},{4,6},{6,4},{5,7},{7,5},{8,10},{10,8},{9,1... | collective-permute-start | bytes 2359304 | tf_op jit(solution)/shard_map/ppermute | solution.py:536
  353.3 20.7 %collective-permute-start.25 = (bf16[4,2,32,1664]{3,2,1,0:T(8,128)(2,1)S(1)}, bf16[4,2,32,1664]{3,2,1,0:T(8,128)(2,1)S(1)}, u32[]{:S(2)}, u32[]{:S(2)}) collective-permute-start(bf16[4,2,32,1664]{3,2,1,0:T(8,128)(2,1)S(1)} %slice.203), channel_id=1, source_target_pairs={{0,4},{4,0},{1,5},{5,1},{2,6},{6,2},{3,7},{7,3},{8,12},{12,8},{9,1... | collective-permute-start | bytes 2555912 | tf_op jit(solution)/shard_map/ppermute | solution.py:536
  374.3 22.5 %collective-permute-start.32 = (bf16[384,1024]{1,0:T(8,128)(2,1)S(1)}, bf16[384,1024]{1,0:T(8,128)(2,1)S(1)}, u32[]{:S(2)}, u32[]{:S(2)}) collective-permute-start(bf16[384,1024]{1,0:T(8,128)(2,1)S(1)} %add_convert_fusion.4), channel_id=1, source_target_pairs={{0,8},{8,16},{16,24},{24,0},{1,9},{9,17},{17,25},{25,1},{2,10},{10... | collective-permute-start | bytes 2359304 | tf_op jit(solution)/shard_map/ppermute | solution.py:541
  398.6 24.5 %all-to-all-start.1 = ((bf16[8,2,48,1024]{3,2,1,0:T(8,128)(2,1)}), bf16[8,2,48,1024]{3,2,1,0:T(8,128)(2,1)S(1)}, u32[]{:S(2)}, u32[]{:S(2)}) async-start(bf16[8,2,48,1024]{3,2,1,0:T(8,128)(2,1)} %copy_bitcast_fusion), calls=%async_computation.3 | async-start | bytes 3145728 | tf_op jit(solution)/shard_map/all_to_all | solution.py:673
  (62 other events, 848.9 us)
Sparse Core Ops, SparseCore 0:
  39.8 46.4 all-gather.3
  109.4 37.9 all-gather.5
  152.7 53.8 all-gather.7
  212.1 74.5 reduce-scatter.2
  289.9 51.2 reduce-scatter.4
